TPU v7x, 256 devices: a whole 4x4x8 slice. The times are simulated.
256 devices in a mesh: slab: 128 (over x, z, y), chan: 2 (over core).
Axes of the slice: x: 4, y: 4, z: 8, core: 2. Of those that a mesh axis runs over, the one named last changes fastest.
Arguments:
- points: bfloat16 [32768, 64, 128], P(('slab', 'chan')), may hold values from -6 to 6
- near_start: int32 [32768, 128], P(('slab', 'chan')), may hold values from 0 to 120
- near_weight: bfloat16 [32768, 8, 128], P(('slab', 'chan')), may hold values from -2 to 2
- dest_slab: int32 [32768, 1], P(('slab', 'chan')), may hold values from 0 to 127; in each aligned block of 128 rows (0 to 127, 128 to 255, ...) at most 2 rows name the same one
- dest_block: int32 [32768], P(('slab', 'chan')), may hold values from 0 to 127
- live_count: int32 [256], P(('slab', 'chan')), may hold values from 1 to 128, 28672 in all
- lift_w: bfloat16 [64, 64], replicated, may hold values from -0.75 to 0.75
- spec_weight: bfloat16 [2, 64, 64, 32, 1024], P(None, None, None, None, ('slab', 'chan')), may hold values from -8.375 to 8.375
- skip_w: bfloat16 [64, 64], replicated, may hold values from -0.75 to 0.75
- skip_bias: float32 [64], replicated, may hold values from -3 to 3
- proj_in: bfloat16 [64, 128], replicated, may hold values from -0.75 to 0.75
- proj_out: bfloat16 [128], replicated, may hold values from -0.5 to 0.5
Outputs:
- pressure: float32 [32768, 128], P(('slab', 'chan'))
Inputs may be any that keep to these rules, and one draw needn't show every extreme that they name: `dest_slab`: among the 128 blocks of one device no slab is named by more than 2 blocks, a bound that some block reaches. `live_count`: blocks of a device at or past its count are padding; some device has all 128 live.
All inputs are finite; a program needn't handle non-finite values.
Results may differ from a plain program's by a relative error of at most 0.015.
Values may be sent and summed in bfloat16 or wider, within the bound.
A program may use at most 128 MiB of HBM per device.

v0:
```python
import math

import jax
import jax.numpy as jnp
from jax import lax
from jax.sharding import PartitionSpec as P

G = 128
M = 32
PB = 128
NB = 8


def signed_modes(count):
    index = jnp.arange(count, dtype=jnp.int32)
    return jnp.where(index < count // 2, index, index - count)


def angles(length, count):
    positions = jnp.arange(length, dtype=jnp.int32)
    product = jnp.mod(positions[:, None] * signed_modes(count)[None, :], length)
    phase = product.astype(jnp.float32) * (2.0 * math.pi / length)
    return (jnp.cos(phase), jnp.sin(phase))


def precise(form, left, right):
    return jnp.einsum(
        form, left, right, precision=lax.Precision.HIGHEST, preferred_element_type=jnp.float32
    )


def widened(form, left, right):
    return jnp.einsum(form, left, right, preferred_element_type=jnp.float32)


def near_matrix(start, weight):
    cells = jnp.arange(G, dtype=jnp.int32)
    offset = cells[None, None, :] - start[:, :, None]
    total = jnp.zeros(offset.shape, weight.dtype)
    for neighbour in range(NB):
        total = total + jnp.where(
            offset == neighbour, weight[:, neighbour, :][:, :, None], jnp.zeros((), weight.dtype)
        )
    return total


def mix_modes(by_mode, spec_weight, cosine, sine):
    x_real = precise("cxm,xp->cpm", by_mode[0], cosine) + precise("cxm,xp->cpm", by_mode[1], sine)
    x_imag = precise("cxm,xp->cpm", by_mode[1], cosine) - precise("cxm,xp->cpm", by_mode[0], sine)
    weight_real = spec_weight[0].astype(jnp.float32)
    weight_imag = spec_weight[1].astype(jnp.float32)
    mixed_real = precise("ipm,iopm->opm", x_real, weight_real) - precise(
        "ipm,iopm->opm", x_imag, weight_imag
    )
    mixed_imag = precise("ipm,iopm->opm", x_real, weight_imag) + precise(
        "ipm,iopm->opm", x_imag, weight_real
    )
    back_real = precise("opm,xp->oxm", mixed_real, cosine) - precise(
        "opm,xp->oxm", mixed_imag, sine
    )
    back_imag = precise("opm,xp->oxm", mixed_imag, cosine) + precise(
        "opm,xp->oxm", mixed_real, sine
    )
    return jnp.stack([back_real, back_imag]).astype(jnp.bfloat16)


def shards(
    points,
    near_start,
    near_weight,
    dest_slab,
    dest_block,
    live_count,
    lift_w,
    spec_weight,
    skip_w,
    skip_bias,
    proj_in,
    proj_out,
):
    slabs = lax.axis_size("slab")
    halves = lax.axis_size("chan")
    chan_index = lax.axis_index("chan")
    blocks = points.shape[0]
    width = points.shape[1]
    part_width = width // halves
    capacity = max(2, 2 * blocks // slabs)
    planes = G // slabs
    cell_lines = planes * G
    slots = slabs * capacity
    live = jnp.arange(blocks, dtype=jnp.int32) < live_count[0]
    target = dest_slab[:, 0]
    match = (target[:, None] == jnp.arange(slabs, dtype=jnp.int32)[None, :]) & live[:, None]
    rank = jnp.cumsum(match.astype(jnp.int32), axis=0) - 1
    rank_own = jnp.sum(jnp.where(match, rank, 0), axis=1)
    slot_of = target * capacity + rank_own
    select = (jnp.arange(slots, dtype=jnp.int32)[:, None] == slot_of[None, :]) & live[None, :]
    select_bf = select.astype(jnp.bfloat16)
    filled = jnp.any(select, axis=1)
    slot_line = jnp.where(filled, jnp.sum(jnp.where(select, dest_block[None, :], 0), axis=1), -1)
    lifted = widened("bcp,cd->bdp", points, lift_w).astype(jnp.bfloat16)
    near = near_matrix(near_start, near_weight)
    cosine, sine = angles(G, M)
    line_ids = jnp.broadcast_to(slot_line.reshape(slabs, capacity, 1), (slabs, capacity, halves))
    lifted_packed = (
        widened("sb,bcp->scp", select_bf, lifted)
        .astype(jnp.bfloat16)
        .reshape(slabs, capacity, width, PB)
    )
    start_packed = jnp.sum(jnp.where(select[:, :, None], near_start[None, :, :], 0), axis=1)
    start_packed = jnp.broadcast_to(
        start_packed.reshape(slabs, capacity, 1, PB), (slabs, capacity, halves, PB)
    )
    weight_packed = widened("sb,bjp->sjp", select_bf, near_weight).astype(jnp.bfloat16)
    weight_packed = jnp.broadcast_to(
        weight_packed.reshape(slabs, capacity, 1, NB, PB), (slabs, capacity, halves, NB, PB)
    )
    got_lifted, got_start, got_weight, received_ids = (
        lax.all_to_all(
            lax.all_to_all(lifted_packed, "slab", split_axis=0, concat_axis=0, tiled=True),
            "chan",
            split_axis=2,
            concat_axis=1,
            tiled=True,
        ),
        lax.all_to_all(
            lax.all_to_all(start_packed, "slab", split_axis=0, concat_axis=0, tiled=True),
            "chan",
            split_axis=2,
            concat_axis=1,
            tiled=True,
        ),
        lax.all_to_all(
            lax.all_to_all(weight_packed, "slab", split_axis=0, concat_axis=0, tiled=True),
            "chan",
            split_axis=2,
            concat_axis=1,
            tiled=True,
        ),
        lax.all_to_all(
            lax.all_to_all(line_ids, "slab", split_axis=0, concat_axis=0, tiled=True),
            "chan",
            split_axis=2,
            concat_axis=1,
            tiled=True,
        ),
    )
    got_near = near_matrix(got_start.reshape(-1, PB), got_weight.reshape(-1, NB, PB))
    flat_part = widened("scp,spz->scz", got_lifted.reshape(-1, part_width, PB), got_near).astype(
        jnp.bfloat16
    )
    flat_ids = received_ids.reshape(-1)
    line_hot = (flat_ids[:, None] == jnp.arange(cell_lines, dtype=jnp.int32)[None, :]).astype(
        jnp.bfloat16
    )
    latent = widened("sk,scz->ckz", line_hot, flat_part).reshape(part_width, planes, G, G)
    z_real = precise("cxyz,zk->cxyk", latent, cosine)
    z_imag = -precise("cxyz,zk->cxyk", latent, sine)
    y_real = precise("cxyk,yq->cxqk", z_real, cosine) + precise("cxyk,yq->cxqk", z_imag, sine)
    y_imag = precise("cxyk,yq->cxqk", z_imag, cosine) - precise("cxyk,yq->cxqk", z_real, sine)
    spectra = jnp.stack([y_real, y_imag]).reshape(2, part_width, planes, M * M).astype(jnp.bfloat16)
    by_mode = lax.all_to_all(
        lax.all_to_all(spectra, "slab", split_axis=3, concat_axis=2, tiled=True),
        "chan",
        split_axis=3,
        concat_axis=1,
        tiled=True,
    ).astype(jnp.float32)
    backward = mix_modes(by_mode, spec_weight, cosine, sine)
    returned = lax.all_to_all(
        lax.all_to_all(backward, "chan", split_axis=1, concat_axis=3, tiled=True),
        "slab",
        split_axis=2,
        concat_axis=3,
        tiled=True,
    ).astype(jnp.float32)
    v_real = returned[0].reshape(part_width, planes, M, M)
    v_imag = returned[1].reshape(part_width, planes, M, M)
    u_real = precise("cxqk,yq->cxyk", v_real, cosine) - precise("cxqk,yq->cxyk", v_imag, sine)
    u_imag = precise("cxqk,yq->cxyk", v_imag, cosine) + precise("cxqk,yq->cxyk", v_real, sine)
    spectral = (
        precise("cxyk,zk->cxyz", u_real, cosine) - precise("cxyk,zk->cxyz", u_imag, sine)
    ) * (1.0 / (G * G * G))
    first = chan_index * part_width
    rows_own = lax.dynamic_slice_in_dim(skip_w, first, part_width, 0).astype(jnp.float32)
    terms = precise("io,ixyz->oxyz", rows_own, latent)
    mixing = lax.psum_scatter(terms, "chan", scatter_dimension=0, tiled=True)
    bias_own = lax.dynamic_slice_in_dim(skip_bias, first, part_width, 0)
    grid_out = jax.nn.gelu(spectral + mixing + bias_own[:, None, None, None]).astype(jnp.bfloat16)
    grid_out = grid_out.reshape(part_width, cell_lines, G)
    picked = widened("sk,ckz->scz", line_hot, grid_out).astype(jnp.bfloat16)
    picked = picked.reshape(slabs, halves * capacity, part_width, G)
    values_back = lax.all_to_all(
        lax.all_to_all(picked, "slab", split_axis=0, concat_axis=0, tiled=True),
        "chan",
        split_axis=1,
        concat_axis=2,
        tiled=True,
    )
    cells = widened("sb,scz->bcz", select_bf, values_back.reshape(slots, width, G)).astype(
        jnp.bfloat16
    )
    near_val = widened("bcz,bpz->bcp", cells, near).astype(jnp.bfloat16)
    dec_hidden = jax.nn.gelu(widened("bcp,ch->bhp", near_val, proj_in)).astype(jnp.bfloat16)
    result = widened("bhp,h->bp", dec_hidden, proj_out)
    return jnp.where(live[:, None], result, jnp.zeros((), jnp.float32))


def solution(mesh):
    placed = (
        P(("slab", "chan"), None, None),
        P(("slab", "chan"), None),
        P(("slab", "chan"), None, None),
        P(("slab", "chan"), None),
        P(("slab", "chan")),
        P(("slab", "chan")),
        P(),
        P(None, None, None, None, ("slab", "chan")),
        P(),
        P(),
        P(),
        P(),
    )
    return jax.shard_map(
        shards, mesh=mesh, in_specs=placed, out_specs=P(("slab", "chan"), None), check_vma=False
    )
```

profile of v0, /device:TPU:1, one launch (start us, length us, event | category | flops | bytes accessed | tf_op | source)
XLA Modules:
  0.0 652.3 jit_solution(17429638328465691680)
XLA Ops:
  11.6 16.3 %all-to-all-start = ((s32[128,2,2]{1,2,0:T(2,128)}), s32[128,2,2]{1,2,0:T(2,128)S(1)}, u32[]{:S(2)}, u32[]{:S(2)}) async-start(s32[128,2,2]{1,2,0:T(2,128)} %broadcast_in_dim.232), calls=%async_computation | async-start | bytes 262144 | tf_op jit(solution)/shard_map/all_to_all | solution.py:141
  28.0 7.6 %select_reduce_fusion = s32[256,128]{1,0:T(8,128)S(1)} fusion(s32[128,128]{1,0:T(8,128)} %param.13, pred[256,128]{1,0:T(8,128)(4,1)S(1)} %copy.281), kind=kLoop, calls=%fused_computation.34 | loop fusion | flops 8355840 | bytes 229376 | tf_op jit(solution)/shard_map/reduce_sum | solution.py:110
  39.6 10.1 %all-to-all-start.4 = ((s32[128,2,2,128]{3,1,2,0:T(2,128)}), s32[128,2,2,128]{3,1,2,0:T(2,128)S(1)}, u32[]{:S(2)}, u32[]{:S(2)}) async-start(s32[128,2,2,128]{3,1,2,0:T(2,128)} %broadcast_in_dim.237), calls=%async_computation.4 | async-start | bytes 524288 | tf_op jit(solution)/shard_map/all_to_all | solution.py:127
  51.4 10.2 %all-to-all-done.4 = s32[128,2,2,128]{3,1,2,0:T(2,128)S(1)} async-done(((s32[128,2,2,128]{3,1,2,0:T(2,128)}), s32[128,2,2,128]{3,1,2,0:T(2,128)S(1)}, u32[]{:S(2)}, u32[]{:S(2)}) %all-to-all-start.4) | async-done | bytes 262176 | tf_op jit(solution)/shard_map/all_to_all | solution.py:127
  63.1 8.3 %all-to-all-start.6 = ((bf16[128,2,2,8,128]{4,1,2,3,0:T(2,128)(2,1)}), bf16[128,2,2,8,128]{4,1,2,3,0:T(2,128)(2,1)}, u32[]{:S(2)}, u32[]{:S(2)}) async-start(bf16[128,2,2,8,128]{4,1,2,3,0:T(2,128)(2,1)} %broadcast_in_dim.239), calls=%async_computation.6 | async-start | bytes 2097152 | tf_op jit(solution)/shard_map/all_to_all | solution.py:134
  74.3 6.7 %copy.277 = bf16[128,2,64,128]{3,1,2,0:T(2,128)(2,1)} copy(bf16[128,2,64,128]{3,1,0,2:T(2,128)(2,1)S(1)} %bitcast.293) | data formatting | bytes 8388608 | tf_op jit(solution)/shard_map/reshape | solution.py:108
  81.8 14.7 %all-to-all-done.6 = bf16[128,2,2,8,128]{4,1,2,3,0:T(2,128)(2,1)} async-done(((bf16[128,2,2,8,128]{4,1,2,3,0:T(2,128)(2,1)}), bf16[128,2,2,8,128]{4,1,2,3,0:T(2,128)(2,1)}, u32[]{:S(2)}, u32[]{:S(2)}) %all-to-all-start.6) | async-done | bytes 1048608 | tf_op jit(solution)/shard_map/all_to_all | solution.py:134
  96.5 8.7 %all-to-all-start.1 = ((s32[128,2,2]{0,1,2:T(2,128)}), s32[128,2,2]{0,1,2:T(2,128)S(1)}, u32[]{:S(2)}, u32[]{:S(2)}) async-start(s32[128,2,2]{0,1,2:T(2,128)} %copy.272), calls=%async_computation.1 | async-start | bytes 4096 | tf_op jit(solution)/shard_map/all_to_all | solution.py:140
  111.0 4.6 all_to_all.155
  115.6 7.4 %all-to-all-start.2 = ((bf16[128,2,64,128]{3,1,2,0:T(2,128)(2,1)}), bf16[128,2,64,128]{3,1,2,0:T(2,128)(2,1)}, u32[]{:S(2)}, u32[]{:S(2)}) async-start(bf16[128,2,64,128]{3,1,2,0:T(2,128)(2,1)} %copy.277), calls=%async_computation.2 | async-start | bytes 8388608 | tf_op jit(solution)/shard_map/all_to_all | solution.py:120
  126.7 89.0 %all-to-all-done.2 = bf16[128,2,64,128]{3,1,2,0:T(2,128)(2,1)} async-done(((bf16[128,2,64,128]{3,1,2,0:T(2,128)(2,1)}), bf16[128,2,64,128]{3,1,2,0:T(2,128)(2,1)}, u32[]{:S(2)}, u32[]{:S(2)}) %all-to-all-start.2) | async-done | bytes 4194336 | tf_op jit(solution)/shard_map/all_to_all | solution.py:120
  215.7 6.8 %copy.278 = bf16[128,2,64,128]{3,1,0,2:T(2,128)(2,1)S(1)} copy(bf16[128,2,64,128]{3,1,2,0:T(2,128)(2,1)} %all-to-all-done.2) | data formatting | bytes 8388608 | tf_op jit(solution)/shard_map/all_to_all | solution.py:120
  222.5 12.6 %all_to_all.156 = bf16[128,2,64,128]{3,1,0,2:T(2,128)(2,1)S(1)} all-to-all(bf16[128,2,64,128]{3,1,0,2:T(2,128)(2,1)S(1)} %copy.278), channel_id=1, replica_groups=mesh['slab'=128,'chan'=2] {'chan'}, dimensions={2} | all-to-all | bytes 8388608 | tf_op jit(solution)/shard_map/all_to_all | solution.py:119
  235.1 4.9 copy.279
  241.3 126.6 %fusion.107 = bf16[512,32,128]{2,1,0:T(8,128)(2,1)S(1)} fusion(bf16[512,32,128]{2,1,0:T(8,128)(2,1)S(1)} %bitcast.297, s32[512,128]{1,0:T(8,128)S(1)} %bitcast.322, bf16[512,128]{1,0:T(8,128)(2,1)S(1)} %get-tuple-element.29, bf16[512,128]{1,0:T(8,128)(2,1)S(1)} %get-tuple-element.30, bf16[512,128]{1,0:T(8,128)(2,1)S(1)} %get-tuple-element.31, ...), kind=kOutput, calls=%fused_computation.95 | convolution fusion | flops 815792128 | bytes 9699328 | tf_op jit(solution)/shard_map/scp,spz->scz/dot_general | solution.py:33
  367.9 4.3 fusion.143
  378.0 4.4 copy.422
  397.8 6.7 %all-to-all-start.8 = ((bf16[128,2,256]{2,1,0:T(2,128)(2,1)}), bf16[128,2,256]{2,1,0:T(2,128)(2,1)S(1)}, u32[]{:S(2)}, u32[]{:S(2)}) async-start(bf16[128,2,256]{2,1,0:T(2,128)(2,1)} %reshape.265), calls=%async_computation.8 | async-start | bytes 262144 | tf_op jit(solution)/shard_map/all_to_all | solution.py:163
  404.5 6.1 slice_bitcast_fusion
  410.5 4.9 all-to-all-done.8
  416.2 5.7 all_to_all.157
  423.4 4.6 fusion.137
  428.0 4.6 fusion.141
  446.3 7.2 %all-to-all-start.11 = ((bf16[128,2,256]{2,1,0:T(2,128)(2,1)}), bf16[128,2,256]{2,1,0:T(2,128)(2,1)S(1)}, u32[]{:S(2)}, u32[]{:S(2)}) async-start(bf16[128,2,256]{2,1,0:T(2,128)(2,1)} %reshape.267), calls=%async_computation.11 | async-start | bytes 262144 | tf_op jit(solution)/shard_map/all_to_all | solution.py:170
  453.7 10.8 %all-to-all-done.11 = bf16[128,2,256]{2,1,0:T(2,128)(2,1)S(1)} async-done(((bf16[128,2,256]{2,1,0:T(2,128)(2,1)}), bf16[128,2,256]{2,1,0:T(2,128)(2,1)S(1)}, u32[]{:S(2)}, u32[]{:S(2)}) %all-to-all-start.11) | async-done | bytes 131104 | tf_op jit(solution)/shard_map/all_to_all | solution.py:170
  471.5 5.9 fusion.146
  478.7 6.9 %copy.310 = bf16[128,4,32,128]{3,2,1,0:T(8,128)(2,1)} copy(bf16[128,4,32,128]{3,1,0,2:T(4,128)(2,1)S(1)} %bitcast.291) | data formatting | bytes 8388608 | tf_op jit(solution)/shard_map/reshape | solution.py:192
  485.5 7.5 %all-to-all-start.12 = ((bf16[128,4,32,128]{3,2,1,0:T(8,128)(2,1)}), bf16[128,4,32,128]{3,2,1,0:T(8,128)(2,1)}, u32[]{:S(2)}, u32[]{:S(2)}) async-start(bf16[128,4,32,128]{3,2,1,0:T(8,128)(2,1)} %copy.310), calls=%async_computation.13 | async-start | bytes 8388608 | tf_op jit(solution)/shard_map/all_to_all | solution.py:194
  493.2 92.2 %all-to-all-done.12 = bf16[128,4,32,128]{3,2,1,0:T(8,128)(2,1)} async-done(((bf16[128,4,32,128]{3,2,1,0:T(8,128)(2,1)}), bf16[128,4,32,128]{3,2,1,0:T(8,128)(2,1)}, u32[]{:S(2)}, u32[]{:S(2)}) %all-to-all-start.12) | async-done | bytes 4194336 | tf_op jit(solution)/shard_map/all_to_all | solution.py:194
  588.3 12.2 %all_to_all.159 = bf16[128,4,32,128]{3,2,0,1:T(8,128)(2,1)S(1)} all-to-all(bf16[128,4,32,128]{3,2,0,1:T(8,128)(2,1)S(1)} %copy.311), channel_id=1, replica_groups=mesh['slab'=128,'chan'=2] {'chan'}, dimensions={1} | all-to-all | bytes 8388608 | tf_op jit(solution)/shard_map/all_to_all | solution.py:193
  604.9 34.8 %fusion.75 = bf16[128,64,128]{2,1,0:T(8,128)(2,1)} fusion(s32[128,128]{1,0:T(8,128)S(1)} %copy-done.5, bf16[128,64,128]{2,0,1:T(8,128)(2,1)S(1)} %fusion.132, bf16[128,128]{1,0:T(8,128)(2,1)S(1)} %get-tuple-element.24, bf16[128,128]{1,0:T(8,128)(2,1)S(1)} %get-tuple-element.18, bf16[128,128]{1,0:T(8,128)(2,1)S(1)} %get-tuple-element.19, ...), kind=kOutput, calls=%fused_computation.71 | convolution fusion | flops 337641472 | bytes 4521984 | tf_op jit(solution)/shard_map/bcz,bpz->bcp/dot_general | solution.py:33
  639.6 4.6 fusion.103
  (120 shorter events, 79.0 us)
Async XLA Ops:
  6.5 64.9 %copy-start = (bf16[128,64,128]{2,1,0:T(8,128)(2,1)S(1)}, bf16[128,64,128]{2,1,0:T(8,128)(2,1)}, u32[]{:S(2)}) copy-start(bf16[128,64,128]{2,1,0:T(8,128)(2,1)} %param.12) | copy-start | bytes 6291460
  6.5 64.9 %copy-start.8 = (bf16[64,64]{1,0:T(8,128)(2,1)S(1)}, bf16[64,64]{1,0:T(8,128)(2,1)}, u32[]{:S(2)}) copy-start(bf16[64,64]{1,0:T(8,128)(2,1)} %param.18) | copy-start | bytes 24580
  7.4 64.9 %copy-start.6 = (pred[128]{0:T(512)(128)(4,1)}, pred[128]{0:T(512)(128)(4,1)S(1)}, u32[]{:S(2)}) copy-start(pred[128]{0:T(512)(128)(4,1)S(1)} %iota_compare_fusion.3) | copy-start | bytes 388
  9.8 62.4 %copy-start.9 = (s32[128]{0:T(128)}, s32[128]{0:T(128)S(1)}, u32[]{:S(2)}) copy-start(s32[128]{0:T(128)S(1)} %multiply_add_fusion) | copy-start | bytes 1540
  11.6 27.3 %all-to-all-start = ((s32[128,2,2]{1,2,0:T(2,128)}), s32[128,2,2]{1,2,0:T(2,128)S(1)}, u32[]{:S(2)}, u32[]{:S(2)}) async-start(s32[128,2,2]{1,2,0:T(2,128)} %broadcast_in_dim.232), calls=%async_computation | async-start | bytes 262144 | tf_op jit(solution)/shard_map/all_to_all | solution.py:141
  39.6 22.0 %all-to-all-start.4 = ((s32[128,2,2,128]{3,1,2,0:T(2,128)}), s32[128,2,2,128]{3,1,2,0:T(2,128)S(1)}, u32[]{:S(2)}, u32[]{:S(2)}) async-start(s32[128,2,2,128]{3,1,2,0:T(2,128)} %broadcast_in_dim.237), calls=%async_computation.4 | async-start | bytes 524288 | tf_op jit(solution)/shard_map/all_to_all | solution.py:127
  63.1 33.3 %all-to-all-start.6 = ((bf16[128,2,2,8,128]{4,1,2,3,0:T(2,128)(2,1)}), bf16[128,2,2,8,128]{4,1,2,3,0:T(2,128)(2,1)}, u32[]{:S(2)}, u32[]{:S(2)}) async-start(bf16[128,2,2,8,128]{4,1,2,3,0:T(2,128)(2,1)} %broadcast_in_dim.239), calls=%async_computation.6 | async-start | bytes 2097152 | tf_op jit(solution)/shard_map/all_to_all | solution.py:134
  96.5 10.9 %all-to-all-start.1 = ((s32[128,2,2]{0,1,2:T(2,128)}), s32[128,2,2]{0,1,2:T(2,128)S(1)}, u32[]{:S(2)}, u32[]{:S(2)}) async-start(s32[128,2,2]{0,1,2:T(2,128)} %copy.272), calls=%async_computation.1 | async-start | bytes 4096 | tf_op jit(solution)/shard_map/all_to_all | solution.py:140
  115.6 100.1 %all-to-all-start.2 = ((bf16[128,2,64,128]{3,1,2,0:T(2,128)(2,1)}), bf16[128,2,64,128]{3,1,2,0:T(2,128)(2,1)}, u32[]{:S(2)}, u32[]{:S(2)}) async-start(bf16[128,2,64,128]{3,1,2,0:T(2,128)(2,1)} %copy.277), calls=%async_computation.2 | async-start | bytes 8388608 | tf_op jit(solution)/shard_map/all_to_all | solution.py:120
  123.0 348.5 %reduce-scatter.2.cloned.1.call-start = ((), (), s32[]{:S(2)}) async-start(), calls=%async_computation.15 | async-start | bytes 6291456 | tf_op jit(solution)/shard_map/reduce_scatter | solution.py:187
  367.9 6.6 %copy-start.11 = (bf16[64,64]{1,0:T(8,128)(2,1)S(1)}, bf16[64,64]{1,0:T(8,128)(2,1)}, u32[]{:S(2)}) copy-start(bf16[64,64]{1,0:T(8,128)(2,1)} %param.20) | copy-start | bytes 24580
  397.8 17.6 %all-to-all-start.8 = ((bf16[128,2,256]{2,1,0:T(2,128)(2,1)}), bf16[128,2,256]{2,1,0:T(2,128)(2,1)S(1)}, u32[]{:S(2)}, u32[]{:S(2)}) async-start(bf16[128,2,256]{2,1,0:T(2,128)(2,1)} %reshape.265), calls=%async_computation.8 | async-start | bytes 262144 | tf_op jit(solution)/shard_map/all_to_all | solution.py:163
  416.2 16.9 %copy-start.3 = (bf16[64,64,32,4]{1,3,2,0:T(4,128)(2,1)S(1)}, bf16[64,64,32,4]{1,3,2,0:T(4,128)(2,1)}, u32[]{:S(2)}) copy-start(bf16[64,64,32,4]{1,3,2,0:T(4,128)(2,1)} %get-tuple-element.5) | copy-start | bytes 3145732
  421.9 14.3 %copy-start.2 = (bf16[64,64,32,4]{1,3,2,0:T(4,128)(2,1)S(1)}, bf16[64,64,32,4]{1,3,2,0:T(4,128)(2,1)}, u32[]{:S(2)}) copy-start(bf16[64,64,32,4]{1,3,2,0:T(4,128)(2,1)} %get-tuple-element.6) | copy-start | bytes 3145732
  433.1 20.4 %copy-start.13 = (f32[64]{0:T(128)S(1)}, f32[64]{0:T(128)}, u32[]{:S(2)}) copy-start(f32[64]{0:T(128)} %param.21) | copy-start | bytes 772
  446.3 18.1 %all-to-all-start.11 = ((bf16[128,2,256]{2,1,0:T(2,128)(2,1)}), bf16[128,2,256]{2,1,0:T(2,128)(2,1)S(1)}, u32[]{:S(2)}, u32[]{:S(2)}) async-start(bf16[128,2,256]{2,1,0:T(2,128)(2,1)} %reshape.267), calls=%async_computation.11 | async-start | bytes 262144 | tf_op jit(solution)/shard_map/all_to_all | solution.py:170
  485.5 7.5 %copy-start.4 = (bf16[128,8,128]{2,1,0:T(8,128)(2,1)S(1)}, bf16[128,8,128]{2,1,0:T(8,128)(2,1)}, u32[]{:S(2)}) copy-start(bf16[128,8,128]{2,1,0:T(8,128)(2,1)} %param.14) | copy-start | bytes 786436
  485.5 99.8 %all-to-all-start.12 = ((bf16[128,4,32,128]{3,2,1,0:T(8,128)(2,1)}), bf16[128,4,32,128]{3,2,1,0:T(8,128)(2,1)}, u32[]{:S(2)}, u32[]{:S(2)}) async-start(bf16[128,4,32,128]{3,2,1,0:T(8,128)(2,1)} %copy.310), calls=%async_computation.13 | async-start | bytes 8388608 | tf_op jit(solution)/shard_map/all_to_all | solution.py:194
  600.6 1.3 copy-start.7
  600.6 1.4 copy-start.10
  601.9 2.9 copy-start.5
  604.8 34.8 %copy-start.12 = (bf16[64,128]{1,0:T(8,128)(2,1)S(1)}, bf16[64,128]{1,0:T(8,128)(2,1)}, u32[]{:S(2)}) copy-start(bf16[64,128]{1,0:T(8,128)(2,1)} %param.22) | copy-start | bytes 49156
  604.8 34.8 %copy-start.14 = (bf16[128]{0:T(256)(128)(2,1)S(1)}, bf16[128]{0:T(256)(128)(2,1)}, u32[]{:S(2)}) copy-start(bf16[128]{0:T(256)(128)(2,1)} %param.23) | copy-start | bytes 772
  639.6 5.4 copy-start.1
Sparse Core Ops, SparseCore 0:
  382.5 11.7 reduce-scatter.1
where the time goes:
time: 660 us; the launch traced here: 652 us
  matrix products  226 us (34%)
  waiting for transfers between devices  225 us (34%)
  starting transfers between devices  72.3 us (11%)
  local copies, waits for them, and re-layouts  59.7 us (9%)
  blocking collectives  42.5 us (6%)
  between operations  15.4 us (2%)
  other arithmetic  11.7 us (2%)
    dot_general x9, matrix products, widened(): return jnp.einsum(form, left, right, preferred_element_type=jnp.float32)  179 us
    all_to_all x1, waiting for transfers between devices, shards(): lax.all_to_all(picked, 'slab', split_axis=0, concat_axis=0, tiled=True)  92.2 us
    all_to_all x1, waiting for transfers between devices, shards(): lax.all_to_all(lifted_packed, 'slab', split_axis=0, concat_axis=0, tiled=...  89 us
    dot_general x21, matrix products, precise(): jnp.einsum(form, left, right, precision=lax.Precision.HIGHEST, preferred_...  45 us
    all_to_all x1, starting transfers between devices, shards(): lax.all_to_all(line_ids, 'slab', split_axis=0, concat_axis=0, tiled=True)  16.3 us
    all_to_all x1, waiting for transfers between devices, shards(): lax.all_to_all(weight_packed, 'slab', split_axis=0, concat_axis=0, tiled=...  14.7 us
  transfers between devices with their start and end apart: 9, of which 7 were waited for; matrix products, arithmetic and copies ran while one was open for 12% of the time, Pallas kernels for 0%

commit v1 on v0

v1 whole, which is shorter than its diff:
```python
import math

import jax
import jax.numpy as jnp
import numpy as np
from jax import lax
from jax.experimental import pallas as pl
from jax.experimental.pallas import tpu as pltpu
from jax.sharding import PartitionSpec as P

G = 128
M = 32
PB = 128
NB = 8
C = 64
HALF = 32
BF = jnp.bfloat16
F32 = jnp.float32
LIMIT = 48 * 1024 * 1024
VM = pl.BlockSpec(memory_space=pltpu.VMEM)
SM = pl.BlockSpec(memory_space=pltpu.SMEM)
UNROLL = 4


def trig():
    modes = np.concatenate([np.arange(M // 2), np.arange(M // 2) - M // 2])
    phase = (np.arange(G)[:, None] * modes[None, :] % G) * (2.0 * math.pi / G)
    return np.cos(phase), np.sin(phase)


def call(kernel, out_shape, in_specs, scratch=(), out_specs=None):
    return pl.pallas_call(
        kernel,
        out_shape=out_shape,
        in_specs=in_specs,
        out_specs=VM if out_specs is None else out_specs,
        scratch_shapes=list(scratch),
        compiler_params=pltpu.CompilerParams(vmem_limit_bytes=LIMIT),
    )


def dot(left, right, dims=((1,), (0,))):
    return lax.dot_general(left, right, (dims, ((), ())), preferred_element_type=F32)


def gelu(x):
    inner = x * (0.7978845608028654 + 0.035677408136300125 * (x * x))
    half = 0.5 * x
    return half + half * jnp.tanh(inner)


def near_transposed(start, weight):
    base = lax.broadcasted_iota(jnp.int32, (NB, PB), 0) - start
    which = base & 7
    tile = -(base >> 3)
    picked = jnp.zeros((NB, PB), F32)
    for j in range(NB):
        picked = jnp.where(which == j, weight[j : j + 1, :], picked)
    rows = [jnp.where(tile == t, picked, 0.0) for t in range(G // NB)]
    return jnp.concatenate(rows, axis=0).astype(BF)


def pack_kernel(blk_ref, line_ref, start_ref, weight_ref, out_ref):
    row = lax.broadcasted_iota(jnp.int32, (8, PB), 0)

    def step(s, carry):
        b0, b1 = blk_ref[2 * s], blk_ref[2 * s + 1]
        c0, c1 = jnp.maximum(b0, 0), jnp.maximum(b1, 0)
        l0 = jnp.where(b0 >= 0, line_ref[c0] + 1, 0)
        l1 = jnp.where(b1 >= 0, line_ref[c1] + 1, 0)
        info = jnp.where(
            row == 0,
            start_ref[pl.ds(c0, 1), :],
            jnp.where(
                row == 1,
                start_ref[pl.ds(c1, 1), :],
                jnp.where(row == 2, l0, jnp.where(row == 3, l1, 0)),
            ),
        )
        out_ref[s, 0:8, :] = weight_ref[c0]
        out_ref[s, 8:16, :] = weight_ref[c1]
        out_ref[s, 16:24, :] = info.astype(F32).astype(BF)
        return carry

    lax.fori_loop(0, G, step, 0)


def encode_kernel(slot_ref, count_ref, points_ref, start_ref, weight_ref, lift_ref, out_ref):
    count = count_ref[0]

    def step(group, carry):
        for u in range(UNROLL):
            b = jnp.minimum(group * UNROLL + u, count - 1)
            slot = slot_ref[b]
            slab, rank = slot >> 1, slot & 1
            lifted = dot(lift_ref[...], points_ref[b]).astype(BF)
            near = near_transposed(start_ref[pl.ds(b, 1), :], weight_ref[b].astype(F32))
            part = dot(lifted, near, ((1,), (1,))).astype(BF)
            out_ref[2 * slab, rank] = part[:HALF]
            out_ref[2 * slab + 1, rank] = part[HALF:]
        return carry

    lax.fori_loop(0, (count + UNROLL - 1) // UNROLL, step, 0)


def forward_kernel(line_ref, parts_ref, dy_ref, dz_ref, latent_ref, spec_ref, acc, ybuf):
    acc[...] = jnp.zeros_like(acc)

    def add(src, carry):
        for r in range(2):
            line = line_ref[2 * src + r]
            rows = pl.ds(pl.multiple_of(line * HALF, HALF), HALF)
            acc[rows, :] += parts_ref[src, r].astype(F32)
        return carry

    lax.fori_loop(0, 256, add, 0)
    latent_ref[...] = acc[0 : G * HALF, :].astype(BF)
    for c in range(HALF):
        plane = acc[pl.ds(c, G, stride=HALF), :].astype(BF)
        ybuf[pl.ds(c, 3 * M, stride=HALF), :] = dot(dy_ref[...], plane)
    for q in range(M):
        real = ybuf[q * HALF : (q + 1) * HALF, :].astype(BF)
        imag = ybuf[(M + q) * HALF : (M + q + 1) * HALF, :].astype(BF)
        minus = ybuf[(2 * M + q) * HALF : (2 * M + q + 1) * HALF, :].astype(BF)
        first = jnp.concatenate([real, imag, imag, minus], axis=0)
        second = jnp.concatenate([imag, minus, minus, -imag], axis=0)
        both = jnp.concatenate([first, second], axis=1)
        spec_ref[q * M : (q + 1) * M, :] = dot(dz_ref[...], both, ((1,), (1,))).astype(BF)


def mix_kernel(spec_ref, weight_ref, fwd_ref, bwd_ref, out_ref, xbuf, rhs):
    prod = dot(fwd_ref[...], spec_ref[...])
    for h in range(2):
        cos = prod[h * 256 : h * 256 + 128, 0:64]
        sin = prod[h * 256 + 128 : h * 256 + 256, 64:128]
        xbuf[h] = cos + sin

    def chunk(t, carry):
        rows = pl.ds(pl.multiple_of(t * 32, 32), 32)
        real = jnp.zeros((32, C), F32)
        imag = jnp.zeros((32, C), F32)
        for h in range(2):
            x = xbuf[h, rows, :]
            for c in range(HALF):
                wr = weight_ref[0, h * HALF + c, rows, :].astype(F32)
                wi = weight_ref[1, h * HALF + c, rows, :].astype(F32)
                xr = x[:, c : c + 1]
                xi = x[:, HALF + c : HALF + c + 1]
                real = real + xr * wr - xi * wi
                imag = imag + xr * wi + xi * wr
        for h in range(2):
            mr = real[:, h * HALF : (h + 1) * HALF]
            mi = imag[:, h * HALF : (h + 1) * HALF]
            top = jnp.concatenate([mr, mi, -mi, mr], axis=1).astype(BF)
            low = jnp.concatenate([-mi, mr, -mr, -mi], axis=1).astype(BF)
            rhs[pl.ds(pl.multiple_of(h * 256 + t * 32, 32), 32), :] = top
            rhs[pl.ds(pl.multiple_of(h * 256 + 128 + t * 32, 32), 32), :] = low
        return carry

    lax.fori_loop(0, 4, chunk, 0)
    out_ref[...] = dot(bwd_ref[...], rhs[...]).astype(BF)


def inverse_kernel(back_ref, own_ref, other_ref, skip_ref, bias_ref, ez_ref, ey_ref, out_ref, ubuf, sbuf):
    for q in range(M):
        both = dot(back_ref[q * M : (q + 1) * M, :], ez_ref[...], ((0,), (0,)))
        ubuf[q * C : (q + 1) * C, :] = both[0:C, 0:G] + both[C : 2 * C, G : 2 * G]
    for c in range(HALF):
        lines = ubuf[pl.ds(c, 2 * M, stride=HALF), :].astype(BF)
        sbuf[pl.ds(c, G, stride=HALF), :] = dot(ey_ref[...], lines)

    def step(group, carry):
        for u in range(4):
            rows = pl.ds(pl.multiple_of((group * 4 + u) * HALF, HALF), HALF)
            latent = jnp.concatenate([own_ref[rows, :], other_ref[rows, :]], axis=0)
            total = sbuf[rows, :] + dot(skip_ref[...], latent) + bias_ref[...]
            out_ref[rows, :] = gelu(total).astype(BF)
        return carry

    lax.fori_loop(0, G // 4, step, 0)


def decode_kernel(line_ref, meta_ref, own_ref, other_ref, proj_in_ref, proj_out_ref, out_ref, todo):
    def collect(s, count):
        todo[count] = s
        return count + jnp.where(line_ref[s] < G, 1, 0)

    count = lax.fori_loop(0, 256, collect, 0)

    def step(group, carry):
        for u in range(UNROLL):
            s = todo[jnp.minimum(group * UNROLL + u, count - 1)]
            src, rank = s >> 1, s & 1
            line = line_ref[s]
            rows = pl.ds(pl.multiple_of(line * HALF, HALF), HALF)
            cells = jnp.concatenate([own_ref[rows, :], other_ref[rows, :]], axis=0)
            info = meta_ref[src, 16:24, :].astype(F32)
            start = jnp.where(rank == 0, info[0:1, :], info[1:2, :]).astype(jnp.int32)
            weight = meta_ref[src, pl.ds(pl.multiple_of(rank * 8, 8), 8), :].astype(F32)
            near = near_transposed(start, weight)
            value = dot(cells, near).astype(BF)
            hidden = gelu(dot(proj_in_ref[...], value)).astype(BF)
            out_ref[pl.ds(s, 1), :] = dot(proj_out_ref[...], hidden)[0:1, :]
        return carry

    lax.fori_loop(0, (count + UNROLL - 1) // UNROLL, step, 0)


def unpack_kernel(slot_ref, values_ref, out_ref):
    def step(b, carry):
        slot = slot_ref[b]
        row = values_ref[pl.ds(jnp.maximum(slot, 0), 1), :]
        out_ref[pl.ds(b, 1), :] = jnp.where(slot >= 0, row, 0.0)
        return carry

    lax.fori_loop(0, 128, step, 0, unroll=8)


def shards(
    points,
    near_start,
    near_weight,
    dest_slab,
    dest_block,
    live_count,
    lift_w,
    spec_weight,
    skip_w,
    skip_bias,
    proj_in,
    proj_out,
):
    cos, sin = trig()
    chan = lax.axis_index("chan")
    every = ("slab", "chan")

    ids = jnp.arange(128, dtype=jnp.int32)
    live = ids < live_count[0]
    target = jnp.where(live, dest_slab[:, 0], -1)
    same = (target[:, None] == target[None, :]) & (ids[None, :] < ids[:, None])
    rank = jnp.sum(same.astype(jnp.int32), axis=1)
    slot = jnp.where(live, target * 2 + rank, -1)
    slot_ids = jnp.arange(256, dtype=jnp.int32)
    block = jnp.max(jnp.where(slot[None, :] == slot_ids[:, None], ids[None, :], -1), axis=1)

    meta = call(pack_kernel, jax.ShapeDtypeStruct((128, 24, PB), BF), [SM, SM, VM, VM])(
        block, dest_block, near_start, near_weight
    )
    meta = lax.all_to_all(meta, "slab", split_axis=0, concat_axis=0, tiled=True)
    parts = call(encode_kernel, jax.ShapeDtypeStruct((256, 2, HALF, G), BF), [SM, SM] + [VM] * 4)(
        slot, live_count, points, near_start, near_weight, lift_w.T
    )
    parts = lax.all_to_all(parts, every, split_axis=0, concat_axis=0, tiled=True)

    lines = meta[:, 18:20, 0].astype(jnp.int32)
    lines = jnp.where(lines > 0, lines - 1, G)
    lines_other = lax.ppermute(lines, "chan", [(0, 1), (1, 0)])
    first = jnp.where(chan == 0, lines, lines_other)
    second = jnp.where(chan == 0, lines_other, lines)
    all_lines = jnp.stack([first, second], axis=1).reshape(512)

    dy = jnp.asarray(np.concatenate([cos.T, -sin.T, -cos.T], axis=0), BF)
    dz = jnp.asarray(np.concatenate([cos.T, sin.T], axis=1), BF)
    latent, spectra = call(
        forward_kernel,
        (jax.ShapeDtypeStruct((G * HALF, G), BF), jax.ShapeDtypeStruct((M * M, 128), BF)),
        [SM] + [VM] * 3,
        [pltpu.VMEM(((G + 1) * HALF, G), F32), pltpu.VMEM((3 * M * HALF, G), F32)],
        (VM, VM),
    )(all_lines, parts, dy, dz)
    latent_other = lax.ppermute(latent, "chan", [(0, 1), (1, 0)])
    spectra = lax.all_to_all(spectra.reshape(256, 4, 128), every, split_axis=0, concat_axis=0, tiled=True)

    eye4, eye2 = np.eye(4), np.eye(2)
    table = np.stack([cos.T, sin.T])
    forward = np.einsum("hg,vkx,mn->hvkmxgn", eye2, table, eye4).reshape(512, 1024)
    weight = jnp.transpose(spec_weight, (0, 1, 3, 4, 2)).reshape(2, C, 128, C)
    back = call(
        mix_kernel,
        jax.ShapeDtypeStruct((1024, 128), BF),
        [VM] * 4,
        [pltpu.VMEM((2, 128, C), F32), pltpu.VMEM((512, 128), BF)],
    )(spectra.reshape(1024, 128), weight, jnp.asarray(forward, BF), jnp.asarray(forward.T, BF))
    back = lax.all_to_all(back.reshape(256, 4, 128), every, split_axis=0, concat_axis=0, tiled=True)

    own = chan * HALF
    other = (1 - chan) * HALF
    skip_own = lax.dynamic_slice_in_dim(skip_w, own, HALF, 1)
    skip = jnp.concatenate(
        [
            lax.dynamic_slice_in_dim(skip_own, own, HALF, 0),
            lax.dynamic_slice_in_dim(skip_own, other, HALF, 0),
        ],
        axis=0,
    ).T
    bias = jnp.broadcast_to(lax.dynamic_slice_in_dim(skip_bias, own, HALF, 0)[:, None], (HALF, G))
    ez = jnp.asarray(np.concatenate([cos.T, sin.T], axis=1), BF)
    ey = jnp.asarray(np.stack([cos, -sin], axis=2).reshape(G, 2 * M) / G**3, BF)
    grid = call(
        inverse_kernel,
        jax.ShapeDtypeStruct((G * HALF, G), BF),
        [VM] * 7,
        [pltpu.VMEM((M * C, G), F32), pltpu.VMEM((G * HALF, G), F32)],
    )(back.reshape(1024, 128), latent, latent_other, skip, bias, ez, ey)
    grid_other = lax.ppermute(grid, "chan", [(0, 1), (1, 0)])

    proj = jnp.concatenate(
        [
            lax.dynamic_slice_in_dim(proj_in, own, HALF, 0),
            lax.dynamic_slice_in_dim(proj_in, other, HALF, 0),
        ],
        axis=0,
    ).T
    proj_row = jnp.broadcast_to(proj_out[None, :], (8, 128))
    values = call(
        decode_kernel,
        jax.ShapeDtypeStruct((256, PB), F32),
        [SM] + [VM] * 5,
        [pltpu.SMEM((257,), jnp.int32)],
    )(lines.reshape(256), meta, grid, grid_other, proj, proj_row)
    values = lax.all_to_all(values.reshape(128, 2, PB), "slab", split_axis=0, concat_axis=0, tiled=True)
    return call(unpack_kernel, jax.ShapeDtypeStruct((128, PB), F32), [SM, VM])(slot, values.reshape(256, PB))


def solution(mesh):
    placed = (
        P(("slab", "chan"), None, None),
        P(("slab", "chan"), None),
        P(("slab", "chan"), None, None),
        P(("slab", "chan"), None),
        P(("slab", "chan")),
        P(("slab", "chan")),
        P(),
        P(None, None, None, None, ("slab", "chan")),
        P(),
        P(),
        P(),
        P(),
    )
    return jax.shard_map(
        shards, mesh=mesh, in_specs=placed, out_specs=P(("slab", "chan"), None), check_vma=False
    )
```

time: 660 us -> 301 us (0.46); the launches traced: 652 us -> 300 us
  matrix products: 226 us -> 0 us
  waiting for transfers between devices: 225 us -> 112 us
  Pallas kernels: 0 us -> 67.7 us
  local copies, waits for them, and re-layouts: 59.7 us -> 12.6 us
  starting transfers between devices: 72.3 us -> 36.3 us
  blocking collectives: 42.5 us -> 66 us
  between operations: 15.4 us -> 0.83 us
  other arithmetic: 11.7 us -> 4.69 us
    dot_general x30 -> x0, matrix products: 224 us -> none  [the longest x9 179 us: widened(): return jnp.einsum(form, left, right, preferred_element_type=jnp.float32)]
    all_to_all x8 -> x3, waiting for transfers between devices: 225 us -> 109 us  [the longest x1 91.6 us: shards(): lax.all_to_all(parts, every, split_axis=0, concat_axis=0, tiled=True)]
    pallas_call x0 -> x7, Pallas kernels: none -> 67.7 us  [the longest x1 23.3 us: shards(): call(decode_kernel, jax.ShapeDtypeStruct((256, PB), F32), [SM] + [VM] * 5...]
    all_to_all x8 -> x3, starting transfers between devices: 72.2 us -> 32.9 us  [the longest x1 16.3 us: shards(): meta = lax.all_to_all(meta, 'slab', split_axis=0, concat_axis=0, tiled=True)]
    all_to_all x6 -> x2, blocking collectives: 42.5 us -> 66 us  [the longest x1 45.1 us: shards(): lax.all_to_all(values.reshape(128, 2, PB), 'slab', split_axis=0, concat_a...]
    all_to_all x16 -> x0, local copies, waits for them, and re-layouts: 22.6 us -> none  [the longest x1 6.78 us: shards(): lax.all_to_all(lifted_packed, 'slab', split_axis=0, concat_axis=0, tiled=...]
    reshape x2 -> x1, local copies, waits for them, and re-layouts: 13.6 us -> 0.19 us  [shards(): all_lines = jnp.stack([first, second], axis=1).reshape(512)]
    reduce_sum x3 -> x1, other arithmetic: 9.25 us -> 0.17 us  [shards(): rank = jnp.sum(same.astype(jnp.int32), axis=1)]
  transfers between devices with their start and end apart: 9 -> 6, of which waited for: 7 -> 5; matrix products, arithmetic and copies ran while one was open for 12% -> 1% of each run, Pallas kernels for 0% -> 8%
where the time goes in v1:
time: 301 us; the launch traced here: 300 us
  waiting for transfers between devices  112 us (37%)
  Pallas kernels  67.7 us (22%)
  blocking collectives  66 us (22%)
  starting transfers between devices  36.3 us (12%)
  local copies, waits for them, and re-layouts  12.6 us (4%)
  other arithmetic  4.69 us (2%)
    all_to_all x1, waiting for transfers between devices, shards(): lax.all_to_all(parts, every, split_axis=0, concat_axis=0, tiled=True)  91.6 us
    all_to_all x1, blocking collectives, shards(): lax.all_to_all(values.reshape(128, 2, PB), 'slab', split_axis=0, concat_a...  45.1 us
    pallas_call x1, Pallas kernels, shards(): call(decode_kernel, jax.ShapeDtypeStruct((256, PB), F32), [SM] + [VM] * 5...  23.3 us
    all_to_all x1, blocking collectives, shards(): lax.all_to_all(spectra.reshape(256, 4, 128), every, split_axis=0, concat_...  20.9 us
    all_to_all x1, starting transfers between devices, shards(): meta = lax.all_to_all(meta, 'slab', split_axis=0, concat_axis=0, tiled=True)  16.3 us
    all_to_all x1, waiting for transfers between devices, shards(): lax.all_to_all(back.reshape(256, 4, 128), every, split_axis=0, concat_axi...  15 us
    pallas_call x1, Pallas kernels, shards(): call(encode_kernel, jax.ShapeDtypeStruct((256, 2, HALF, G), BF), [SM, SM]...  14.8 us
    unnamed x39, local copies, waits for them, and re-layouts  11.8 us
  transfers between devices with their start and end apart: 6, of which 5 were waited for; matrix products, arithmetic and copies ran while one was open for 1% of the time, Pallas kernels for 8%

profile of v1, /device:TPU:1, one launch (start us, length us, event | category | flops | bytes accessed | tf_op | source)
XLA Modules:
  0.0 300.4 jit_solution(9710813169232235094)
XLA Ops:
  0.7 0.7 compare_select_fusion.3
  2.1 0.7 compare_select_fusion.2.slot_ref
  3.0 0.9 copy-done.1
  3.9 0.8 copy-done.7
  5.4 3.5 %shard_map.172 = bf16[128,24,128]{2,1,0:T(8,128)(2,1)} custom-call(s32[256]{0:T(256)S(1)} %select_reduce_fusion.blk_ref, s32[128]{0:T(128)S(1)} %copy-done.12, s32[128,128]{1,0:T(8,128)S(1)} %copy-done.7, bf16[128,8,128]{2,1,0:T(8,128)(2,1)S(1)} %copy-done.1), custom_call_target="tpu_custom_call" | custom-call | tf_op jit(solution)/shard_map/pallas_call | solution.py:246
  8.9 16.3 %all-to-all-start = ((bf16[128,24,128]{2,1,0:T(8,128)(2,1)}), bf16[128,24,128]{2,1,0:T(8,128)(2,1)S(1)}, u32[]{:S(2)}, u32[]{:S(2)}) async-start(bf16[128,24,128]{2,1,0:T(8,128)(2,1)} %shard_map.172), calls=%async_computation | async-start | bytes 1572864 | tf_op jit(solution)/shard_map/all_to_all | solution.py:249
  25.3 0.8 copy.33
  26.1 1.6 copy-done
  27.7 0.9 copy-done.2
  28.6 0.8 copy-done.8
  29.5 14.8 %shard_map.173 = bf16[256,2,32,128]{3,2,1,0:T(8,128)(2,1)} custom-call(s32[128]{0:T(128)S(1)} %compare_select_fusion.2.slot_ref, s32[1]{0:T(128)} %copy.42.count_ref, bf16[128,64,128]{2,1,0:T(8,128)(2,1)S(1)} %copy-done, s32[128,128]{1,0:T(8,128)S(1)} %copy-done.8, bf16[128,8,128]{2,1,0:T(8,128)(2,1)S(1)} %copy-done.2, bf16[64,64]{1,0:T(8,128)(2,1)S(1)} %bitcast.36), custom_call_target="tpu_custom_call" | custom-call | tf_op jit(solution)/shard_map/pallas_call | solution.py:250
  44.3 2.6 all-to-all-done.meta_ref
  46.9 11.4 %all-to-all-start.1 = ((bf16[256,2,32,128]{3,2,1,0:T(8,128)(2,1)}), bf16[256,2,32,128]{3,2,1,0:T(8,128)(2,1)}, u32[]{:S(2)}, u32[]{:S(2)}) async-start(bf16[256,2,32,128]{3,2,1,0:T(8,128)(2,1)} %shard_map.173), calls=%async_computation.1 | async-start | bytes 8388608 | tf_op jit(solution)/shard_map/all_to_all | solution.py:253
  58.3 2.2 compare_select_fusion
  60.7 2.3 collective-permute-start
  62.9 0.8 collective-permute-done
  64.1 91.6 %all-to-all-done.1.parts_ref = bf16[256,2,32,128]{3,2,1,0:T(8,128)(2,1)} async-done(((bf16[256,2,32,128]{3,2,1,0:T(8,128)(2,1)}), bf16[256,2,32,128]{3,2,1,0:T(8,128)(2,1)}, u32[]{:S(2)}, u32[]{:S(2)}) %all-to-all-start.1) | async-done | bytes 4194336 | tf_op jit(solution)/shard_map/all_to_all | solution.py:253
  155.7 8.3 %shard_map.174 = (bf16[4096,128]{1,0:T(8,128)(2,1)S(1)}, bf16[1024,128]{1,0:T(8,128)(2,1)S(1)}) custom-call(s32[512]{0:T(512)S(1)} %reshape.68.line_ref, bf16[256,2,32,128]{3,2,1,0:T(8,128)(2,1)} %all-to-all-done.1.parts_ref, bf16[96,128]{1,0:T(8,128)(2,1)S(1)} %copy-done.11, bf16[32,256]{1,0:T(8,128)(2,1)S(1)} %copy-done.9), custom_call_target="tpu_custom_call" | custom-call | tf_op jit(solution)/shard_map/pallas_call | solution.py:264
  164.0 1.1 collective-permute-start.1
  165.1 20.9 %all_to_all.25 = bf16[256,4,128]{2,1,0:T(4,128)(2,1)S(1)} all-to-all(bf16[256,4,128]{2,1,0:T(4,128)(2,1)S(1)} %bitcast.35), channel_id=1, replica_groups=mesh['slab'=128,'chan'=2] {'slab','chan'}, dimensions={0} | all-to-all | bytes 524288 | tf_op jit(solution)/shard_map/all_to_all | solution.py:272
  186.0 1.2 copy-done.5
  187.2 1.2 copy-done.6
  188.5 8.5 %shard_map.175 = bf16[1024,128]{1,0:T(8,128)(2,1)} custom-call(bf16[1024,128]{1,0:T(8,128)(2,1)S(1)} %bitcast.32, bf16[2,64,128,64]{3,2,1,0:T(8,128)(2,1)} %bitcast.37, bf16[512,1024]{1,0:T(8,128)(2,1)S(1)} %copy-done.5, bf16[1024,512]{1,0:T(8,128)(2,1)S(1)} %copy-done.6), custom_call_target="tpu_custom_call" | custom-call | tf_op jit(solution)/shard_map/pallas_call | solution.py:278
  197.0 5.2 %all-to-all-start.3 = ((bf16[256,4,128]{2,1,0:T(4,128)(2,1)}), bf16[256,4,128]{2,1,0:T(4,128)(2,1)S(1)}, u32[]{:S(2)}, u32[]{:S(2)}) async-start(bf16[256,4,128]{2,1,0:T(4,128)(2,1)} %bitcast.11), calls=%async_computation.3 | async-start | bytes 524288 | tf_op jit(solution)/shard_map/all_to_all | solution.py:284
  202.6 15.0 %all-to-all-done.3 = bf16[256,4,128]{2,1,0:T(4,128)(2,1)S(1)} async-done(((bf16[256,4,128]{2,1,0:T(4,128)(2,1)}), bf16[256,4,128]{2,1,0:T(4,128)(2,1)S(1)}, u32[]{:S(2)}, u32[]{:S(2)}) %all-to-all-start.3) | async-done | bytes 262176 | tf_op jit(solution)/shard_map/all_to_all | solution.py:284
  217.6 1.0 copy-done.3
  218.7 1.2 copy-done.4
  219.9 7.7 %shard_map.176.own_ref = bf16[4096,128]{1,0:T(8,128)(2,1)S(1)} custom-call(bf16[1024,128]{1,0:T(8,128)(2,1)S(1)} %bitcast.31, bf16[4096,128]{1,0:T(8,128)(2,1)S(1)} %get-tuple-element.8.own_ref, bf16[4096,128]{1,0:T(8,128)(2,1)S(1)} %copy-done.4, bf16[32,64]{1,0:T(8,128)(2,1)S(1)} %maximum_bitcast_fusion.1.skip_ref, ...), custom_call_target="tpu_custom_call" | custom-call | tf_op jit(solution)/shard_map/pallas_call | solution.py:299
  228.3 2.1 collective-permute-done.2.other_ref
  230.4 23.3 %shard_map.177 = f32[256,128]{1,0:T(8,128)S(1)} custom-call(s32[256]{0:T(256)S(1)} %select_n.63.line_ref, bf16[128,24,128]{2,1,0:T(8,128)(2,1)S(1)} %all-to-all-done.meta_ref, bf16[4096,128]{1,0:T(8,128)(2,1)S(1)} %shard_map.176.own_ref, bf16[4096,128]{1,0:T(8,128)(2,1)S(1)} %collective-permute-done.2.other_ref, ...), custom_call_target="tpu_custom_call" | custom-call | tf_op jit(solution)/shard_map/pallas_call | solution.py:315
  253.8 45.1 %all_to_all.26 = f32[128,2,128]{2,1,0:T(2,128)S(1)} all-to-all(f32[128,2,128]{2,1,0:T(2,128)S(1)} %bitcast.33), channel_id=1, replica_groups=mesh['slab'=128,'chan'=2] {'slab'}, dimensions={0} | all-to-all | bytes 262144 | tf_op jit(solution)/shard_map/all_to_all | solution.py:321
  298.8 1.5 shard_map.178
  (47 shorter events, 3.2 us)
Async XLA Ops:
  2.9 1.0 copy-start.1
  3.9 0.8 copy-start.7
  4.7 0.7 copy-start.12
  8.9 38.0 %all-to-all-start = ((bf16[128,24,128]{2,1,0:T(8,128)(2,1)}), bf16[128,24,128]{2,1,0:T(8,128)(2,1)S(1)}, u32[]{:S(2)}, u32[]{:S(2)}) async-start(bf16[128,24,128]{2,1,0:T(8,128)(2,1)} %shard_map.172), calls=%async_computation | async-start | bytes 1572864 | tf_op jit(solution)/shard_map/all_to_all | solution.py:249
  26.1 1.6 copy-start
  27.7 0.9 copy-start.2
  28.6 0.8 copy-start.8
  44.3 111.4 %copy-start.9 = (bf16[32,256]{1,0:T(8,128)(2,1)S(1)}, bf16[32,256]{1,0:T(8,128)(2,1)}, u32[]{:S(2)}) copy-start(bf16[32,256]{1,0:T(8,128)(2,1)} %constant.54.clone.dz_ref.ez_ref) | copy-start | bytes 49156
  44.3 111.4 %copy-start.11 = (bf16[96,128]{1,0:T(8,128)(2,1)S(1)}, bf16[96,128]{1,0:T(8,128)(2,1)}, u32[]{:S(2)}) copy-start(bf16[96,128]{1,0:T(8,128)(2,1)} %constant.53.clone.dy_ref) | copy-start | bytes 73732
  46.9 108.8 %all-to-all-start.1 = ((bf16[256,2,32,128]{3,2,1,0:T(8,128)(2,1)}), bf16[256,2,32,128]{3,2,1,0:T(8,128)(2,1)}, u32[]{:S(2)}, u32[]{:S(2)}) async-start(bf16[256,2,32,128]{3,2,1,0:T(8,128)(2,1)} %shard_map.173), calls=%async_computation.1 | async-start | bytes 8388608 | tf_op jit(solution)/shard_map/all_to_all | solution.py:253
  60.7 3.1 %collective-permute-start = (s32[128,2]{0,1:T(2,128)S(1)}, s32[128,2]{0,1:T(2,128)S(1)}, u32[]{:S(2)}, u32[]{:S(2)}) collective-permute-start(s32[128,2]{0,1:T(2,128)S(1)} %bitcast.38), channel_id=1, source_target_pairs={{0,1},{1,0},{2,3},{3,2},{4,5},{5,4},{6,7},{7,6},{8,9},{9,8},{10,11... | collective-permute-start | bytes 3080 | tf_op jit(solution)/shard_map/ppermute | solution.py:257
  164.0 38.2 %copy-start.13 = (bf16[64,64]{1,0:T(8,128)(2,1)S(1)}, bf16[64,64]{1,0:T(8,128)(2,1)}, u32[]{:S(2)}) copy-start(bf16[64,64]{1,0:T(8,128)(2,1)} %param.26) | copy-start | bytes 24580
  164.0 38.4 %copy-start.16 = (f32[64]{0:T(128)S(1)}, f32[64]{0:T(128)}, u32[]{:S(2)}) copy-start(f32[64]{0:T(128)} %param.27) | copy-start | bytes 772
  164.0 54.7 %copy-start.10 = (bf16[128,64]{1,0:T(8,128)(2,1)S(1)}, bf16[128,64]{1,0:T(8,128)(2,1)}, u32[]{:S(2)}) copy-start(bf16[128,64]{1,0:T(8,128)(2,1)} %constant.57.clone.ey_ref) | copy-start | bytes 49156
  164.0 53.6 %collective-permute-start.1 = (bf16[4096,128]{1,0:T(8,128)(2,1)S(1)}, bf16[4096,128]{1,0:T(8,128)(2,1)S(1)}, u32[]{:S(2)}, u32[]{:S(2)}) collective-permute-start(bf16[4096,128]{1,0:T(8,128)(2,1)S(1)} %get-tuple-element.8.own_ref), channel_id=1, source_target_pairs={{0,1},{1,0},{2,3},{3,2},{4,5},{5,4},{6,7},{7,6},{8,9},{9,8},{10,11... | collective-permute-start | bytes 3145736 | tf_op jit(solution)/shard_map/ppermute | solution.py:271
  186.0 1.2 copy-start.5
  187.2 1.2 copy-start.6
  188.5 39.3 %copy-start.14 = (bf16[64,128]{1,0:T(8,128)(2,1)S(1)}, bf16[64,128]{1,0:T(8,128)(2,1)}, u32[]{:S(2)}) copy-start(bf16[64,128]{1,0:T(8,128)(2,1)} %param.28) | copy-start | bytes 49156
  188.5 42.0 %copy-start.15 = (bf16[128]{0:T(256)(128)(2,1)S(1)}, bf16[128]{0:T(256)(128)(2,1)}, u32[]{:S(2)}) copy-start(bf16[128]{0:T(256)(128)(2,1)} %param.29) | copy-start | bytes 772
  197.0 20.7 %all-to-all-start.3 = ((bf16[256,4,128]{2,1,0:T(4,128)(2,1)}), bf16[256,4,128]{2,1,0:T(4,128)(2,1)S(1)}, u32[]{:S(2)}, u32[]{:S(2)}) async-start(bf16[256,4,128]{2,1,0:T(4,128)(2,1)} %bitcast.11), calls=%async_computation.3 | async-start | bytes 524288 | tf_op jit(solution)/shard_map/all_to_all | solution.py:284
  217.6 1.0 copy-start.3
  218.7 1.2 copy-start.4
  227.7 2.7 collective-permute-start.2

commit v2 on v1

--- a/solution.py
+++ b/solution.py
@@ -19,7 +19,7 @@
 LIMIT = 48 * 1024 * 1024
 VM = pl.BlockSpec(memory_space=pltpu.VMEM)
 SM = pl.BlockSpec(memory_space=pltpu.SMEM)
-UNROLL = 4
+WIDE = 16
 
 
 def trig():
@@ -89,18 +89,21 @@
     count = count_ref[0]
 
     def step(group, carry):
-        for u in range(UNROLL):
-            b = jnp.minimum(group * UNROLL + u, count - 1)
-            slot = slot_ref[b]
+        blocks = [jnp.minimum(group * WIDE + u, count - 1) for u in range(WIDE)]
+        nears = [
+            near_transposed(start_ref[pl.ds(b, 1), :], weight_ref[b].astype(F32)) for b in blocks
+        ]
+        points = jnp.concatenate([points_ref[b] for b in blocks], axis=1)
+        lifted = dot(lift_ref[...], points).astype(BF)
+        for u in range(WIDE):
+            slot = slot_ref[blocks[u]]
             slab, rank = slot >> 1, slot & 1
-            lifted = dot(lift_ref[...], points_ref[b]).astype(BF)
-            near = near_transposed(start_ref[pl.ds(b, 1), :], weight_ref[b].astype(F32))
-            part = dot(lifted, near, ((1,), (1,))).astype(BF)
+            part = dot(lifted[:, u * PB : (u + 1) * PB], nears[u], ((1,), (1,))).astype(BF)
             out_ref[2 * slab, rank] = part[:HALF]
             out_ref[2 * slab + 1, rank] = part[HALF:]
         return carry
 
-    lax.fori_loop(0, (count + UNROLL - 1) // UNROLL, step, 0)
+    lax.fori_loop(0, (count + WIDE - 1) // WIDE, step, 0)
 
 
 def forward_kernel(line_ref, parts_ref, dy_ref, dz_ref, latent_ref, spec_ref, acc, ybuf):
@@ -188,22 +191,25 @@
     count = lax.fori_loop(0, 256, collect, 0)
 
     def step(group, carry):
-        for u in range(UNROLL):
-            s = todo[jnp.minimum(group * UNROLL + u, count - 1)]
+        slots, cells, nears = [], [], []
+        for u in range(WIDE):
+            s = todo[jnp.minimum(group * WIDE + u, count - 1)]
             src, rank = s >> 1, s & 1
-            line = line_ref[s]
-            rows = pl.ds(pl.multiple_of(line * HALF, HALF), HALF)
-            cells = jnp.concatenate([own_ref[rows, :], other_ref[rows, :]], axis=0)
+            rows = pl.ds(pl.multiple_of(line_ref[s] * HALF, HALF), HALF)
             info = meta_ref[src, 16:24, :].astype(F32)
             start = jnp.where(rank == 0, info[0:1, :], info[1:2, :]).astype(jnp.int32)
             weight = meta_ref[src, pl.ds(pl.multiple_of(rank * 8, 8), 8), :].astype(F32)
-            near = near_transposed(start, weight)
-            value = dot(cells, near).astype(BF)
-            hidden = gelu(dot(proj_in_ref[...], value)).astype(BF)
-            out_ref[pl.ds(s, 1), :] = dot(proj_out_ref[...], hidden)[0:1, :]
-        return carry
-
-    lax.fori_loop(0, (count + UNROLL - 1) // UNROLL, step, 0)
+            slots.append(s)
+            cells.append(jnp.concatenate([own_ref[rows, :], other_ref[rows, :]], axis=0))
+            nears.append(near_transposed(start, weight))
+        values = [dot(cells[u], nears[u]).astype(BF) for u in range(WIDE)]
+        hidden = gelu(dot(proj_in_ref[...], jnp.concatenate(values, axis=1))).astype(BF)
+        result = dot(proj_out_ref[...], hidden)
+        for u in range(WIDE):
+            out_ref[pl.ds(slots[u], 1), :] = result[0:1, u * PB : (u + 1) * PB]
+        return carry
+
+    lax.fori_loop(0, (count + WIDE - 1) // WIDE, step, 0)
 
 
 def unpack_kernel(slot_ref, values_ref, out_ref):

time: 301 us -> 261 us (0.87)
  Pallas kernels: 67.7 us -> 44 us
  blocking collectives: 66 us -> 43 us
  waiting for transfers between devices: 112 us -> 120 us
    all_to_all x1, blocking collectives: 45.1 us -> 22 us  [shards(): lax.all_to_all(values.reshape(128, 2, PB), 'slab', split_axis=0, concat_a...]
    pallas_call x1, Pallas kernels: 23.3 us -> 7.38 us  [shards(): call(decode_kernel, jax.ShapeDtypeStruct((256, PB), F32), [SM] + [VM] * 5...]
    all_to_all x1, waiting for transfers between devices: 2.65 us -> 10.4 us  [shards(): meta = lax.all_to_all(meta, 'slab', split_axis=0, concat_axis=0, tiled=True)]
    pallas_call x1, Pallas kernels: 14.8 us -> 7.04 us  [shards(): call(encode_kernel, jax.ShapeDtypeStruct((256, 2, HALF, G), BF), [SM, SM]...]
  transfers between devices with their start and end apart: 6 -> 6, of which waited for: 5 -> 5; matrix products, arithmetic and copies ran while one was open for 1% -> 2% of each run, Pallas kernels for 8% -> 6%
where the time goes in v2:
time: 261 us; the launch traced here: 260 us
  waiting for transfers between devices  120 us (46%)
  Pallas kernels  44 us (17%)
  blocking collectives  43 us (16%)
  starting transfers between devices  35.4 us (14%)
  local copies, waits for them, and re-layouts  12.6 us (5%)
  other arithmetic  4.69 us (2%)
    all_to_all x1, waiting for transfers between devices, shards(): lax.all_to_all(parts, every, split_axis=0, concat_axis=0, tiled=True)  91.5 us
    all_to_all x1, blocking collectives, shards(): lax.all_to_all(values.reshape(128, 2, PB), 'slab', split_axis=0, concat_a...  22 us
    all_to_all x1, blocking collectives, shards(): lax.all_to_all(spectra.reshape(256, 4, 128), every, split_axis=0, concat_...  21 us
    all_to_all x1, starting transfers between devices, shards(): meta = lax.all_to_all(meta, 'slab', split_axis=0, concat_axis=0, tiled=True)  16.3 us
    all_to_all x1, waiting for transfers between devices, shards(): lax.all_to_all(back.reshape(256, 4, 128), every, split_axis=0, concat_axi...  15 us
    unnamed x39, local copies, waits for them, and re-layouts  11.8 us
    all_to_all x1, waiting for transfers between devices, shards(): meta = lax.all_to_all(meta, 'slab', split_axis=0, concat_axis=0, tiled=True)  10.4 us
    all_to_all x1, starting transfers between devices, shards(): lax.all_to_all(parts, every, split_axis=0, concat_axis=0, tiled=True)  10.4 us
  transfers between devices with their start and end apart: 6, of which 5 were waited for; matrix products, arithmetic and copies ran while one was open for 2% of the time, Pallas kernels for 6%

profile of v2, /device:TPU:1, one launch (start us, length us, event | category | flops | bytes accessed | tf_op | source)
XLA Modules:
  0.0 260.4 jit_solution(9313706001839431465)
XLA Ops:
  0.7 0.7 compare_select_fusion.3
  2.1 0.7 compare_select_fusion.2.slot_ref
  3.0 0.9 copy-done.1
  3.9 0.8 copy-done.7
  5.4 3.5 %shard_map.172 = bf16[128,24,128]{2,1,0:T(8,128)(2,1)} custom-call(s32[256]{0:T(256)S(1)} %select_reduce_fusion.blk_ref, s32[128]{0:T(128)S(1)} %copy-done.12, s32[128,128]{1,0:T(8,128)S(1)} %copy-done.7, bf16[128,8,128]{2,1,0:T(8,128)(2,1)S(1)} %copy-done.1), custom_call_target="tpu_custom_call" | custom-call | tf_op jit(solution)/shard_map/pallas_call | solution.py:252
  8.9 16.3 %all-to-all-start = ((bf16[128,24,128]{2,1,0:T(8,128)(2,1)}), bf16[128,24,128]{2,1,0:T(8,128)(2,1)S(1)}, u32[]{:S(2)}, u32[]{:S(2)}) async-start(bf16[128,24,128]{2,1,0:T(8,128)(2,1)} %shard_map.172), calls=%async_computation | async-start | bytes 1572864 | tf_op jit(solution)/shard_map/all_to_all | solution.py:255
  25.3 0.8 copy.33
  26.1 1.6 copy-done
  27.7 0.9 copy-done.2
  28.6 0.8 copy-done.8
  29.5 7.0 %shard_map.173 = bf16[256,2,32,128]{3,2,1,0:T(8,128)(2,1)} custom-call(s32[128]{0:T(128)S(1)} %compare_select_fusion.2.slot_ref, s32[1]{0:T(128)} %copy.42.count_ref, bf16[128,64,128]{2,1,0:T(8,128)(2,1)S(1)} %copy-done, s32[128,128]{1,0:T(8,128)S(1)} %copy-done.8, bf16[128,8,128]{2,1,0:T(8,128)(2,1)S(1)} %copy-done.2, bf16[64,64]{1,0:T(8,128)(2,1)S(1)} %bitcast.36), custom_call_target="tpu_custom_call" | custom-call | tf_op jit(solution)/shard_map/pallas_call | solution.py:256
  36.5 10.4 %all-to-all-done.meta_ref = bf16[128,24,128]{2,1,0:T(8,128)(2,1)S(1)} async-done(((bf16[128,24,128]{2,1,0:T(8,128)(2,1)}), bf16[128,24,128]{2,1,0:T(8,128)(2,1)S(1)}, u32[]{:S(2)}, u32[]{:S(2)}) %all-to-all-start) | async-done | bytes 786464 | tf_op jit(solution)/shard_map/all_to_all | solution.py:255
  46.9 10.4 %all-to-all-start.1 = ((bf16[256,2,32,128]{3,2,1,0:T(8,128)(2,1)}), bf16[256,2,32,128]{3,2,1,0:T(8,128)(2,1)}, u32[]{:S(2)}, u32[]{:S(2)}) async-start(bf16[256,2,32,128]{3,2,1,0:T(8,128)(2,1)} %shard_map.173), calls=%async_computation.1 | async-start | bytes 8388608 | tf_op jit(solution)/shard_map/all_to_all | solution.py:259
  57.3 2.2 compare_select_fusion
  59.6 2.4 collective-permute-start
  62.0 0.8 collective-permute-done
  63.2 91.5 %all-to-all-done.1.parts_ref = bf16[256,2,32,128]{3,2,1,0:T(8,128)(2,1)} async-done(((bf16[256,2,32,128]{3,2,1,0:T(8,128)(2,1)}), bf16[256,2,32,128]{3,2,1,0:T(8,128)(2,1)}, u32[]{:S(2)}, u32[]{:S(2)}) %all-to-all-start.1) | async-done | bytes 4194336 | tf_op jit(solution)/shard_map/all_to_all | solution.py:259
  154.7 8.3 %shard_map.174 = (bf16[4096,128]{1,0:T(8,128)(2,1)S(1)}, bf16[1024,128]{1,0:T(8,128)(2,1)S(1)}) custom-call(s32[512]{0:T(512)S(1)} %reshape.68.line_ref, bf16[256,2,32,128]{3,2,1,0:T(8,128)(2,1)} %all-to-all-done.1.parts_ref, bf16[96,128]{1,0:T(8,128)(2,1)S(1)} %copy-done.11, bf16[32,256]{1,0:T(8,128)(2,1)S(1)} %copy-done.9), custom_call_target="tpu_custom_call" | custom-call | tf_op jit(solution)/shard_map/pallas_call | solution.py:270
  163.0 1.1 collective-permute-start.1
  164.0 21.0 %all_to_all.25 = bf16[256,4,128]{2,1,0:T(4,128)(2,1)S(1)} all-to-all(bf16[256,4,128]{2,1,0:T(4,128)(2,1)S(1)} %bitcast.35), channel_id=1, replica_groups=mesh['slab'=128,'chan'=2] {'slab','chan'}, dimensions={0} | all-to-all | bytes 524288 | tf_op jit(solution)/shard_map/all_to_all | solution.py:278
  185.0 1.2 copy-done.5
  186.2 1.2 copy-done.6
  187.5 8.5 %shard_map.175 = bf16[1024,128]{1,0:T(8,128)(2,1)} custom-call(bf16[1024,128]{1,0:T(8,128)(2,1)S(1)} %bitcast.32, bf16[2,64,128,64]{3,2,1,0:T(8,128)(2,1)} %bitcast.37, bf16[512,1024]{1,0:T(8,128)(2,1)S(1)} %copy-done.5, bf16[1024,512]{1,0:T(8,128)(2,1)S(1)} %copy-done.6), custom_call_target="tpu_custom_call" | custom-call | tf_op jit(solution)/shard_map/pallas_call | solution.py:284
  196.0 5.2 %all-to-all-start.3 = ((bf16[256,4,128]{2,1,0:T(4,128)(2,1)}), bf16[256,4,128]{2,1,0:T(4,128)(2,1)S(1)}, u32[]{:S(2)}, u32[]{:S(2)}) async-start(bf16[256,4,128]{2,1,0:T(4,128)(2,1)} %bitcast.11), calls=%async_computation.3 | async-start | bytes 524288 | tf_op jit(solution)/shard_map/all_to_all | solution.py:290
  201.6 15.0 %all-to-all-done.3 = bf16[256,4,128]{2,1,0:T(4,128)(2,1)S(1)} async-done(((bf16[256,4,128]{2,1,0:T(4,128)(2,1)}), bf16[256,4,128]{2,1,0:T(4,128)(2,1)S(1)}, u32[]{:S(2)}, u32[]{:S(2)}) %all-to-all-start.3) | async-done | bytes 262176 | tf_op jit(solution)/shard_map/all_to_all | solution.py:290
  216.7 1.0 copy-done.3
  217.7 1.2 copy-done.4
  219.0 7.7 %shard_map.176.own_ref = bf16[4096,128]{1,0:T(8,128)(2,1)S(1)} custom-call(bf16[1024,128]{1,0:T(8,128)(2,1)S(1)} %bitcast.31, bf16[4096,128]{1,0:T(8,128)(2,1)S(1)} %get-tuple-element.8.own_ref, bf16[4096,128]{1,0:T(8,128)(2,1)S(1)} %copy-done.4, bf16[32,64]{1,0:T(8,128)(2,1)S(1)} %maximum_bitcast_fusion.1.skip_ref, ...), custom_call_target="tpu_custom_call" | custom-call | tf_op jit(solution)/shard_map/pallas_call | solution.py:305
  227.3 2.1 collective-permute-done.2.other_ref
  229.5 7.4 %shard_map.177 = f32[256,128]{1,0:T(8,128)S(1)} custom-call(s32[256]{0:T(256)S(1)} %select_n.63.line_ref, bf16[128,24,128]{2,1,0:T(8,128)(2,1)S(1)} %all-to-all-done.meta_ref, bf16[4096,128]{1,0:T(8,128)(2,1)S(1)} %shard_map.176.own_ref, bf16[4096,128]{1,0:T(8,128)(2,1)S(1)} %collective-permute-done.2.other_ref, ...), custom_call_target="tpu_custom_call" | custom-call | tf_op jit(solution)/shard_map/pallas_call | solution.py:321
  236.8 22.0 %all_to_all.26 = f32[128,2,128]{2,1,0:T(2,128)S(1)} all-to-all(f32[128,2,128]{2,1,0:T(2,128)S(1)} %bitcast.33), channel_id=1, replica_groups=mesh['slab'=128,'chan'=2] {'slab'}, dimensions={0} | all-to-all | bytes 262144 | tf_op jit(solution)/shard_map/all_to_all | solution.py:327
  258.9 1.5 shard_map.178
  (47 shorter events, 3.2 us)
Async XLA Ops:
  2.9 1.0 copy-start.1
  3.9 0.8 copy-start.7
  4.7 0.7 copy-start.12
  8.9 38.0 %all-to-all-start = ((bf16[128,24,128]{2,1,0:T(8,128)(2,1)}), bf16[128,24,128]{2,1,0:T(8,128)(2,1)S(1)}, u32[]{:S(2)}, u32[]{:S(2)}) async-start(bf16[128,24,128]{2,1,0:T(8,128)(2,1)} %shard_map.172), calls=%async_computation | async-start | bytes 1572864 | tf_op jit(solution)/shard_map/all_to_all | solution.py:255
  26.1 1.6 copy-start
  27.7 0.9 copy-start.2
  28.6 0.8 copy-start.8
  36.5 118.2 %copy-start.9 = (bf16[32,256]{1,0:T(8,128)(2,1)S(1)}, bf16[32,256]{1,0:T(8,128)(2,1)}, u32[]{:S(2)}) copy-start(bf16[32,256]{1,0:T(8,128)(2,1)} %constant.54.clone.dz_ref.ez_ref) | copy-start | bytes 49156
  36.5 118.2 %copy-start.11 = (bf16[96,128]{1,0:T(8,128)(2,1)S(1)}, bf16[96,128]{1,0:T(8,128)(2,1)}, u32[]{:S(2)}) copy-start(bf16[96,128]{1,0:T(8,128)(2,1)} %constant.53.clone.dy_ref) | copy-start | bytes 73732
  46.9 107.7 %all-to-all-start.1 = ((bf16[256,2,32,128]{3,2,1,0:T(8,128)(2,1)}), bf16[256,2,32,128]{3,2,1,0:T(8,128)(2,1)}, u32[]{:S(2)}, u32[]{:S(2)}) async-start(bf16[256,2,32,128]{3,2,1,0:T(8,128)(2,1)} %shard_map.173), calls=%async_computation.1 | async-start | bytes 8388608 | tf_op jit(solution)/shard_map/all_to_all | solution.py:259
  59.6 3.2 %collective-permute-start = (s32[128,2]{0,1:T(2,128)S(1)}, s32[128,2]{0,1:T(2,128)S(1)}, u32[]{:S(2)}, u32[]{:S(2)}) collective-permute-start(s32[128,2]{0,1:T(2,128)S(1)} %bitcast.38), channel_id=1, source_target_pairs={{0,1},{1,0},{2,3},{3,2},{4,5},{5,4},{6,7},{7,6},{8,9},{9,8},{10,11... | collective-permute-start | bytes 3080 | tf_op jit(solution)/shard_map/ppermute | solution.py:263
  162.9 38.3 %copy-start.13 = (bf16[64,64]{1,0:T(8,128)(2,1)S(1)}, bf16[64,64]{1,0:T(8,128)(2,1)}, u32[]{:S(2)}) copy-start(bf16[64,64]{1,0:T(8,128)(2,1)} %param.26) | copy-start | bytes 24580
  163.0 38.5 %copy-start.16 = (f32[64]{0:T(128)S(1)}, f32[64]{0:T(128)}, u32[]{:S(2)}) copy-start(f32[64]{0:T(128)} %param.27) | copy-start | bytes 772
  163.0 54.8 %copy-start.10 = (bf16[128,64]{1,0:T(8,128)(2,1)S(1)}, bf16[128,64]{1,0:T(8,128)(2,1)}, u32[]{:S(2)}) copy-start(bf16[128,64]{1,0:T(8,128)(2,1)} %constant.57.clone.ey_ref) | copy-start | bytes 49156
  163.0 53.7 %collective-permute-start.1 = (bf16[4096,128]{1,0:T(8,128)(2,1)S(1)}, bf16[4096,128]{1,0:T(8,128)(2,1)S(1)}, u32[]{:S(2)}, u32[]{:S(2)}) collective-permute-start(bf16[4096,128]{1,0:T(8,128)(2,1)S(1)} %get-tuple-element.8.own_ref), channel_id=1, source_target_pairs={{0,1},{1,0},{2,3},{3,2},{4,5},{5,4},{6,7},{7,6},{8,9},{9,8},{10,11... | collective-permute-start | bytes 3145736 | tf_op jit(solution)/shard_map/ppermute | solution.py:277
  185.0 1.2 copy-start.5
  186.2 1.2 copy-start.6
  187.5 39.3 %copy-start.14 = (bf16[64,128]{1,0:T(8,128)(2,1)S(1)}, bf16[64,128]{1,0:T(8,128)(2,1)}, u32[]{:S(2)}) copy-start(bf16[64,128]{1,0:T(8,128)(2,1)} %param.28) | copy-start | bytes 49156
  187.5 42.0 %copy-start.15 = (bf16[128]{0:T(256)(128)(2,1)S(1)}, bf16[128]{0:T(256)(128)(2,1)}, u32[]{:S(2)}) copy-start(bf16[128]{0:T(256)(128)(2,1)} %param.29) | copy-start | bytes 772
  196.0 20.7 %all-to-all-start.3 = ((bf16[256,4,128]{2,1,0:T(4,128)(2,1)}), bf16[256,4,128]{2,1,0:T(4,128)(2,1)S(1)}, u32[]{:S(2)}, u32[]{:S(2)}) async-start(bf16[256,4,128]{2,1,0:T(4,128)(2,1)} %bitcast.11), calls=%async_computation.3 | async-start | bytes 524288 | tf_op jit(solution)/shard_map/all_to_all | solution.py:290
  216.7 1.0 copy-start.3
  217.7 1.2 copy-start.4
  226.7 2.7 %collective-permute-start.2 = (bf16[4096,128]{1,0:T(8,128)(2,1)S(1)}, bf16[4096,128]{1,0:T(8,128)(2,1)S(1)}, u32[]{:S(2)}, u32[]{:S(2)}) collective-permute-start(bf16[4096,128]{1,0:T(8,128)(2,1)S(1)} %shard_map.176.own_ref), channel_id=1, source_target_pairs={{0,1},{1,0},{2,3},{3,2},{4,5},{5,4},{6,7},{7,6},{8,9},{9,8},{10,11... | collective-permute-start | bytes 3145736 | tf_op jit(solution)/shard_map/ppermute | solution.py:311

commit v3 on v2

--- a/solution.py
+++ b/solution.py
@@ -20,6 +20,7 @@
 VM = pl.BlockSpec(memory_space=pltpu.VMEM)
 SM = pl.BlockSpec(memory_space=pltpu.SMEM)
 WIDE = 16
+ROWS = 152
 
 
 def trig():
@@ -60,64 +61,95 @@
     return jnp.concatenate(rows, axis=0).astype(BF)
 
 
-def pack_kernel(blk_ref, line_ref, start_ref, weight_ref, out_ref):
+def dispatch_kernel(
+    blk_ref, line_ref, points_ref, start_ref, weight_ref, lift_ref, out_ref, stage, send_sem, recv_sem, own_sem
+):
+    me, chan = lax.axis_index("slab"), lax.axis_index("chan")
+    x, z, y = me // 32, (me // 4) % 8, me % 4
+    barrier = pltpu.get_barrier_semaphore()
+
+    def greet(i, carry):
+        pl.semaphore_signal(
+            barrier, inc=1, device_id=((me + i) % G, chan), device_id_type=pl.DeviceIdType.MESH
+        )
+        return carry
+
+    lax.fori_loop(1, G, greet, 0)
+    pl.semaphore_wait(barrier, G - 1)
     row = lax.broadcasted_iota(jnp.int32, (8, PB), 0)
 
-    def step(s, carry):
-        b0, b1 = blk_ref[2 * s], blk_ref[2 * s + 1]
-        c0, c1 = jnp.maximum(b0, 0), jnp.maximum(b1, 0)
-        l0 = jnp.where(b0 >= 0, line_ref[c0] + 1, 0)
-        l1 = jnp.where(b1 >= 0, line_ref[c1] + 1, 0)
-        info = jnp.where(
-            row == 0,
-            start_ref[pl.ds(c0, 1), :],
-            jnp.where(
-                row == 1,
-                start_ref[pl.ds(c1, 1), :],
-                jnp.where(row == 2, l0, jnp.where(row == 3, l1, 0)),
-            ),
-        )
-        out_ref[s, 0:8, :] = weight_ref[c0]
-        out_ref[s, 8:16, :] = weight_ref[c1]
-        out_ref[s, 16:24, :] = info.astype(F32).astype(BF)
-        return carry
-
-    lax.fori_loop(0, G, step, 0)
-
-
-def encode_kernel(slot_ref, count_ref, points_ref, start_ref, weight_ref, lift_ref, out_ref):
-    count = count_ref[0]
-
-    def step(group, carry):
-        blocks = [jnp.minimum(group * WIDE + u, count - 1) for u in range(WIDE)]
-        nears = [
-            near_transposed(start_ref[pl.ds(b, 1), :], weight_ref[b].astype(F32)) for b in blocks
-        ]
+    def group(g, carry):
+        line_x = (x + g // 4) % 4 * 32 + (y + g % 4) % 4
+        targets, blocks, nears = [], [], []
+        for j in range(8):
+            hop = (j + 1) // 2
+            target = line_x + (z + (4 + hop if j % 2 else 4 - hop)) % 8 * 4
+            found = [blk_ref[2 * target + r] for r in range(2)]
+            taken = [jnp.maximum(b, 0) for b in found]
+            lines = [jnp.where(b >= 0, line_ref[c] + 1, 0) for b, c in zip(found, taken)]
+            starts = [start_ref[pl.ds(c, 1), :] for c in taken]
+            info = jnp.where(row == 2, lines[0], jnp.where(row == 3, lines[1], 0))
+            info = jnp.where(row == 0, starts[0], jnp.where(row == 1, starts[1], info))
+            weights = [weight_ref[c] for c in taken]
+            stage[g * 8 + j, 128:136, :] = weights[0]
+            stage[g * 8 + j, 136:144, :] = weights[1]
+            stage[g * 8 + j, 144:152, :] = info.astype(F32).astype(BF)
+            targets.append(target)
+            blocks.extend(taken)
+            nears.extend(near_transposed(s, w.astype(F32)) for s, w in zip(starts, weights))
         points = jnp.concatenate([points_ref[b] for b in blocks], axis=1)
         lifted = dot(lift_ref[...], points).astype(BF)
-        for u in range(WIDE):
-            slot = slot_ref[blocks[u]]
-            slab, rank = slot >> 1, slot & 1
-            part = dot(lifted[:, u * PB : (u + 1) * PB], nears[u], ((1,), (1,))).astype(BF)
-            out_ref[2 * slab, rank] = part[:HALF]
-            out_ref[2 * slab + 1, rank] = part[HALF:]
-        return carry
-
-    lax.fori_loop(0, (count + WIDE - 1) // WIDE, step, 0)
-
-
-def forward_kernel(line_ref, parts_ref, dy_ref, dz_ref, latent_ref, spec_ref, acc, ybuf):
+        for j in range(8):
+            for r in range(2):
+                u = 2 * j + r
+                part = dot(lifted[:, u * PB : (u + 1) * PB], nears[u], ((1,), (1,)))
+                stage[g * 8 + j, r * C : (r + 1) * C, :] = part.astype(BF)
+        for j in range(8):
+            copy = pltpu.make_async_remote_copy(
+                src_ref=stage.at[g * 8 + j],
+                dst_ref=out_ref.at[me],
+                send_sem=send_sem,
+                recv_sem=recv_sem,
+                device_id=(targets[j], chan),
+                device_id_type=pl.DeviceIdType.MESH,
+            )
+            if j < 7:
+                copy.start()
+            else:
+                pl.when(g > 0)(copy.start)
+        return carry
+
+    lax.fori_loop(0, 16, group, 0)
+    own = pltpu.make_async_copy(stage.at[7], out_ref.at[me], own_sem)
+    own.start()
+    own.wait()
+    sent = stage.at[pl.ds(0, G - 1)]
+    pltpu.make_async_copy(sent, sent, send_sem).wait()
+    got = out_ref.at[pl.ds(0, G - 1)]
+    pltpu.make_async_copy(got, got, recv_sem).wait()
+
+
+def gather_kernel(chan_ref, line_ref, parts_ref, own_ref, other_ref, acc):
     acc[...] = jnp.zeros_like(acc)
 
     def add(src, carry):
         for r in range(2):
             line = line_ref[2 * src + r]
             rows = pl.ds(pl.multiple_of(line * HALF, HALF), HALF)
-            acc[rows, :] += parts_ref[src, r].astype(F32)
-        return carry
-
-    lax.fori_loop(0, 256, add, 0)
-    latent_ref[...] = acc[0 : G * HALF, :].astype(BF)
+            for h in range(2):
+                first = r * C + h * HALF
+                acc[h, rows, :] += parts_ref[src, first : first + HALF, :].astype(F32)
+        return carry
+
+    lax.fori_loop(0, G, add, 0)
+    chan = chan_ref[0]
+    own_ref[...] = acc[chan, 0 : G * HALF, :]
+    other_ref[...] = acc[1 - chan, 0 : G * HALF, :].astype(BF)
+
+
+def forward_kernel(own_ref, other_ref, dy_ref, dz_ref, latent_ref, spec_ref, acc, ybuf):
+    acc[...] = own_ref[...] + other_ref[...].astype(F32)
+    latent_ref[...] = acc[...].astype(BF)
     for c in range(HALF):
         plane = acc[pl.ds(c, G, stride=HALF), :].astype(BF)
         ybuf[pl.ds(c, 3 * M, stride=HALF), :] = dot(dy_ref[...], plane)
@@ -249,31 +281,37 @@
     slot_ids = jnp.arange(256, dtype=jnp.int32)
     block = jnp.max(jnp.where(slot[None, :] == slot_ids[:, None], ids[None, :], -1), axis=1)
 
-    meta = call(pack_kernel, jax.ShapeDtypeStruct((128, 24, PB), BF), [SM, SM, VM, VM])(
-        block, dest_block, near_start, near_weight
-    )
-    meta = lax.all_to_all(meta, "slab", split_axis=0, concat_axis=0, tiled=True)
-    parts = call(encode_kernel, jax.ShapeDtypeStruct((256, 2, HALF, G), BF), [SM, SM] + [VM] * 4)(
-        slot, live_count, points, near_start, near_weight, lift_w.T
-    )
-    parts = lax.all_to_all(parts, every, split_axis=0, concat_axis=0, tiled=True)
-
+    parts = pl.pallas_call(
+        dispatch_kernel,
+        out_shape=jax.ShapeDtypeStruct((G, ROWS, PB), BF),
+        in_specs=[SM, SM] + [VM] * 4,
+        out_specs=pl.BlockSpec(memory_space=pl.ANY),
+        scratch_shapes=[pltpu.VMEM((G, ROWS, PB), BF)] + [pltpu.SemaphoreType.DMA] * 3,
+        compiler_params=pltpu.CompilerParams(
+            vmem_limit_bytes=LIMIT, collective_id=0, has_side_effects=True
+        ),
+    )(block, dest_block, points, near_start, near_weight, lift_w.T)
+    meta = parts[:, 128:152, :]
     lines = meta[:, 18:20, 0].astype(jnp.int32)
-    lines = jnp.where(lines > 0, lines - 1, G)
-    lines_other = lax.ppermute(lines, "chan", [(0, 1), (1, 0)])
-    first = jnp.where(chan == 0, lines, lines_other)
-    second = jnp.where(chan == 0, lines_other, lines)
-    all_lines = jnp.stack([first, second], axis=1).reshape(512)
+    lines = jnp.where(lines > 0, lines - 1, G).reshape(256)
+    mine, theirs = call(
+        gather_kernel,
+        (jax.ShapeDtypeStruct((G * HALF, G), F32), jax.ShapeDtypeStruct((G * HALF, G), BF)),
+        [SM, SM, VM],
+        [pltpu.VMEM((2, (G + 1) * HALF, G), F32)],
+        (VM, VM),
+    )(chan.reshape(1), lines, parts)
+    received = lax.ppermute(theirs, "chan", [(0, 1), (1, 0)])
 
     dy = jnp.asarray(np.concatenate([cos.T, -sin.T, -cos.T], axis=0), BF)
     dz = jnp.asarray(np.concatenate([cos.T, sin.T], axis=1), BF)
     latent, spectra = call(
         forward_kernel,
         (jax.ShapeDtypeStruct((G * HALF, G), BF), jax.ShapeDtypeStruct((M * M, 128), BF)),
-        [SM] + [VM] * 3,
-        [pltpu.VMEM(((G + 1) * HALF, G), F32), pltpu.VMEM((3 * M * HALF, G), F32)],
+        [VM] * 4,
+        [pltpu.VMEM((G * HALF, G), F32), pltpu.VMEM((3 * M * HALF, G), F32)],
         (VM, VM),
-    )(all_lines, parts, dy, dz)
+    )(mine, received, dy, dz)
     latent_other = lax.ppermute(latent, "chan", [(0, 1), (1, 0)])
     spectra = lax.all_to_all(spectra.reshape(256, 4, 128), every, split_axis=0, concat_axis=0, tiled=True)
 
@@ -323,7 +361,7 @@
         jax.ShapeDtypeStruct((256, PB), F32),
         [SM] + [VM] * 5,
         [pltpu.SMEM((257,), jnp.int32)],
-    )(lines.reshape(256), meta, grid, grid_other, proj, proj_row)
+    )(lines, meta, grid, grid_other, proj, proj_row)
     values = lax.all_to_all(values.reshape(128, 2, PB), "slab", split_axis=0, concat_axis=0, tiled=True)
     return call(unpack_kernel, jax.ShapeDtypeStruct((128, PB), F32), [SM, VM])(slot, values.reshape(256, PB))
 

time: 261 us -> 246 us (0.943)
  Pallas kernels: 44 us -> 156 us
  waiting for transfers between devices: 120 us -> 18.1 us
  starting transfers between devices: 35.4 us -> 7.83 us
  blocking collectives: 43 us -> 49.8 us
  local copies, waits for them, and re-layouts: 12.6 us -> 6.94 us
    pallas_call x2, Pallas kernels: 10.6 us -> 128 us  [the longest x1 124 us: shards(): pl.pallas_call(dispatch_kernel, out_shape=jax.ShapeDtypeStruct((G, ROWS,...]
    all_to_all x2 -> x0, waiting for transfers between devices: 102 us -> none  [the longest x1 91.5 us: shards(): lax.all_to_all(parts, every, split_axis=0, concat_axis=0, tiled=True)]
    all_to_all x2 -> x0, starting transfers between devices: 26.7 us -> none  [the longest x1 16.3 us: shards(): meta = lax.all_to_all(meta, 'slab', split_axis=0, concat_axis=0, tiled=True)]
    unnamed x39 -> x31, local copies, waits for them, and re-layouts: 11.8 us -> 5.3 us
    all_to_all x1, blocking collectives: 21 us -> 26.4 us  [shards(): lax.all_to_all(spectra.reshape(256, 4, 128), every, split_axis=0, concat_...]
    pallas_call x1, Pallas kernels: 8.27 us -> 3.51 us  [shards(): call(forward_kernel, (jax.ShapeDtypeStruct((G * HALF, G), BF), jax.ShapeD...]
  transfers between devices with their start and end apart: 6 -> 4, of which waited for: 5 -> 3; matrix products, arithmetic and copies ran while one was open for 2% -> 1% of each run, Pallas kernels for 6% -> 3%
where the time goes in v3:
time: 246 us; the launch traced here: 245 us
  Pallas kernels  156 us (63%)
  blocking collectives  49.8 us (20%)
  waiting for transfers between devices  18.1 us (7%)
  starting transfers between devices  7.83 us (3%)
  local copies, waits for them, and re-layouts  6.94 us (3%)
  other arithmetic  5.64 us (2%)
    pallas_call x1, Pallas kernels, shards(): pl.pallas_call(dispatch_kernel, out_shape=jax.ShapeDtypeStruct((G, ROWS,...  124 us
    all_to_all x1, blocking collectives, shards(): lax.all_to_all(spectra.reshape(256, 4, 128), every, split_axis=0, concat_...  26.4 us
    all_to_all x1, blocking collectives, shards(): lax.all_to_all(values.reshape(128, 2, PB), 'slab', split_axis=0, concat_a...  23.4 us
    all_to_all x1, waiting for transfers between devices, shards(): lax.all_to_all(back.reshape(256, 4, 128), every, split_axis=0, concat_axi...  14.8 us
    pallas_call x1, Pallas kernels, shards(): call(mix_kernel, jax.ShapeDtypeStruct((1024, 128), BF), [VM] * 4, [pltpu....  8.51 us
    pallas_call x1, Pallas kernels, shards(): call(inverse_kernel, jax.ShapeDtypeStruct((G * HALF, G), BF), [VM] * 7, [...  7.79 us
    pallas_call x1, Pallas kernels, shards(): call(decode_kernel, jax.ShapeDtypeStruct((256, PB), F32), [SM] + [VM] * 5...  6.66 us
    all_to_all x1, starting transfers between devices, shards(): lax.all_to_all(back.reshape(256, 4, 128), every, split_axis=0, concat_axi...  5.43 us
  transfers between devices with their start and end apart: 4, of which 3 were waited for; matrix products, arithmetic and copies ran while one was open for 1% of the time, Pallas kernels for 3%

profile of v3, /device:TPU:1, one launch (start us, length us, event | category | flops | bytes accessed | tf_op | source)
XLA Modules:
  0.0 245.4 jit_solution(14912236374826628980)
XLA Ops:
  0.7 0.7 compare_select_fusion.3
  1.3 0.7 fusion.2
  2.0 0.2 convert_reduce_fusion
  2.1 0.7 compare_select_fusion.2.slot_ref
  2.8 0.1 select_reduce_fusion.blk_ref
  2.9 0.8 copy.29
  3.8 1.6 copy-done
  5.3 0.9 copy-done.3
  6.3 0.8 copy-done.4
  7.1 0.7 copy-done.8
  7.8 123.6 %shard_map.172.parts_ref = bf16[128,152,128]{2,1,0:T(8,128)(2,1)} custom-call(s32[256]{0:T(256)S(1)} %select_reduce_fusion.blk_ref, s32[128]{0:T(128)S(1)} %copy-done.8, bf16[128,64,128]{2,1,0:T(8,128)(2,1)S(1)} %copy-done, s32[128,128]{1,0:T(8,128)S(1)} %copy-done.4, bf16[128,8,128]{2,1,0:T(8,128)(2,1)S(1)} %copy-done.3, bf16[64,64]{1,0:T(8,128)(2,1)S(1)} %bitcast.30), custom_call_target="tpu_custom_call" | custom-call | tf_op jit(solution)/shard_map/pallas_call | solution.py:284
  131.5 3.2 %fusion = s32[128,2]{1,0:T(8,128)S(1)} fusion(bf16[128,152,128]{2,1,0:T(8,128)(2,1)} %shard_map.172.parts_ref), kind=kLoop, calls=%fused_computation.2 | loop fusion | flops 1024 | bytes 1536 | tf_op jit(solution)/shard_map/jit(_where)/select_n | solution.py:296
  134.7 0.1 select_n.48.line_ref
  134.8 4.7 %shard_map.173 = (f32[4096,128]{1,0:T(8,128)S(1)}, bf16[4096,128]{1,0:T(8,128)(2,1)S(1)}) custom-call(s32[1]{0:T(128)} %bitcast.4.chan_ref, s32[256]{0:T(256)S(1)} %select_n.48.line_ref, bf16[128,152,128]{2,1,0:T(8,128)(2,1)} %shard_map.172.parts_ref), custom_call_target="tpu_custom_call" | custom-call | tf_op jit(solution)/shard_map/pallas_call | solution.py:297
  139.6 1.8 collective-permute-start
  141.4 2.3 collective-permute-done.other_ref
  143.7 3.5 %shard_map.174 = (bf16[4096,128]{1,0:T(8,128)(2,1)S(1)}, bf16[1024,128]{1,0:T(8,128)(2,1)S(1)}) custom-call(f32[4096,128]{1,0:T(8,128)S(1)} %get-tuple-element.9.own_ref, bf16[4096,128]{1,0:T(8,128)(2,1)S(1)} %collective-permute-done.other_ref, bf16[96,128]{1,0:T(8,128)(2,1)S(1)} %copy-done.7, bf16[32,256]{1,0:T(8,128)(2,1)S(1)} %copy-done.5), custom_call_target="tpu_custom_call" | custom-call | tf_op jit(solution)/shard_map/pallas_call | solution.py:308
  147.2 0.5 collective-permute-start.1
  147.7 26.4 %all_to_all.15 = bf16[256,4,128]{2,1,0:T(4,128)(2,1)S(1)} all-to-all(bf16[256,4,128]{2,1,0:T(4,128)(2,1)S(1)} %bitcast.29), channel_id=1, replica_groups=mesh['slab'=128,'chan'=2] {'slab','chan'}, dimensions={0} | all-to-all | bytes 524288 | tf_op jit(solution)/shard_map/all_to_all | solution.py:316
  174.1 8.5 %shard_map.175 = bf16[1024,128]{1,0:T(8,128)(2,1)} custom-call(bf16[1024,128]{1,0:T(8,128)(2,1)S(1)} %bitcast.26, bf16[2,64,128,64]{3,2,1,0:T(8,128)(2,1)} %bitcast.31, bf16[512,1024]{1,0:T(8,128)(2,1)S(1)} %copy-done.1, bf16[1024,512]{1,0:T(8,128)(2,1)S(1)} %copy-done.2), custom_call_target="tpu_custom_call" | custom-call | tf_op jit(solution)/shard_map/pallas_call | solution.py:322
  182.6 5.4 %all-to-all-start.1 = ((bf16[256,4,128]{2,1,0:T(4,128)(2,1)}), bf16[256,4,128]{2,1,0:T(4,128)(2,1)S(1)}, u32[]{:S(2)}, u32[]{:S(2)}) async-start(bf16[256,4,128]{2,1,0:T(4,128)(2,1)} %bitcast.9), calls=%async_computation.1 | async-start | bytes 524288 | tf_op jit(solution)/shard_map/all_to_all | solution.py:328
  188.0 0.1 fusion.3
  188.5 14.8 %all-to-all-done.1 = bf16[256,4,128]{2,1,0:T(4,128)(2,1)S(1)} async-done(((bf16[256,4,128]{2,1,0:T(4,128)(2,1)}), bf16[256,4,128]{2,1,0:T(4,128)(2,1)S(1)}, u32[]{:S(2)}, u32[]{:S(2)}) %all-to-all-start.1) | async-done | bytes 262176 | tf_op jit(solution)/shard_map/all_to_all | solution.py:328
  203.3 7.8 %shard_map.176.own_ref = bf16[4096,128]{1,0:T(8,128)(2,1)S(1)} custom-call(bf16[1024,128]{1,0:T(8,128)(2,1)S(1)} %bitcast.25, bf16[4096,128]{1,0:T(8,128)(2,1)S(1)} %get-tuple-element.12.own_ref, bf16[4096,128]{1,0:T(8,128)(2,1)S(1)} %collective-permute-done.1.other_ref, bf16[32,64]{1,0:T(8,128)(2,1)S(1)} %maximum_bitcast_fusion.1.skip_ref, ...), custom_call_target="tpu_custom_call" | custom-call | tf_op jit(solution)/shard_map/pallas_call | solution.py:343
  211.1 0.1 collective-permute-start.2
  211.2 1.2 slice.8.meta_ref
  212.5 0.1 copy.37
  212.6 0.1 copy.36
  212.8 1.0 collective-permute-done.2.other_ref
  213.9 6.7 %shard_map.177 = f32[256,128]{1,0:T(8,128)S(1)} custom-call(s32[256]{0:T(256)S(1)} %select_n.48.line_ref, bf16[128,24,128]{2,1,0:T(8,128)(2,1)S(1)} %slice.8.meta_ref, bf16[4096,128]{1,0:T(8,128)(2,1)S(1)} %shard_map.176.own_ref, bf16[4096,128]{1,0:T(8,128)(2,1)S(1)} %collective-permute-done.2.other_ref, ...), custom_call_target="tpu_custom_call" | custom-call | tf_op jit(solution)/shard_map/pallas_call | solution.py:359
  220.5 23.4 %all_to_all.16 = f32[128,2,128]{2,1,0:T(2,128)S(1)} all-to-all(f32[128,2,128]{2,1,0:T(2,128)S(1)} %bitcast.27), channel_id=1, replica_groups=mesh['slab'=128,'chan'=2] {'slab'}, dimensions={0} | all-to-all | bytes 262144 | tf_op jit(solution)/shard_map/all_to_all | solution.py:365
  243.9 1.5 shard_map.178
  (31 shorter events, 0.6 us)
Async XLA Ops:
  3.7 1.6 copy-start
  5.3 0.9 copy-start.3
  6.3 0.8 copy-start.4
  7.1 0.7 copy-start.8
  131.4 12.2 %copy-start.5 = (bf16[32,256]{1,0:T(8,128)(2,1)S(1)}, bf16[32,256]{1,0:T(8,128)(2,1)}, u32[]{:S(2)}) copy-start(bf16[32,256]{1,0:T(8,128)(2,1)} %constant.54.clone.dz_ref.ez_ref) | copy-start | bytes 49156
  131.5 12.2 %copy-start.7 = (bf16[96,128]{1,0:T(8,128)(2,1)S(1)}, bf16[96,128]{1,0:T(8,128)(2,1)}, u32[]{:S(2)}) copy-start(bf16[96,128]{1,0:T(8,128)(2,1)} %constant.53.clone.dy_ref) | copy-start | bytes 73732
  134.8 39.3 %copy-start.1 = (bf16[512,1024]{1,0:T(8,128)(2,1)S(1)}, bf16[512,1024]{1,0:T(8,128)(2,1)}, u32[]{:S(2)}) copy-start(bf16[512,1024]{1,0:T(8,128)(2,1)} %constant.55.clone.fwd_ref) | copy-start | bytes 3145732
  134.8 39.2 %copy-start.2 = (bf16[1024,512]{1,0:T(8,128)(2,1)S(1)}, bf16[1024,512]{1,0:T(8,128)(2,1)}, u32[]{:S(2)}) copy-start(bf16[1024,512]{1,0:T(8,128)(2,1)} %constant.56.clone.bwd_ref) | copy-start | bytes 3145732
  139.6 4.1 %collective-permute-start = (bf16[4096,128]{1,0:T(8,128)(2,1)S(1)}, bf16[4096,128]{1,0:T(8,128)(2,1)S(1)}, u32[]{:S(2)}, u32[]{:S(2)}) collective-permute-start(bf16[4096,128]{1,0:T(8,128)(2,1)S(1)} %get-tuple-element.10), channel_id=1, source_target_pairs={{0,1},{1,0},{2,3},{3,2},{4,5},{5,4},{6,7},{7,6},{8,9},{9,8},{10,11... | collective-permute-start | bytes 3145736 | tf_op jit(solution)/shard_map/ppermute | solution.py:304
  147.2 40.8 %copy-start.9 = (bf16[64,64]{1,0:T(8,128)(2,1)S(1)}, bf16[64,64]{1,0:T(8,128)(2,1)}, u32[]{:S(2)}) copy-start(bf16[64,64]{1,0:T(8,128)(2,1)} %param.26) | copy-start | bytes 24580
  147.2 41.1 %copy-start.12 = (f32[64]{0:T(128)S(1)}, f32[64]{0:T(128)}, u32[]{:S(2)}) copy-start(f32[64]{0:T(128)} %param.27) | copy-start | bytes 772
  147.2 56.1 %copy-start.6 = (bf16[128,64]{1,0:T(8,128)(2,1)S(1)}, bf16[128,64]{1,0:T(8,128)(2,1)}, u32[]{:S(2)}) copy-start(bf16[128,64]{1,0:T(8,128)(2,1)} %constant.57.clone.ey_ref) | copy-start | bytes 49156
  147.2 56.0 %collective-permute-start.1 = (bf16[4096,128]{1,0:T(8,128)(2,1)S(1)}, bf16[4096,128]{1,0:T(8,128)(2,1)S(1)}, u32[]{:S(2)}, u32[]{:S(2)}) collective-permute-start(bf16[4096,128]{1,0:T(8,128)(2,1)S(1)} %get-tuple-element.12.own_ref), channel_id=1, source_target_pairs={{0,1},{1,0},{2,3},{3,2},{4,5},{5,4},{6,7},{7,6},{8,9},{9,8},{10,11... | collective-permute-start | bytes 3145736 | tf_op jit(solution)/shard_map/ppermute | solution.py:315
  182.6 29.9 %copy-start.10 = (bf16[64,128]{1,0:T(8,128)(2,1)S(1)}, bf16[64,128]{1,0:T(8,128)(2,1)}, u32[]{:S(2)}) copy-start(bf16[64,128]{1,0:T(8,128)(2,1)} %param.28) | copy-start | bytes 49156
  182.6 31.3 %copy-start.11 = (bf16[128]{0:T(256)(128)(2,1)S(1)}, bf16[128]{0:T(256)(128)(2,1)}, u32[]{:S(2)}) copy-start(bf16[128]{0:T(256)(128)(2,1)} %param.29) | copy-start | bytes 772
  182.6 20.7 %all-to-all-start.1 = ((bf16[256,4,128]{2,1,0:T(4,128)(2,1)}), bf16[256,4,128]{2,1,0:T(4,128)(2,1)S(1)}, u32[]{:S(2)}, u32[]{:S(2)}) async-start(bf16[256,4,128]{2,1,0:T(4,128)(2,1)} %bitcast.9), calls=%async_computation.1 | async-start | bytes 524288 | tf_op jit(solution)/shard_map/all_to_all | solution.py:328
  211.1 2.7 %collective-permute-start.2 = (bf16[4096,128]{1,0:T(8,128)(2,1)S(1)}, bf16[4096,128]{1,0:T(8,128)(2,1)S(1)}, u32[]{:S(2)}, u32[]{:S(2)}) collective-permute-start(bf16[4096,128]{1,0:T(8,128)(2,1)S(1)} %shard_map.176.own_ref), channel_id=1, source_target_pairs={{0,1},{1,0},{2,3},{3,2},{4,5},{5,4},{6,7},{7,6},{8,9},{9,8},{10,11... | collective-permute-start | bytes 3145736 | tf_op jit(solution)/shard_map/ppermute | solution.py:349

commit v4 on v3

--- a/solution.py
+++ b/solution.py
@@ -66,16 +66,7 @@
 ):
     me, chan = lax.axis_index("slab"), lax.axis_index("chan")
     x, z, y = me // 32, (me // 4) % 8, me % 4
-    barrier = pltpu.get_barrier_semaphore()
-
-    def greet(i, carry):
-        pl.semaphore_signal(
-            barrier, inc=1, device_id=((me + i) % G, chan), device_id_type=pl.DeviceIdType.MESH
-        )
-        return carry
-
-    lax.fori_loop(1, G, greet, 0)
-    pl.semaphore_wait(barrier, G - 1)
+    pl.semaphore_wait(greet_all(me, chan), G - 1)
     row = lax.broadcasted_iota(jnp.int32, (8, PB), 0)
 
     def group(g, carry):
@@ -147,11 +138,73 @@
     other_ref[...] = acc[1 - chan, 0 : G * HALF, :].astype(BF)
 
 
-def forward_kernel(own_ref, other_ref, dy_ref, dz_ref, latent_ref, spec_ref, acc, ybuf):
-    acc[...] = own_ref[...] + other_ref[...].astype(F32)
-    latent_ref[...] = acc[...].astype(BF)
+def greet_all(me, chan):
+    barrier = pltpu.get_barrier_semaphore()
+
+    def greet(i, carry):
+        pl.semaphore_signal(
+            barrier, inc=1, device_id=((me + i) % G, chan), device_id_type=pl.DeviceIdType.MESH
+        )
+        return carry
+
+    lax.fori_loop(1, G, greet, 0)
+    return barrier
+
+
+def scatter(me, chan, src, dst, send_sem, recv_sem):
+    def send(i, carry):
+        target = (me + i) % G
+        pltpu.make_async_remote_copy(
+            src_ref=src.at[target],
+            dst_ref=dst.at[me],
+            send_sem=send_sem,
+            recv_sem=recv_sem,
+            device_id=(target, chan),
+            device_id_type=pl.DeviceIdType.MESH,
+        ).start()
+        return carry
+
+    lax.fori_loop(1, G, send, 0)
+    dst[me] = src[me]
+
+
+def settle(src, dst, send_sem, recv_sem):
+    sent, got = src.at[pl.ds(0, G - 1)], dst.at[pl.ds(0, G - 1)]
+    pltpu.make_async_copy(sent, sent, send_sem).wait()
+    pltpu.make_async_copy(got, got, recv_sem).wait()
+
+
+def middle_kernel(
+    mine_ref, theirs_ref, weight_ref, fwd_ref, bwd_ref, dy_ref, dz_ref, ez_ref, ey_ref, skip_ref, bias_ref,
+    grid_ref, grid_other_ref,
+    got, latent, latent_other, total, ybuf, spec, spec_other, send_b, recv_b, xbuf, rhs, send_c, recv_c, recv_d, ubuf,
+    send_sem, recv_sem,
+):
+    me, chan = lax.axis_index("slab"), lax.axis_index("chan")
+    barrier = greet_all(me, chan)
+    pl.semaphore_signal(barrier, inc=1, device_id=(me, 1 - chan), device_id_type=pl.DeviceIdType.MESH)
+    pl.semaphore_wait(barrier, G)
+
+    def swap(src, dst, index):
+        return pltpu.make_async_remote_copy(
+            src_ref=src,
+            dst_ref=dst,
+            send_sem=send_sem.at[index],
+            recv_sem=recv_sem.at[index],
+            device_id=(me, 1 - chan),
+            device_id_type=pl.DeviceIdType.MESH,
+        )
+
+    swap_latent = swap(theirs_ref, got, 0)
+    swap_latent.start()
+    swap_latent.wait()
+    total[...] = mine_ref[...] + got[...].astype(F32)
+    latent[...] = total[...].astype(BF)
+    swap_other = swap(latent, latent_other, 1)
+    swap_other.start()
+
     for c in range(HALF):
-        plane = acc[pl.ds(c, G, stride=HALF), :].astype(BF)
+        plane = total[pl.ds(c, G, stride=HALF), :].astype(BF)
         ybuf[pl.ds(c, 3 * M, stride=HALF), :] = dot(dy_ref[...], plane)
     for q in range(M):
         real = ybuf[q * HALF : (q + 1) * HALF, :].astype(BF)
@@ -160,15 +213,39 @@
         first = jnp.concatenate([real, imag, imag, minus], axis=0)
         second = jnp.concatenate([imag, minus, minus, -imag], axis=0)
         both = jnp.concatenate([first, second], axis=1)
-        spec_ref[q * M : (q + 1) * M, :] = dot(dz_ref[...], both, ((1,), (1,))).astype(BF)
-
-
-def mix_kernel(spec_ref, weight_ref, fwd_ref, bwd_ref, out_ref, xbuf, rhs):
-    prod = dot(fwd_ref[...], spec_ref[...])
+        modes = dot(dz_ref[...], both, ((1,), (1,))).astype(BF)
+        spec[0, q * M : (q + 1) * M, :] = modes[:M]
+        spec[1, q * M : (q + 1) * M, :] = modes[M:]
+
+    swap_spec = swap(spec.at[1 - chan], spec_other, 2)
+    swap_spec.start()
+    swap_spec.wait()
+    row = lax.broadcasted_iota(jnp.int32, (8, 128), 0)
+    from_own = (row // 4) == chan
+    for q in range(M):
+        own = spec[chan, q * M : (q + 1) * M, :].astype(F32)
+        other = spec_other[q * M : (q + 1) * M, :].astype(F32)
+        for j in range(4):
+            rows = slice(j * 8, (j + 1) * 8)
+            send_b[q * 4 + j] = jnp.where(from_own, own[rows], other[rows]).astype(BF)
+    scatter(me, chan, send_b, recv_b, send_sem.at[3], recv_sem.at[3])
+
+    swap_other.wait()
+
+    def mix_channels(group, carry):
+        for u in range(8):
+            rows = pl.ds(pl.multiple_of((group * 8 + u) * HALF, HALF), HALF)
+            both = jnp.concatenate([latent[rows, :], latent_other[rows, :]], axis=0)
+            total[rows, :] = dot(skip_ref[...], both) + bias_ref[...]
+        return carry
+
+    lax.fori_loop(0, G // 8, mix_channels, 0)
+    settle(send_b, recv_b, send_sem.at[3], recv_sem.at[3])
+
+    spectra = recv_b[...].astype(F32).reshape(1024, 128).astype(BF)
+    prod = dot(fwd_ref[...], spectra)
     for h in range(2):
-        cos = prod[h * 256 : h * 256 + 128, 0:64]
-        sin = prod[h * 256 + 128 : h * 256 + 256, 64:128]
-        xbuf[h] = cos + sin
+        xbuf[h] = prod[h * 256 : h * 256 + 128, 0:64] + prod[h * 256 + 128 : h * 256 + 256, 64:128]
 
     def chunk(t, carry):
         rows = pl.ds(pl.multiple_of(t * 32, 32), 32)
@@ -193,26 +270,33 @@
         return carry
 
     lax.fori_loop(0, 4, chunk, 0)
-    out_ref[...] = dot(bwd_ref[...], rhs[...]).astype(BF)
-
-
-def inverse_kernel(back_ref, own_ref, other_ref, skip_ref, bias_ref, ez_ref, ey_ref, out_ref, ubuf, sbuf):
+    send_c[...] = dot(bwd_ref[...], rhs[...]).reshape(G, 8, 128).astype(BF)
+    scatter(me, chan, send_c, recv_c, send_sem.at[4], recv_sem.at[4])
+    settle(send_c, recv_c, send_sem.at[4], recv_sem.at[4])
+    swap_back = swap(recv_c, recv_d, 5)
+    swap_back.start()
+    swap_back.wait()
+
     for q in range(M):
-        both = dot(back_ref[q * M : (q + 1) * M, :], ez_ref[...], ((0,), (0,)))
+        own = recv_c[q * 4 : (q + 1) * 4].astype(F32).reshape(M, 128).astype(BF)
+        other = recv_d[q * 4 : (q + 1) * 4].astype(F32).reshape(M, 128).astype(BF)
+        lines = jnp.concatenate([own, other], axis=0)
+        both = dot(lines, ez_ref[chan], ((0,), (0,)))
         ubuf[q * C : (q + 1) * C, :] = both[0:C, 0:G] + both[C : 2 * C, G : 2 * G]
     for c in range(HALF):
         lines = ubuf[pl.ds(c, 2 * M, stride=HALF), :].astype(BF)
-        sbuf[pl.ds(c, G, stride=HALF), :] = dot(ey_ref[...], lines)
-
-    def step(group, carry):
+        total[pl.ds(c, G, stride=HALF), :] = total[pl.ds(c, G, stride=HALF), :] + dot(ey_ref[...], lines)
+
+    def finish(group, carry):
         for u in range(4):
             rows = pl.ds(pl.multiple_of((group * 4 + u) * HALF, HALF), HALF)
-            latent = jnp.concatenate([own_ref[rows, :], other_ref[rows, :]], axis=0)
-            total = sbuf[rows, :] + dot(skip_ref[...], latent) + bias_ref[...]
-            out_ref[rows, :] = gelu(total).astype(BF)
-        return carry
-
-    lax.fori_loop(0, G // 4, step, 0)
+            grid_ref[rows, :] = gelu(total[rows, :]).astype(BF)
+        return carry
+
+    lax.fori_loop(0, G // 4, finish, 0)
+    swap_grid = swap(grid_ref, grid_other_ref, 6)
+    swap_grid.start()
+    swap_grid.wait()
 
 
 def decode_kernel(line_ref, meta_ref, own_ref, other_ref, proj_in_ref, proj_out_ref, out_ref, todo):
@@ -244,11 +328,16 @@
     lax.fori_loop(0, (count + WIDE - 1) // WIDE, step, 0)
 
 
-def unpack_kernel(slot_ref, values_ref, out_ref):
+def return_kernel(slot_ref, values_ref, out_ref, got, send_sem, recv_sem):
+    me, chan = lax.axis_index("slab"), lax.axis_index("chan")
+    pl.semaphore_wait(greet_all(me, chan), G - 1)
+    scatter(me, chan, values_ref, got, send_sem, recv_sem)
+    settle(values_ref, got, send_sem, recv_sem)
+
     def step(b, carry):
         slot = slot_ref[b]
-        row = values_ref[pl.ds(jnp.maximum(slot, 0), 1), :]
-        out_ref[pl.ds(b, 1), :] = jnp.where(slot >= 0, row, 0.0)
+        taken = jnp.maximum(slot, 0)
+        out_ref[pl.ds(b, 1), :] = jnp.where(slot >= 0, got[taken >> 1, pl.ds(taken & 1, 1), :], 0.0)
         return carry
 
     lax.fori_loop(0, 128, step, 0, unroll=8)
@@ -270,7 +359,6 @@
 ):
     cos, sin = trig()
     chan = lax.axis_index("chan")
-    every = ("slab", "chan")
 
     ids = jnp.arange(128, dtype=jnp.int32)
     live = ids < live_count[0]
@@ -301,32 +389,20 @@
         [pltpu.VMEM((2, (G + 1) * HALF, G), F32)],
         (VM, VM),
     )(chan.reshape(1), lines, parts)
-    received = lax.ppermute(theirs, "chan", [(0, 1), (1, 0)])
 
     dy = jnp.asarray(np.concatenate([cos.T, -sin.T, -cos.T], axis=0), BF)
-    dz = jnp.asarray(np.concatenate([cos.T, sin.T], axis=1), BF)
-    latent, spectra = call(
-        forward_kernel,
-        (jax.ShapeDtypeStruct((G * HALF, G), BF), jax.ShapeDtypeStruct((M * M, 128), BF)),
-        [VM] * 4,
-        [pltpu.VMEM((G * HALF, G), F32), pltpu.VMEM((3 * M * HALF, G), F32)],
-        (VM, VM),
-    )(mine, received, dy, dz)
-    latent_other = lax.ppermute(latent, "chan", [(0, 1), (1, 0)])
-    spectra = lax.all_to_all(spectra.reshape(256, 4, 128), every, split_axis=0, concat_axis=0, tiled=True)
-
+    quads = np.concatenate([cos.T, sin.T], axis=1).reshape(4, 2, 1, 4, 2 * G)
+    dz = np.broadcast_to(quads, (4, 2, 2, 4, 2 * G)).transpose(1, 0, 2, 3, 4).reshape(2 * M, 2 * G)
     eye4, eye2 = np.eye(4), np.eye(2)
     table = np.stack([cos.T, sin.T])
     forward = np.einsum("hg,vkx,mn->hvkmxgn", eye2, table, eye4).reshape(512, 1024)
+    ez = np.zeros((2, 2, 4, 2, 4, 2 * G))
+    for h in range(2):
+        for side in range(2):
+            ez[h, side, :, h, :, :] = quads[:, h if side == 0 else 1 - h, 0]
+    ez = ez.reshape(2, 2 * M, 2 * G)
+    ey = np.stack([cos, -sin], axis=2).reshape(G, 2 * M) / G**3
     weight = jnp.transpose(spec_weight, (0, 1, 3, 4, 2)).reshape(2, C, 128, C)
-    back = call(
-        mix_kernel,
-        jax.ShapeDtypeStruct((1024, 128), BF),
-        [VM] * 4,
-        [pltpu.VMEM((2, 128, C), F32), pltpu.VMEM((512, 128), BF)],
-    )(spectra.reshape(1024, 128), weight, jnp.asarray(forward, BF), jnp.asarray(forward.T, BF))
-    back = lax.all_to_all(back.reshape(256, 4, 128), every, split_axis=0, concat_axis=0, tiled=True)
-
     own = chan * HALF
     other = (1 - chan) * HALF
     skip_own = lax.dynamic_slice_in_dim(skip_w, own, HALF, 1)
@@ -338,15 +414,39 @@
         axis=0,
     ).T
     bias = jnp.broadcast_to(lax.dynamic_slice_in_dim(skip_bias, own, HALF, 0)[:, None], (HALF, G))
-    ez = jnp.asarray(np.concatenate([cos.T, sin.T], axis=1), BF)
-    ey = jnp.asarray(np.stack([cos, -sin], axis=2).reshape(G, 2 * M) / G**3, BF)
-    grid = call(
-        inverse_kernel,
-        jax.ShapeDtypeStruct((G * HALF, G), BF),
-        [VM] * 7,
-        [pltpu.VMEM((M * C, G), F32), pltpu.VMEM((G * HALF, G), F32)],
-    )(back.reshape(1024, 128), latent, latent_other, skip, bias, ez, ey)
-    grid_other = lax.ppermute(grid, "chan", [(0, 1), (1, 0)])
+    plane = (G * HALF, G)
+    block8 = pltpu.VMEM((G, 8, 128), BF)
+    grid, grid_other = pl.pallas_call(
+        middle_kernel,
+        out_shape=(jax.ShapeDtypeStruct(plane, BF), jax.ShapeDtypeStruct(plane, BF)),
+        in_specs=[VM] * 11,
+        out_specs=(VM, VM),
+        scratch_shapes=[
+            pltpu.VMEM(plane, BF),
+            pltpu.VMEM(plane, BF),
+            pltpu.VMEM(plane, BF),
+            pltpu.VMEM(plane, F32),
+            pltpu.VMEM((3 * M * HALF, G), F32),
+            pltpu.VMEM((2, 1024, 128), BF),
+            pltpu.VMEM((1024, 128), BF),
+            block8,
+            block8,
+            pltpu.VMEM((2, 128, C), F32),
+            pltpu.VMEM((512, 128), BF),
+            block8,
+            block8,
+            block8,
+            pltpu.VMEM((M * C, G), F32),
+            pltpu.SemaphoreType.DMA((7,)),
+            pltpu.SemaphoreType.DMA((7,)),
+        ],
+        compiler_params=pltpu.CompilerParams(
+            vmem_limit_bytes=LIMIT, collective_id=1, has_side_effects=True
+        ),
+    )(
+        mine, theirs, weight, jnp.asarray(forward, BF), jnp.asarray(forward.T, BF), dy, jnp.asarray(dz, BF),
+        jnp.asarray(ez, BF), jnp.asarray(ey, BF), skip, bias,
+    )
 
     proj = jnp.concatenate(
         [
@@ -362,8 +462,16 @@
         [SM] + [VM] * 5,
         [pltpu.SMEM((257,), jnp.int32)],
     )(lines, meta, grid, grid_other, proj, proj_row)
-    values = lax.all_to_all(values.reshape(128, 2, PB), "slab", split_axis=0, concat_axis=0, tiled=True)
-    return call(unpack_kernel, jax.ShapeDtypeStruct((128, PB), F32), [SM, VM])(slot, values.reshape(256, PB))
+    return pl.pallas_call(
+        return_kernel,
+        out_shape=jax.ShapeDtypeStruct((128, PB), F32),
+        in_specs=[SM, VM],
+        out_specs=VM,
+        scratch_shapes=[pltpu.VMEM((G, 2, PB), F32)] + [pltpu.SemaphoreType.DMA] * 2,
+        compiler_params=pltpu.CompilerParams(
+            vmem_limit_bytes=LIMIT, collective_id=2, has_side_effects=True
+        ),
+    )(slot, values.reshape(G, 2, PB))
 
 
 def solution(mesh):

time: 246 us -> 234 us (0.951)
  Pallas kernels: 156 us -> 211 us
  blocking collectives: 49.8 us -> 0 us
  waiting for transfers between devices: 18.1 us -> 0 us
  local copies, waits for them, and re-layouts: 6.94 us -> 15.5 us
  starting transfers between devices: 7.83 us -> 0 us
    all_to_all x2 -> x0, blocking collectives: 49.8 us -> none  [the longest x1 26.4 us: shards(): lax.all_to_all(spectra.reshape(256, 4, 128), every, split_axis=0, concat_...]
    pallas_call x4 -> x2, Pallas kernels: 21.3 us -> 70.4 us  [the longest x1 55 us: shards(): pl.pallas_call(middle_kernel, out_shape=(jax.ShapeDtypeStruct(plane, BF),...]
    all_to_all x1 -> x0, waiting for transfers between devices: 14.8 us -> none  [shards(): lax.all_to_all(back.reshape(256, 4, 128), every, split_axis=0, concat_axi...]
    unnamed x31 -> x48, local copies, waits for them, and re-layouts: 5.3 us -> 13.9 us
    pallas_call x1, Pallas kernels: 6.66 us -> 12.4 us  [shards(): call(decode_kernel, jax.ShapeDtypeStruct((256, PB), F32), [SM] + [VM] * 5...]
    all_to_all x1 -> x0, starting transfers between devices: 5.43 us -> none  [shards(): lax.all_to_all(back.reshape(256, 4, 128), every, split_axis=0, concat_axi...]
    ppermute x3 -> x0, waiting for transfers between devices: 3.33 us -> none  [the longest x1 2.29 us: shards(): received = lax.ppermute(theirs, 'chan', [(0, 1), (1, 0)])]
  transfers between devices with their start and end apart: 4 -> 0, of which waited for: 3 -> 0; matrix products, arithmetic and copies ran while one was open for 1% -> 0% of each run, Pallas kernels for 3% -> 0%
where the time goes in v4:
time: 234 us; the launch traced here: 233 us
  Pallas kernels  211 us (90%)
  local copies, waits for them, and re-layouts  15.5 us (7%)
  other arithmetic  5.78 us (2%)
    pallas_call x1, Pallas kernels, shards(): pl.pallas_call(dispatch_kernel, out_shape=jax.ShapeDtypeStruct((G, ROWS,...  124 us
    pallas_call x1, Pallas kernels, shards(): pl.pallas_call(middle_kernel, out_shape=(jax.ShapeDtypeStruct(plane, BF),...  55 us
    pallas_call x1, Pallas kernels, shards(): pl.pallas_call(return_kernel, out_shape=jax.ShapeDtypeStruct((128, PB), F...  15.4 us
    unnamed x48, local copies, waits for them, and re-layouts  13.9 us
    pallas_call x1, Pallas kernels, shards(): call(decode_kernel, jax.ShapeDtypeStruct((256, PB), F32), [SM] + [VM] * 5...  12.4 us

profile of v4, /device:TPU:1, one launch (start us, length us, event | category | flops | bytes accessed | tf_op | source)
XLA Modules:
  0.0 233.2 jit_solution(16313639394885793002)
XLA Ops:
  0.7 0.7 compare_select_fusion.3
  1.3 0.7 fusion.2
  2.0 0.2 convert_reduce_fusion
  2.1 0.7 compare_select_fusion.2.slot_ref
  2.8 0.1 select_reduce_fusion.blk_ref
  2.9 0.8 copy.29
  3.8 1.6 copy-done
  5.3 0.9 copy-done.10
  6.3 0.8 copy-done.11
  7.1 0.7 copy-done.16
  7.8 123.7 %shard_map.172.parts_ref = bf16[128,152,128]{2,1,0:T(8,128)(2,1)} custom-call(s32[256]{0:T(256)S(1)} %select_reduce_fusion.blk_ref, s32[128]{0:T(128)S(1)} %copy-done.16, bf16[128,64,128]{2,1,0:T(8,128)(2,1)S(1)} %copy-done, s32[128,128]{1,0:T(8,128)S(1)} %copy-done.11, bf16[128,8,128]{2,1,0:T(8,128)(2,1)S(1)} %copy-done.10, bf16[64,64]{1,0:T(8,128)(2,1)S(1)} %bitcast.21), custom_call_target="tpu_custom_call" | custom-call | tf_op jit(solution)/shard_map/pallas_call | solution.py:372
  131.6 3.3 %fusion = s32[128,2]{1,0:T(8,128)S(1)} fusion(bf16[128,152,128]{2,1,0:T(8,128)(2,1)} %shard_map.172.parts_ref), kind=kLoop, calls=%fused_computation.2 | loop fusion | flops 1024 | bytes 1536 | tf_op jit(solution)/shard_map/jit(_where)/select_n | solution.py:384
  134.9 0.1 select_n.48.line_ref
  135.0 1.2 slice.8.meta_ref
  136.3 4.5 %shard_map.173 = (f32[4096,128]{1,0:T(8,128)S(1)}, bf16[4096,128]{1,0:T(8,128)(2,1)S(1)}) custom-call(s32[1]{0:T(128)} %bitcast.4.chan_ref, s32[256]{0:T(256)S(1)} %select_n.48.line_ref, bf16[128,152,128]{2,1,0:T(8,128)(2,1)} %shard_map.172.parts_ref), custom_call_target="tpu_custom_call" | custom-call | tf_op jit(solution)/shard_map/pallas_call | solution.py:385
  140.9 1.3 copy-done.1
  142.2 1.0 copy-done.4
  143.1 0.1 fusion.3
  143.2 0.1 copy.35
  143.3 0.1 copy.34
  143.7 1.2 copy-done.5
  144.9 55.0 %shard_map.174 = (bf16[4096,128]{1,0:T(8,128)(2,1)S(1)}, bf16[4096,128]{1,0:T(8,128)(2,1)S(1)}) custom-call(f32[4096,128]{1,0:T(8,128)} %copy-done.1, bf16[4096,128]{1,0:T(8,128)(2,1)S(1)} %copy-done.5, bf16[2,64,128,64]{3,2,1,0:T(8,128)(2,1)} %bitcast.22, bf16[512,1024]{1,0:T(8,128)(2,1)S(1)} %copy-done.2, bf16[1024,512]{1,0:T(8,128)(2,1)S(1)} %copy-done.3, ...), custom_call_target="tpu_custom_call" | custom-call | tf_op jit(solution)/shard_map/pallas_call | solution.py:419
  199.9 1.0 copy-done.6
  200.9 1.0 copy-done.8
  201.9 0.1 copy.37
  202.0 0.1 copy.36
  202.2 0.1 maximum_bitcast_fusion.proj_in_ref
  202.3 1.2 copy-done.7
  203.5 1.2 copy-done.9
  204.7 12.4 %shard_map.175 = f32[256,128]{1,0:T(8,128)S(1)} custom-call(s32[256]{0:T(256)S(1)} %select_n.48.line_ref, bf16[128,24,128]{2,1,0:T(8,128)(2,1)S(1)} %slice.8.meta_ref, bf16[4096,128]{1,0:T(8,128)(2,1)S(1)} %copy-done.7, bf16[4096,128]{1,0:T(8,128)(2,1)S(1)} %copy-done.9, bf16[128,64]{1,0:T(8,128)(2,1)S(1)} %maximum_bitcast_fusion.proj_in_ref, ...), custom_call_target="tpu_custom_call" | custom-call | tf_op jit(solution)/shard_map/pallas_call | solution.py:459
  217.2 15.4 %shard_map.176 = f32[128,128]{1,0:T(8,128)S(1)} custom-call(s32[128]{0:T(128)S(1)} %compare_select_fusion.2.slot_ref, f32[128,2,128]{2,1,0:T(2,128)S(1)} %bitcast.20), custom_call_target="tpu_custom_call" | custom-call | tf_op jit(solution)/shard_map/pallas_call | solution.py:465
  232.6 0.6 copy.40
  (36 shorter events, 0.3 us)
Async XLA Ops:
  3.7 1.6 copy-start
  5.3 0.9 copy-start.10
  6.3 0.8 copy-start.11
  7.1 0.7 copy-start.16
  131.5 11.7 %copy-start.17 = (bf16[64,64]{1,0:T(8,128)(2,1)S(1)}, bf16[64,64]{1,0:T(8,128)(2,1)}, u32[]{:S(2)}) copy-start(bf16[64,64]{1,0:T(8,128)(2,1)} %param.26) | copy-start | bytes 24580
  131.5 12.0 %copy-start.20 = (f32[64]{0:T(128)S(1)}, f32[64]{0:T(128)}, u32[]{:S(2)}) copy-start(f32[64]{0:T(128)} %param.27) | copy-start | bytes 772
  131.5 12.2 %copy-start.2 = (bf16[512,1024]{1,0:T(8,128)(2,1)S(1)}, bf16[512,1024]{1,0:T(8,128)(2,1)}, u32[]{:S(2)}) copy-start(bf16[512,1024]{1,0:T(8,128)(2,1)} %constant.56.clone.fwd_ref) | copy-start | bytes 3145732
  131.5 12.1 %copy-start.3 = (bf16[1024,512]{1,0:T(8,128)(2,1)S(1)}, bf16[1024,512]{1,0:T(8,128)(2,1)}, u32[]{:S(2)}) copy-start(bf16[1024,512]{1,0:T(8,128)(2,1)} %constant.57.clone.bwd_ref) | copy-start | bytes 3145732
  131.5 12.1 %copy-start.12 = (bf16[2,64,256]{2,1,0:T(8,128)(2,1)S(1)}, bf16[2,64,256]{2,1,0:T(8,128)(2,1)}, u32[]{:S(2)}) copy-start(bf16[2,64,256]{2,1,0:T(8,128)(2,1)} %constant.59.clone.ez_ref) | copy-start | bytes 196612
  131.5 12.1 %copy-start.13 = (bf16[64,256]{1,0:T(8,128)(2,1)S(1)}, bf16[64,256]{1,0:T(8,128)(2,1)}, u32[]{:S(2)}) copy-start(bf16[64,256]{1,0:T(8,128)(2,1)} %constant.58.clone.dz_ref) | copy-start | bytes 98308
  131.5 12.1 %copy-start.14 = (bf16[128,64]{1,0:T(8,128)(2,1)S(1)}, bf16[128,64]{1,0:T(8,128)(2,1)}, u32[]{:S(2)}) copy-start(bf16[128,64]{1,0:T(8,128)(2,1)} %constant.60.clone.ey_ref) | copy-start | bytes 49156
  131.6 12.1 %copy-start.15 = (bf16[96,128]{1,0:T(8,128)(2,1)S(1)}, bf16[96,128]{1,0:T(8,128)(2,1)}, u32[]{:S(2)}) copy-start(bf16[96,128]{1,0:T(8,128)(2,1)} %constant.55.clone.dy_ref) | copy-start | bytes 73732
  140.8 1.3 copy-start.1
  142.2 1.0 copy-start.4
  143.7 1.2 copy-start.5
  144.9 57.0 %copy-start.18 = (bf16[64,128]{1,0:T(8,128)(2,1)S(1)}, bf16[64,128]{1,0:T(8,128)(2,1)}, u32[]{:S(2)}) copy-start(bf16[64,128]{1,0:T(8,128)(2,1)} %param.28) | copy-start | bytes 49156
  144.9 57.3 %copy-start.19 = (bf16[128]{0:T(256)(128)(2,1)S(1)}, bf16[128]{0:T(256)(128)(2,1)}, u32[]{:S(2)}) copy-start(bf16[128]{0:T(256)(128)(2,1)} %param.29) | copy-start | bytes 772
  199.9 1.0 copy-start.6
  200.9 1.0 copy-start.8
  202.3 1.2 copy-start.7
  203.5 1.2 copy-start.9

commit v5 on v4

--- a/solution.py
+++ b/solution.py
@@ -19,8 +19,6 @@
 LIMIT = 48 * 1024 * 1024
 VM = pl.BlockSpec(memory_space=pltpu.VMEM)
 SM = pl.BlockSpec(memory_space=pltpu.SMEM)
-WIDE = 16
-ROWS = 152
 
 
 def trig():
@@ -62,11 +60,25 @@
 
 
 def dispatch_kernel(
-    blk_ref, line_ref, points_ref, start_ref, weight_ref, lift_ref, out_ref, stage, send_sem, recv_sem, own_sem
+    blk_ref, line_ref, points_hbm, start_hbm, weight_hbm, lift_ref,
+    out_ref, got_line_ref, meta_ref,
+    points_ref, start_ref, weight_ref, stage, stage_line, send_sem, recv_sem, own_sem,
 ):
     me, chan = lax.axis_index("slab"), lax.axis_index("chan")
     x, z, y = me // 32, (me // 4) % 8, me % 4
-    pl.semaphore_wait(greet_all(me, chan), G - 1)
+    loads = [
+        pltpu.make_async_copy(src, dst, own_sem.at[2 + n])
+        for n, (src, dst) in enumerate(
+            ((points_hbm, points_ref), (start_hbm, start_ref), (weight_hbm, weight_ref))
+        )
+    ]
+    for load in loads:
+        load.start()
+    barrier = greet_all(me, chan)
+    for load in loads:
+        load.wait()
+    pl.semaphore_wait(barrier, G - 1)
+    lane = lax.broadcasted_iota(jnp.int32, (1, PB), 1)
     row = lax.broadcasted_iota(jnp.int32, (8, PB), 0)
 
     def group(g, carry):
@@ -79,12 +91,12 @@
             taken = [jnp.maximum(b, 0) for b in found]
             lines = [jnp.where(b >= 0, line_ref[c] + 1, 0) for b, c in zip(found, taken)]
             starts = [start_ref[pl.ds(c, 1), :] for c in taken]
-            info = jnp.where(row == 2, lines[0], jnp.where(row == 3, lines[1], 0))
-            info = jnp.where(row == 0, starts[0], jnp.where(row == 1, starts[1], info))
+            info = jnp.where(row == 0, starts[0], jnp.where(row == 1, starts[1], 0))
             weights = [weight_ref[c] for c in taken]
-            stage[g * 8 + j, 128:136, :] = weights[0]
-            stage[g * 8 + j, 136:144, :] = weights[1]
-            stage[g * 8 + j, 144:152, :] = info.astype(F32).astype(BF)
+            meta_ref[target, 0:8, :] = weights[0]
+            meta_ref[target, 8:16, :] = weights[1]
+            meta_ref[target, 16:24, :] = info.astype(F32).astype(BF)
+            stage_line[g * 8 + j] = jnp.where(lane == 0, lines[0], jnp.where(lane == 1, lines[1], 0))
             targets.append(target)
             blocks.extend(taken)
             nears.extend(near_transposed(s, w.astype(F32)) for s, w in zip(starts, weights))
@@ -96,28 +108,32 @@
                 part = dot(lifted[:, u * PB : (u + 1) * PB], nears[u], ((1,), (1,)))
                 stage[g * 8 + j, r * C : (r + 1) * C, :] = part.astype(BF)
         for j in range(8):
-            copy = pltpu.make_async_remote_copy(
-                src_ref=stage.at[g * 8 + j],
-                dst_ref=out_ref.at[me],
-                send_sem=send_sem,
-                recv_sem=recv_sem,
-                device_id=(targets[j], chan),
-                device_id_type=pl.DeviceIdType.MESH,
-            )
-            if j < 7:
-                copy.start()
-            else:
-                pl.when(g > 0)(copy.start)
+            for n, (src, dst) in enumerate(((stage_line, got_line_ref), (stage, out_ref))):
+                copy = pltpu.make_async_remote_copy(
+                    src_ref=src.at[g * 8 + j],
+                    dst_ref=dst.at[me],
+                    send_sem=send_sem.at[n],
+                    recv_sem=recv_sem.at[n],
+                    device_id=(targets[j], chan),
+                    device_id_type=pl.DeviceIdType.MESH,
+                )
+                if j < 7:
+                    copy.start()
+                else:
+                    pl.when(g > 0)(copy.start)
         return carry
 
     lax.fori_loop(0, 16, group, 0)
-    own = pltpu.make_async_copy(stage.at[7], out_ref.at[me], own_sem)
-    own.start()
-    own.wait()
-    sent = stage.at[pl.ds(0, G - 1)]
-    pltpu.make_async_copy(sent, sent, send_sem).wait()
-    got = out_ref.at[pl.ds(0, G - 1)]
-    pltpu.make_async_copy(got, got, recv_sem).wait()
+    own = [
+        pltpu.make_async_copy(stage_line.at[7], got_line_ref.at[me], own_sem.at[0]),
+        pltpu.make_async_copy(stage.at[7], out_ref.at[me], own_sem.at[1]),
+    ]
+    for copy in own:
+        copy.start()
+    for copy in own:
+        copy.wait()
+    settle(stage_line, got_line_ref, send_sem.at[0], recv_sem.at[0])
+    settle(stage, out_ref, send_sem.at[1], recv_sem.at[1])
 
 
 def gather_kernel(chan_ref, line_ref, parts_ref, own_ref, other_ref, acc):
@@ -125,7 +141,8 @@
 
     def add(src, carry):
         for r in range(2):
-            line = line_ref[2 * src + r]
+            line = line_ref[src, 0, r]
+            line = jnp.where(line > 0, line - 1, G)
             rows = pl.ds(pl.multiple_of(line * HALF, HALF), HALF)
             for h in range(2):
                 first = r * C + h * HALF
@@ -151,7 +168,7 @@
     return barrier
 
 
-def scatter(me, chan, src, dst, send_sem, recv_sem):
+def send_blocks(first, last, me, chan, src, dst, send_sem, recv_sem):
     def send(i, carry):
         target = (me + i) % G
         pltpu.make_async_remote_copy(
@@ -164,7 +181,11 @@
         ).start()
         return carry
 
-    lax.fori_loop(1, G, send, 0)
+    lax.fori_loop(first, last, send, 0)
+
+
+def scatter(me, chan, src, dst, send_sem, recv_sem):
+    send_blocks(1, G, me, chan, src, dst, send_sem, recv_sem)
     dst[me] = src[me]
 
 
@@ -175,8 +196,10 @@
 
 
 def middle_kernel(
-    mine_ref, theirs_ref, weight_ref, fwd_ref, bwd_ref, dy_ref, dz_ref, ez_ref, ey_ref, skip_ref, bias_ref,
-    grid_ref, grid_other_ref,
+    line_ref, slot_ref, mine_ref, theirs_ref, weight_ref, fwd_ref, bwd_ref, dy_ref, dz_ref, ez_ref, ey_ref, skip_ref,
+    bias_ref, meta_ref, proj_in_ref, proj_out_ref,
+    out_ref,
+    grid_ref, grid_other_ref, got_meta, send_v, recv_v,
     got, latent, latent_other, total, ybuf, spec, spec_other, send_b, recv_b, xbuf, rhs, send_c, recv_c, recv_d, ubuf,
     send_sem, recv_sem,
 ):
@@ -197,6 +220,8 @@
 
     swap_latent = swap(theirs_ref, got, 0)
     swap_latent.start()
+    send_blocks(1, G // 2, me, chan, meta_ref, got_meta, send_sem.at[7], recv_sem.at[7])
+    got_meta[me] = meta_ref[me]
     swap_latent.wait()
     total[...] = mine_ref[...] + got[...].astype(F32)
     latent[...] = total[...].astype(BF)
@@ -241,6 +266,7 @@
 
     lax.fori_loop(0, G // 8, mix_channels, 0)
     settle(send_b, recv_b, send_sem.at[3], recv_sem.at[3])
+    send_blocks(G // 2, G, me, chan, meta_ref, got_meta, send_sem.at[7], recv_sem.at[7])
 
     spectra = recv_b[...].astype(F32).reshape(1024, 128).astype(BF)
     prod = dot(fwd_ref[...], spectra)
@@ -289,58 +315,61 @@
 
     def finish(group, carry):
         for u in range(4):
-            rows = pl.ds(pl.multiple_of((group * 4 + u) * HALF, HALF), HALF)
-            grid_ref[rows, :] = gelu(total[rows, :]).astype(BF)
+            y = group * 4 + u
+            rows = pl.ds(pl.multiple_of(y * HALF, HALF), HALF)
+            grid_ref[y] = gelu(total[rows, :]).astype(BF)
         return carry
 
     lax.fori_loop(0, G // 4, finish, 0)
     swap_grid = swap(grid_ref, grid_other_ref, 6)
     swap_grid.start()
+    settle(meta_ref, got_meta, send_sem.at[7], recv_sem.at[7])
     swap_grid.wait()
 
-
-def decode_kernel(line_ref, meta_ref, own_ref, other_ref, proj_in_ref, proj_out_ref, out_ref, todo):
-    def collect(s, count):
-        todo[count] = s
-        return count + jnp.where(line_ref[s] < G, 1, 0)
-
-    count = lax.fori_loop(0, 256, collect, 0)
-
-    def step(group, carry):
-        slots, cells, nears = [], [], []
-        for u in range(WIDE):
-            s = todo[jnp.minimum(group * WIDE + u, count - 1)]
-            src, rank = s >> 1, s & 1
-            rows = pl.ds(pl.multiple_of(line_ref[s] * HALF, HALF), HALF)
-            info = meta_ref[src, 16:24, :].astype(F32)
-            start = jnp.where(rank == 0, info[0:1, :], info[1:2, :]).astype(jnp.int32)
-            weight = meta_ref[src, pl.ds(pl.multiple_of(rank * 8, 8), 8), :].astype(F32)
-            slots.append(s)
-            cells.append(jnp.concatenate([own_ref[rows, :], other_ref[rows, :]], axis=0))
-            nears.append(near_transposed(start, weight))
-        values = [dot(cells[u], nears[u]).astype(BF) for u in range(WIDE)]
+    def decode(group, carry):
+        slabs, cells, nears = [], [], []
+        for j in range(8):
+            slab = (me + group * 8 + j) % G
+            slabs.append(slab)
+            info = got_meta[slab, 16:24, :].astype(F32).astype(jnp.int32)
+            for r in range(2):
+                line = jnp.maximum(line_ref[slab, 0, r] - 1, 0)
+                weight = got_meta[slab, r * 8 : (r + 1) * 8, :].astype(F32)
+                cells.append(jnp.concatenate([grid_ref[line], grid_other_ref[line]], axis=0))
+                nears.append(near_transposed(info[r : r + 1, :], weight))
+        values = [dot(cell, near).astype(BF) for cell, near in zip(cells, nears)]
         hidden = gelu(dot(proj_in_ref[...], jnp.concatenate(values, axis=1))).astype(BF)
         result = dot(proj_out_ref[...], hidden)
-        for u in range(WIDE):
-            out_ref[pl.ds(slots[u], 1), :] = result[0:1, u * PB : (u + 1) * PB]
-        return carry
-
-    lax.fori_loop(0, (count + WIDE - 1) // WIDE, step, 0)
-
-
-def return_kernel(slot_ref, values_ref, out_ref, got, send_sem, recv_sem):
-    me, chan = lax.axis_index("slab"), lax.axis_index("chan")
-    pl.semaphore_wait(greet_all(me, chan), G - 1)
-    scatter(me, chan, values_ref, got, send_sem, recv_sem)
-    settle(values_ref, got, send_sem, recv_sem)
-
-    def step(b, carry):
+        for j in range(8):
+            for r in range(2):
+                u = 2 * j + r
+                send_v[slabs[j], r : r + 1, :] = result[0:1, u * PB : (u + 1) * PB]
+        for j in range(8):
+            copy = pltpu.make_async_remote_copy(
+                src_ref=send_v.at[slabs[j]],
+                dst_ref=recv_v.at[me],
+                send_sem=send_sem.at[8],
+                recv_sem=recv_sem.at[8],
+                device_id=(slabs[j], chan),
+                device_id_type=pl.DeviceIdType.MESH,
+            )
+            if j > 0:
+                copy.start()
+            else:
+                pl.when(group > 0)(copy.start)
+        return carry
+
+    lax.fori_loop(0, 16, decode, 0)
+    recv_v[me] = send_v[me]
+    settle(send_v, recv_v, send_sem.at[8], recv_sem.at[8])
+
+    def unpack(b, carry):
         slot = slot_ref[b]
         taken = jnp.maximum(slot, 0)
-        out_ref[pl.ds(b, 1), :] = jnp.where(slot >= 0, got[taken >> 1, pl.ds(taken & 1, 1), :], 0.0)
-        return carry
-
-    lax.fori_loop(0, 128, step, 0, unroll=8)
+        out_ref[pl.ds(b, 1), :] = jnp.where(slot >= 0, recv_v[taken >> 1, pl.ds(taken & 1, 1), :], 0.0)
+        return carry
+
+    lax.fori_loop(0, 128, unpack, 0, unroll=8)
 
 
 def shards(
@@ -369,19 +398,30 @@
     slot_ids = jnp.arange(256, dtype=jnp.int32)
     block = jnp.max(jnp.where(slot[None, :] == slot_ids[:, None], ids[None, :], -1), axis=1)
 
-    parts = pl.pallas_call(
+    ANY = pl.BlockSpec(memory_space=pl.ANY)
+    parts, lines, meta = pl.pallas_call(
         dispatch_kernel,
-        out_shape=jax.ShapeDtypeStruct((G, ROWS, PB), BF),
-        in_specs=[SM, SM] + [VM] * 4,
-        out_specs=pl.BlockSpec(memory_space=pl.ANY),
-        scratch_shapes=[pltpu.VMEM((G, ROWS, PB), BF)] + [pltpu.SemaphoreType.DMA] * 3,
+        out_shape=(
+            jax.ShapeDtypeStruct((G, 2 * C, PB), BF),
+            jax.ShapeDtypeStruct((G, 1, PB), jnp.int32),
+            jax.ShapeDtypeStruct((G, 24, PB), BF),
+        ),
+        in_specs=[SM, SM, ANY, ANY, ANY, VM],
+        out_specs=(ANY, ANY, VM),
+        scratch_shapes=[
+            pltpu.VMEM((128, C, PB), BF),
+            pltpu.VMEM((128, PB), jnp.int32),
+            pltpu.VMEM((128, NB, PB), BF),
+            pltpu.VMEM((G, 2 * C, PB), BF),
+            pltpu.VMEM((G, 1, PB), jnp.int32),
+            pltpu.SemaphoreType.DMA((2,)),
+            pltpu.SemaphoreType.DMA((2,)),
+            pltpu.SemaphoreType.DMA((5,)),
+        ],
         compiler_params=pltpu.CompilerParams(
             vmem_limit_bytes=LIMIT, collective_id=0, has_side_effects=True
         ),
     )(block, dest_block, points, near_start, near_weight, lift_w.T)
-    meta = parts[:, 128:152, :]
-    lines = meta[:, 18:20, 0].astype(jnp.int32)
-    lines = jnp.where(lines > 0, lines - 1, G).reshape(256)
     mine, theirs = call(
         gather_kernel,
         (jax.ShapeDtypeStruct((G * HALF, G), F32), jax.ShapeDtypeStruct((G * HALF, G), BF)),
@@ -416,12 +456,25 @@
     bias = jnp.broadcast_to(lax.dynamic_slice_in_dim(skip_bias, own, HALF, 0)[:, None], (HALF, G))
     plane = (G * HALF, G)
     block8 = pltpu.VMEM((G, 8, 128), BF)
-    grid, grid_other = pl.pallas_call(
+    proj = jnp.concatenate(
+        [
+            lax.dynamic_slice_in_dim(proj_in, own, HALF, 0),
+            lax.dynamic_slice_in_dim(proj_in, other, HALF, 0),
+        ],
+        axis=0,
+    ).T
+    proj_row = jnp.broadcast_to(proj_out[None, :], (8, 128))
+    return pl.pallas_call(
         middle_kernel,
-        out_shape=(jax.ShapeDtypeStruct(plane, BF), jax.ShapeDtypeStruct(plane, BF)),
-        in_specs=[VM] * 11,
-        out_specs=(VM, VM),
+        out_shape=jax.ShapeDtypeStruct((128, PB), F32),
+        in_specs=[SM, SM] + [VM] * 14,
+        out_specs=VM,
         scratch_shapes=[
+            pltpu.VMEM((G, HALF, G), BF),
+            pltpu.VMEM((G, HALF, G), BF),
+            pltpu.VMEM((G, 24, PB), BF),
+            pltpu.VMEM((G, 2, PB), F32),
+            pltpu.VMEM((G, 2, PB), F32),
             pltpu.VMEM(plane, BF),
             pltpu.VMEM(plane, BF),
             pltpu.VMEM(plane, BF),
@@ -437,41 +490,16 @@
             block8,
             block8,
             pltpu.VMEM((M * C, G), F32),
-            pltpu.SemaphoreType.DMA((7,)),
-            pltpu.SemaphoreType.DMA((7,)),
+            pltpu.SemaphoreType.DMA((9,)),
+            pltpu.SemaphoreType.DMA((9,)),
         ],
         compiler_params=pltpu.CompilerParams(
             vmem_limit_bytes=LIMIT, collective_id=1, has_side_effects=True
         ),
     )(
-        mine, theirs, weight, jnp.asarray(forward, BF), jnp.asarray(forward.T, BF), dy, jnp.asarray(dz, BF),
-        jnp.asarray(ez, BF), jnp.asarray(ey, BF), skip, bias,
+        lines, slot, mine, theirs, weight, jnp.asarray(forward, BF), jnp.asarray(forward.T, BF), dy, jnp.asarray(dz, BF),
+        jnp.asarray(ez, BF), jnp.asarray(ey, BF), skip, bias, meta, proj, proj_row,
     )
-
-    proj = jnp.concatenate(
-        [
-            lax.dynamic_slice_in_dim(proj_in, own, HALF, 0),
-            lax.dynamic_slice_in_dim(proj_in, other, HALF, 0),
-        ],
-        axis=0,
-    ).T
-    proj_row = jnp.broadcast_to(proj_out[None, :], (8, 128))
-    values = call(
-        decode_kernel,
-        jax.ShapeDtypeStruct((256, PB), F32),
-        [SM] + [VM] * 5,
-        [pltpu.SMEM((257,), jnp.int32)],
-    )(lines, meta, grid, grid_other, proj, proj_row)
-    return pl.pallas_call(
-        return_kernel,
-        out_shape=jax.ShapeDtypeStruct((128, PB), F32),
-        in_specs=[SM, VM],
-        out_specs=VM,
-        scratch_shapes=[pltpu.VMEM((G, 2, PB), F32)] + [pltpu.SemaphoreType.DMA] * 2,
-        compiler_params=pltpu.CompilerParams(
-            vmem_limit_bytes=LIMIT, collective_id=2, has_side_effects=True
-        ),
-    )(slot, values.reshape(G, 2, PB))
 
 
 def solution(mesh):

time: 234 us -> 201 us (0.86)
  Pallas kernels: 211 us -> 188 us
  local copies, waits for them, and re-layouts: 15.5 us -> 9.52 us
  other arithmetic: 5.78 us -> 2.45 us
    pallas_call x4 -> x2, Pallas kernels: 207 us -> 183 us  [the longest x1 108 us: shards(): pl.pallas_call(dispatch_kernel, out_shape=(jax.ShapeDtypeStruct((G, 2 * C...]
    unnamed x48 -> x40, local copies, waits for them, and re-layouts: 13.9 us -> 9.27 us
    select_n x1 -> x0, other arithmetic: 3.33 us -> none  [shards(): lines = jnp.where(lines > 0, lines - 1, G).reshape(256)]
where the time goes in v5:
time: 201 us; the launch traced here: 200 us
  Pallas kernels  188 us (94%)
  local copies, waits for them, and re-layouts  9.52 us (5%)
  other arithmetic  2.45 us (1%)
    pallas_call x1, Pallas kernels, shards(): pl.pallas_call(dispatch_kernel, out_shape=(jax.ShapeDtypeStruct((G, 2 * C...  108 us
    pallas_call x1, Pallas kernels, shards(): pl.pallas_call(middle_kernel, out_shape=jax.ShapeDtypeStruct((128, PB), F...  74.6 us
    unnamed x40, local copies, waits for them, and re-layouts  9.27 us
    pallas_call x1, Pallas kernels, shards(): call(gather_kernel, (jax.ShapeDtypeStruct((G * HALF, G), F32), jax.ShapeD...  4.53 us

profile of v5, /device:TPU:1, one launch (start us, length us, event | category | flops | bytes accessed | tf_op | source)
XLA Modules:
  0.0 200.4 jit_solution(10956471759885186019)
XLA Ops:
  0.7 0.7 compare_select_fusion.2
  1.3 0.7 fusion.1
  2.0 0.2 convert_reduce_fusion
  2.2 0.7 compare_select_fusion.1.slot_ref
  2.9 0.1 select_reduce_fusion.blk_ref
  3.0 0.8 copy.24
  3.8 0.0 copy-start
  3.8 1.6 copy-done
  5.4 0.9 copy-done.6
  6.3 0.8 copy-done.8
  7.2 0.7 copy-done.12
  7.8 0.0 copy-start.3
  7.8 0.0 copy-start.7
  7.9 0.0 copy-start.10
  7.9 108.4 %shard_map.172 = (bf16[128,128,128]{2,1,0:T(8,128)(2,1)}, s32[128,1,128]{2,1,0:T(1,128)S(1)}, bf16[128,24,128]{2,1,0:T(8,128)(2,1)S(1)}) custom-call(s32[256]{0:T(256)S(1)} %select_reduce_fusion.blk_ref, s32[128]{0:T(128)S(1)} %copy-done.12, bf16[128,64,128]{2,1,0:T(8,128)(2,1)S(1)} %copy-done, s32[128,128]{1,0:T(8,128)S(1)} %copy-done.8, ...), custom_call_target="tpu_custom_call" | custom-call | tf_op jit(solution)/shard_map/pallas_call | solution.py:402
  116.3 0.0 copy-start.4
  116.3 0.9 copy-done.4
  117.2 4.5 %shard_map.173 = (f32[4096,128]{1,0:T(8,128)S(1)}, bf16[4096,128]{1,0:T(8,128)(2,1)S(1)}) custom-call(s32[1]{0:T(128)} %bitcast.4.chan_ref, s32[128,1,128]{2,1,0:T(1,128)S(1)} %get-tuple-element.10.line_ref, bf16[128,128,128]{2,1,0:T(8,128)(2,1)} %get-tuple-element.11.parts_ref), custom_call_target="tpu_custom_call" | custom-call | tf_op jit(solution)/shard_map/pallas_call | solution.py:425
  121.7 1.3 copy-done.1
  123.1 0.0 copy-done.13
  123.1 0.1 fusion.2
  123.2 0.1 copy.30
  123.2 0.1 copy.29
  123.3 0.1 maximum_bitcast_fusion.1.skip_ref
  123.4 0.1 dynamic_slice.18
  123.5 0.1 broadcast_in_dim.42.bias_ref
  123.6 0.1 copy.32
  123.7 0.1 copy.31
  123.8 0.1 maximum_bitcast_fusion.proj_in_ref
  124.0 1.1 copy-done.5
  125.1 74.6 %shard_map.174 = f32[128,128]{1,0:T(8,128)S(1)} custom-call(s32[128,1,128]{2,1,0:T(1,128)S(1)} %get-tuple-element.10.line_ref, s32[128]{0:T(128)S(1)} %compare_select_fusion.1.slot_ref, f32[4096,128]{1,0:T(8,128)} %copy-done.1, bf16[4096,128]{1,0:T(8,128)(2,1)S(1)} %get-tuple-element.13.theirs_ref, bf16[2,64,128,64]{3,2,1,0:T(8,128)(2,1)} %bitcast.20, ...), custom_call_target="tpu_custom_call" | custom-call | tf_op jit(solution)/shard_map/pallas_call | solution.py:467
  199.7 0.6 copy.35
  (23 shorter events, 0.0 us)
Async XLA Ops:
  0.0 124.0 %copy-start.11 = (bf16[96,128]{1,0:T(8,128)(2,1)S(1)}, bf16[96,128]{1,0:T(8,128)(2,1)}, u32[]{:S(2)}) copy-start(bf16[96,128]{1,0:T(8,128)(2,1)} %constant.50.clone.dy_ref) | copy-start | bytes 73732
  0.0 124.0 %copy-start.9 = (bf16[64,256]{1,0:T(8,128)(2,1)S(1)}, bf16[64,256]{1,0:T(8,128)(2,1)}, u32[]{:S(2)}) copy-start(bf16[64,256]{1,0:T(8,128)(2,1)} %constant.53.clone.dz_ref) | copy-start | bytes 98308
  0.0 123.9 %copy-start.15 = (bf16[128]{0:T(256)(128)(2,1)S(1)}, bf16[128]{0:T(256)(128)(2,1)}, u32[]{:S(2)}) copy-start(bf16[128]{0:T(256)(128)(2,1)} %param.29) | copy-start | bytes 772
  3.8 1.6 copy-start
  5.4 0.9 copy-start.6
  6.3 0.8 copy-start.8
  7.2 0.7 copy-start.12
  7.8 115.2 %copy-start.13 = (bf16[64,64]{1,0:T(8,128)(2,1)S(1)}, bf16[64,64]{1,0:T(8,128)(2,1)}, u32[]{:S(2)}) copy-start(bf16[64,64]{1,0:T(8,128)(2,1)} %param.26) | copy-start | bytes 24580
  7.8 115.6 %copy-start.16 = (f32[64]{0:T(128)S(1)}, f32[64]{0:T(128)}, u32[]{:S(2)}) copy-start(f32[64]{0:T(128)} %param.27) | copy-start | bytes 772
  7.8 115.7 %copy-start.14 = (bf16[64,128]{1,0:T(8,128)(2,1)S(1)}, bf16[64,128]{1,0:T(8,128)(2,1)}, u32[]{:S(2)}) copy-start(bf16[64,128]{1,0:T(8,128)(2,1)} %param.28) | copy-start | bytes 49156
  7.8 116.1 %copy-start.2 = (bf16[512,1024]{1,0:T(8,128)(2,1)S(1)}, bf16[512,1024]{1,0:T(8,128)(2,1)}, u32[]{:S(2)}) copy-start(bf16[512,1024]{1,0:T(8,128)(2,1)} %constant.51.clone.fwd_ref) | copy-start | bytes 3145732
  7.8 116.1 %copy-start.3 = (bf16[1024,512]{1,0:T(8,128)(2,1)S(1)}, bf16[1024,512]{1,0:T(8,128)(2,1)}, u32[]{:S(2)}) copy-start(bf16[1024,512]{1,0:T(8,128)(2,1)} %constant.52.clone.bwd_ref) | copy-start | bytes 3145732
  7.8 116.1 %copy-start.7 = (bf16[2,64,256]{2,1,0:T(8,128)(2,1)S(1)}, bf16[2,64,256]{2,1,0:T(8,128)(2,1)}, u32[]{:S(2)}) copy-start(bf16[2,64,256]{2,1,0:T(8,128)(2,1)} %constant.54.clone.ez_ref) | copy-start | bytes 196612
  7.9 116.1 %copy-start.10 = (bf16[128,64]{1,0:T(8,128)(2,1)S(1)}, bf16[128,64]{1,0:T(8,128)(2,1)}, u32[]{:S(2)}) copy-start(bf16[128,64]{1,0:T(8,128)(2,1)} %constant.55.clone.ey_ref) | copy-start | bytes 49156
  116.3 0.9 copy-start.4
  121.7 1.3 copy-start.1
  124.0 1.1 copy-start.5

commit v6 on v5

--- a/solution.py
+++ b/solution.py
@@ -16,9 +16,11 @@
 HALF = 32
 BF = jnp.bfloat16
 F32 = jnp.float32
-LIMIT = 48 * 1024 * 1024
+LIMIT = 60 * 1024 * 1024
 VM = pl.BlockSpec(memory_space=pltpu.VMEM)
 SM = pl.BlockSpec(memory_space=pltpu.SMEM)
+ANY = pl.BlockSpec(memory_space=pl.ANY)
+SELF = 7
 
 
 def trig():
@@ -60,7 +62,7 @@
 
 
 def dispatch_kernel(
-    blk_ref, line_ref, points_hbm, start_hbm, weight_hbm, lift_ref,
+    lo_ref, hi_ref, line_ref, points_hbm, start_hbm, weight_hbm, lift_ref,
     out_ref, got_line_ref, meta_ref,
     points_ref, start_ref, weight_ref, stage, stage_line, send_sem, recv_sem, own_sem,
 ):
@@ -82,12 +84,15 @@
     row = lax.broadcasted_iota(jnp.int32, (8, PB), 0)
 
     def group(g, carry):
-        line_x = (x + g // 4) % 4 * 32 + (y + g % 4) % 4
         targets, blocks, nears = [], [], []
         for j in range(8):
             hop = (j + 1) // 2
-            target = line_x + (z + (4 + hop if j % 2 else 4 - hop)) % 8 * 4
-            found = [blk_ref[2 * target + r] for r in range(2)]
+            to_z = (z + (4 + hop if j % 2 else 4 - hop)) % 8
+            to_x = (x + g // 4 + j) % 4
+            to_y = (y + g + j + j // 4 * 2) % 4
+            target = to_x * 32 + to_z * 4 + to_y
+            lo, hi = lo_ref[target], hi_ref[target]
+            found = [jnp.where(hi >= 0, lo, -1), jnp.where(hi > lo, hi, -1)]
             taken = [jnp.maximum(b, 0) for b in found]
             lines = [jnp.where(b >= 0, line_ref[c] + 1, 0) for b, c in zip(found, taken)]
             starts = [start_ref[pl.ds(c, 1), :] for c in taken]
@@ -101,7 +106,7 @@
             blocks.extend(taken)
             nears.extend(near_transposed(s, w.astype(F32)) for s, w in zip(starts, weights))
         points = jnp.concatenate([points_ref[b] for b in blocks], axis=1)
-        lifted = dot(lift_ref[...], points).astype(BF)
+        lifted = dot(lift_ref[...], points, ((0,), (0,))).astype(BF)
         for j in range(8):
             for r in range(2):
                 u = 2 * j + r
@@ -120,13 +125,13 @@
                 if j < 7:
                     copy.start()
                 else:
-                    pl.when(g > 0)(copy.start)
+                    pl.when(g != SELF)(copy.start)
         return carry
 
     lax.fori_loop(0, 16, group, 0)
     own = [
-        pltpu.make_async_copy(stage_line.at[7], got_line_ref.at[me], own_sem.at[0]),
-        pltpu.make_async_copy(stage.at[7], out_ref.at[me], own_sem.at[1]),
+        pltpu.make_async_copy(stage_line.at[SELF * 8 + 7], got_line_ref.at[me], own_sem.at[0]),
+        pltpu.make_async_copy(stage.at[SELF * 8 + 7], out_ref.at[me], own_sem.at[1]),
     ]
     for copy in own:
         copy.start()
@@ -137,22 +142,29 @@
 
 
 def gather_kernel(chan_ref, line_ref, parts_ref, own_ref, other_ref, acc):
-    acc[...] = jnp.zeros_like(acc)
-
-    def add(src, carry):
+    step = pl.program_id(0)
+    chan = chan_ref[0]
+
+    @pl.when(step == 0)
+    def clear():
+        own_ref[...] = jnp.zeros_like(own_ref)
+        acc[...] = jnp.zeros_like(acc)
+
+    def add(i, carry):
         for r in range(2):
-            line = line_ref[src, 0, r]
+            line = line_ref[step * 16 + i, 0, r]
             line = jnp.where(line > 0, line - 1, G)
             rows = pl.ds(pl.multiple_of(line * HALF, HALF), HALF)
-            for h in range(2):
-                first = r * C + h * HALF
-                acc[h, rows, :] += parts_ref[src, first : first + HALF, :].astype(F32)
-        return carry
-
-    lax.fori_loop(0, G, add, 0)
-    chan = chan_ref[0]
-    own_ref[...] = acc[chan, 0 : G * HALF, :]
-    other_ref[...] = acc[1 - chan, 0 : G * HALF, :].astype(BF)
+            for half, total in ((chan, own_ref), (1 - chan, acc)):
+                first = pl.multiple_of(r * C + half * HALF, HALF)
+                total[rows, :] += parts_ref[i, pl.ds(first, HALF), :].astype(F32)
+        return carry
+
+    lax.fori_loop(0, 16, add, 0, unroll=4)
+
+    @pl.when(step == 7)
+    def finish():
+        other_ref[...] = acc[0 : G * HALF, :].astype(BF)
 
 
 def greet_all(me, chan):
@@ -196,14 +208,29 @@
 
 
 def middle_kernel(
-    line_ref, slot_ref, mine_ref, theirs_ref, weight_ref, fwd_ref, bwd_ref, dy_ref, dz_ref, ez_ref, ey_ref, skip_ref,
-    bias_ref, meta_ref, proj_in_ref, proj_out_ref,
+    line_ref, low_ref, slab_ref, count_ref, mine_ref, theirs_ref, weight_hbm, fwd_hbm, bwd_hbm, meta_ref,
+    dy_ref, dz_ref, ez_ref, ey_ref, skip_ref, bias_ref, proj_in_ref, proj_out_ref,
     out_ref,
+    weight_ref, fwd_ref, bwd_ref, load_sem,
     grid_ref, grid_other_ref, got_meta, send_v, recv_v,
     got, latent, latent_other, total, ybuf, spec, spec_other, send_b, recv_b, xbuf, rhs, send_c, recv_c, recv_d, ubuf,
     send_sem, recv_sem,
 ):
     me, chan = lax.axis_index("slab"), lax.axis_index("chan")
+    loads = [
+        pltpu.make_async_copy(src, dst, load_sem.at[n])
+        for n, (src, dst) in enumerate(
+            (
+                (mine_ref.at[pl.ds(0, G * HALF)], total),
+                (meta_ref.at[me], got_meta.at[me]),
+                (fwd_hbm, fwd_ref),
+                (weight_hbm, weight_ref),
+                (bwd_hbm, bwd_ref),
+            )
+        )
+    ]
+    for load in loads:
+        load.start()
     barrier = greet_all(me, chan)
     pl.semaphore_signal(barrier, inc=1, device_id=(me, 1 - chan), device_id_type=pl.DeviceIdType.MESH)
     pl.semaphore_wait(barrier, G)
@@ -221,9 +248,9 @@
     swap_latent = swap(theirs_ref, got, 0)
     swap_latent.start()
     send_blocks(1, G // 2, me, chan, meta_ref, got_meta, send_sem.at[7], recv_sem.at[7])
-    got_meta[me] = meta_ref[me]
+    loads[0].wait()
     swap_latent.wait()
-    total[...] = mine_ref[...] + got[...].astype(F32)
+    total[...] = total[...] + got[...].astype(F32)
     latent[...] = total[...].astype(BF)
     swap_other = swap(latent, latent_other, 1)
     swap_other.start()
@@ -268,6 +295,8 @@
     settle(send_b, recv_b, send_sem.at[3], recv_sem.at[3])
     send_blocks(G // 2, G, me, chan, meta_ref, got_meta, send_sem.at[7], recv_sem.at[7])
 
+    for load in loads[1:]:
+        load.wait()
     spectra = recv_b[...].astype(F32).reshape(1024, 128).astype(BF)
     prod = dot(fwd_ref[...], spectra)
     for h in range(2):
@@ -364,9 +393,10 @@
     settle(send_v, recv_v, send_sem.at[8], recv_sem.at[8])
 
     def unpack(b, carry):
-        slot = slot_ref[b]
-        taken = jnp.maximum(slot, 0)
-        out_ref[pl.ds(b, 1), :] = jnp.where(slot >= 0, recv_v[taken >> 1, pl.ds(taken & 1, 1), :], 0.0)
+        slab = slab_ref[b]
+        rank = jnp.where(low_ref[slab] == b, 0, 1)
+        value = recv_v[slab, pl.ds(rank, 1), :]
+        out_ref[pl.ds(b, 1), :] = jnp.where(b < count_ref[0], value, 0.0)
         return carry
 
     lax.fori_loop(0, 128, unpack, 0, unroll=8)
@@ -390,15 +420,11 @@
     chan = lax.axis_index("chan")
 
     ids = jnp.arange(128, dtype=jnp.int32)
-    live = ids < live_count[0]
-    target = jnp.where(live, dest_slab[:, 0], -1)
-    same = (target[:, None] == target[None, :]) & (ids[None, :] < ids[:, None])
-    rank = jnp.sum(same.astype(jnp.int32), axis=1)
-    slot = jnp.where(live, target * 2 + rank, -1)
-    slot_ids = jnp.arange(256, dtype=jnp.int32)
-    block = jnp.max(jnp.where(slot[None, :] == slot_ids[:, None], ids[None, :], -1), axis=1)
-
-    ANY = pl.BlockSpec(memory_space=pl.ANY)
+    target = jnp.where(ids < live_count[0], dest_slab[:, 0], -1)
+    match = target[None, :] == ids[:, None]
+    low = jnp.min(jnp.where(match, ids[None, :], 128), axis=1)
+    high = jnp.max(jnp.where(match, ids[None, :], -1), axis=1)
+
     parts, lines, meta = pl.pallas_call(
         dispatch_kernel,
         out_shape=(
@@ -406,7 +432,7 @@
             jax.ShapeDtypeStruct((G, 1, PB), jnp.int32),
             jax.ShapeDtypeStruct((G, 24, PB), BF),
         ),
-        in_specs=[SM, SM, ANY, ANY, ANY, VM],
+        in_specs=[SM, SM, SM, ANY, ANY, ANY, VM],
         out_specs=(ANY, ANY, VM),
         scratch_shapes=[
             pltpu.VMEM((128, C, PB), BF),
@@ -421,13 +447,21 @@
         compiler_params=pltpu.CompilerParams(
             vmem_limit_bytes=LIMIT, collective_id=0, has_side_effects=True
         ),
-    )(block, dest_block, points, near_start, near_weight, lift_w.T)
-    mine, theirs = call(
+    )(low, high, dest_block, points, near_start, near_weight, lift_w)
+    mine, theirs = pl.pallas_call(
         gather_kernel,
-        (jax.ShapeDtypeStruct((G * HALF, G), F32), jax.ShapeDtypeStruct((G * HALF, G), BF)),
-        [SM, SM, VM],
-        [pltpu.VMEM((2, (G + 1) * HALF, G), F32)],
-        (VM, VM),
+        grid=(8,),
+        out_shape=(
+            jax.ShapeDtypeStruct(((G + 1) * HALF, G), F32),
+            jax.ShapeDtypeStruct((G * HALF, G), BF),
+        ),
+        in_specs=[SM, SM, pl.BlockSpec((16, 2 * C, PB), lambda i: (i, 0, 0))],
+        out_specs=(
+            pl.BlockSpec(((G + 1) * HALF, G), lambda i: (0, 0)),
+            pl.BlockSpec((G * HALF, G), lambda i: (0, 0)),
+        ),
+        scratch_shapes=[pltpu.VMEM(((G + 1) * HALF, G), F32)],
+        compiler_params=pltpu.CompilerParams(vmem_limit_bytes=LIMIT),
     )(chan.reshape(1), lines, parts)
 
     dy = jnp.asarray(np.concatenate([cos.T, -sin.T, -cos.T], axis=0), BF)
@@ -467,9 +501,13 @@
     return pl.pallas_call(
         middle_kernel,
         out_shape=jax.ShapeDtypeStruct((128, PB), F32),
-        in_specs=[SM, SM] + [VM] * 14,
+        in_specs=[SM] * 4 + [ANY] * 6 + [VM] * 8,
         out_specs=VM,
         scratch_shapes=[
+            pltpu.VMEM((2, C, 128, C), BF),
+            pltpu.VMEM((512, 1024), BF),
+            pltpu.VMEM((1024, 512), BF),
+            pltpu.SemaphoreType.DMA((5,)),
             pltpu.VMEM((G, HALF, G), BF),
             pltpu.VMEM((G, HALF, G), BF),
             pltpu.VMEM((G, 24, PB), BF),
@@ -497,8 +535,9 @@
             vmem_limit_bytes=LIMIT, collective_id=1, has_side_effects=True
         ),
     )(
-        lines, slot, mine, theirs, weight, jnp.asarray(forward, BF), jnp.asarray(forward.T, BF), dy, jnp.asarray(dz, BF),
-        jnp.asarray(ez, BF), jnp.asarray(ey, BF), skip, bias, meta, proj, proj_row,
+        lines, low, dest_slab[:, 0], live_count, mine, theirs, weight,
+        jnp.asarray(forward, BF), jnp.asarray(forward.T, BF), meta,
+        dy, jnp.asarray(dz, BF), jnp.asarray(ez, BF), jnp.asarray(ey, BF), skip, bias, proj, proj_row,
     )
 
 

time: 201 us -> 198 us (0.985)
  local copies, waits for them, and re-layouts: 9.52 us -> 3.3 us
  Pallas kernels: 188 us -> 191 us
    unnamed x40 -> x13, local copies, waits for them, and re-layouts: 9.27 us -> 1.9 us
    pallas_call x1, Pallas kernels: 4.53 us -> 8.26 us  [shards(): pl.pallas_call(gather_kernel, grid=(8,), out_shape=(jax.ShapeDtypeStruct(...]
where the time goes in v6:
time: 198 us; the launch traced here: 197 us
  Pallas kernels  191 us (96%)
  local copies, waits for them, and re-layouts  3.3 us (2%)
  other arithmetic  2.75 us (1%)
    pallas_call x1, Pallas kernels, shards(): pl.pallas_call(dispatch_kernel, out_shape=(jax.ShapeDtypeStruct((G, 2 * C...  110 us
    pallas_call x1, Pallas kernels, shards(): pl.pallas_call(middle_kernel, out_shape=jax.ShapeDtypeStruct((128, PB), F...  72.7 us
    pallas_call x1, Pallas kernels, shards(): pl.pallas_call(gather_kernel, grid=(8,), out_shape=(jax.ShapeDtypeStruct(...  8.26 us

profile of v6, /device:TPU:1, one launch (start us, length us, event | category | flops | bytes accessed | tf_op | source)
XLA Modules:
  0.0 197.4 jit_solution(9366165682035087114)
XLA Ops:
  0.0 0.0 copy-start
  0.0 0.0 copy-start.3
  0.0 0.0 copy-start.1
  0.0 0.0 copy-start.2
  0.7 0.7 compare_select_fusion
  1.4 0.7 select_reduce_fusion
  2.1 109.7 %shard_map.172 = (bf16[128,128,128]{2,1,0:T(8,128)(2,1)}, s32[128,1,128]{2,1,0:T(1,128)}, bf16[128,24,128]{2,1,0:T(8,128)(2,1)}) custom-call(s32[128]{0:T(128)} %get-tuple-element.16.lo_ref.low_ref, s32[128]{0:T(128)} %get-tuple-element.15.hi_ref, s32[128]{0:T(128)} %line_ref.1, bf16[128,64,128]{2,1,0:T(8,128)(2,1)} %points_hbm.1, s32[128,128]{1,0:T(8,128)} %start_hbm.1, ...), custom_call_target="tpu_custom_call" | custom-call | tf_op jit(solution)/shard_map/pallas_call | solution.py:428
  111.8 8.3 %shard_map.173 = (f32[4128,128]{1,0:T(8,128)}, bf16[4096,128]{1,0:T(8,128)(2,1)}) custom-call(s32[1]{0:T(128)} %bitcast.2.chan_ref, s32[128,1,128]{2,1,0:T(1,128)} %get-tuple-element.10.line_ref, bf16[128,128,128]{2,1,0:T(8,128)(2,1)} %get-tuple-element.11.parts_ref), custom_call_target="tpu_custom_call" | custom-call | tf_op jit(solution)/shard_map/pallas_call | solution.py:451
  120.0 0.0 copy-done
  120.0 0.1 fusion
  120.1 0.1 copy.28
  120.2 0.1 copy.27
  120.3 0.7 maximum_bitcast_fusion.1.skip_ref
  121.0 0.0 copy-done.3
  121.0 0.1 dynamic_slice.18
  121.1 0.7 broadcast_in_dim.45.bias_ref
  121.7 0.0 copy-done.1
  121.7 0.1 copy.30
  121.9 0.1 copy.29
  122.0 0.7 maximum_bitcast_fusion.proj_in_ref
  122.7 0.0 copy-done.2
  122.7 0.6 broadcast_in_dim.46.proj_out_ref
  123.3 72.7 %shard_map.174 = f32[128,128]{1,0:T(8,128)} custom-call(s32[128,1,128]{2,1,0:T(1,128)} %get-tuple-element.10.line_ref, s32[128]{0:T(128)} %get-tuple-element.16.lo_ref.low_ref, s32[128]{0:T(128)} %bitcast.13, s32[1]{0:T(128)} %copy.32.count_ref, f32[4128,128]{1,0:T(8,128)} %get-tuple-element.12.mine_ref, bf16[4096,128]{1,0:T(8,128)(2,1)} %get-tuple-element.13.theirs_ref, ...), custom_call_target="tpu_custom_call" | custom-call | tf_op jit(solution)/shard_map/pallas_call | solution.py:501
  195.9 1.5 copy.33
  (1 shorter events, 0.0 us)
Async XLA Ops:
  0.0 120.0 %copy-start = (bf16[64,64]{1,0:T(8,128)(2,1)S(1)}, bf16[64,64]{1,0:T(8,128)(2,1)}, u32[]{:S(2)}) copy-start(bf16[64,64]{1,0:T(8,128)(2,1)} %param.26) | copy-start | bytes 24580
  0.0 121.0 %copy-start.3 = (f32[64]{0:T(128)S(1)}, f32[64]{0:T(128)}, u32[]{:S(2)}) copy-start(f32[64]{0:T(128)} %param.27) | copy-start | bytes 772
  0.0 121.7 %copy-start.1 = (bf16[64,128]{1,0:T(8,128)(2,1)S(1)}, bf16[64,128]{1,0:T(8,128)(2,1)}, u32[]{:S(2)}) copy-start(bf16[64,128]{1,0:T(8,128)(2,1)} %param.28) | copy-start | bytes 49156
  0.0 122.7 %copy-start.2 = (bf16[128]{0:T(256)(128)(2,1)S(1)}, bf16[128]{0:T(256)(128)(2,1)}, u32[]{:S(2)}) copy-start(bf16[128]{0:T(256)(128)(2,1)} %param.29) | copy-start | bytes 772

commit v7 on v6

--- a/solution.py
+++ b/solution.py
@@ -67,7 +67,7 @@
     points_ref, start_ref, weight_ref, stage, stage_line, send_sem, recv_sem, own_sem,
 ):
     me, chan = lax.axis_index("slab"), lax.axis_index("chan")
-    x, z, y = me // 32, (me // 4) % 8, me % 4
+    x, z, y = me >> 5, (me >> 2) & 7, me & 3
     loads = [
         pltpu.make_async_copy(src, dst, own_sem.at[2 + n])
         for n, (src, dst) in enumerate(
@@ -87,9 +87,9 @@
         targets, blocks, nears = [], [], []
         for j in range(8):
             hop = (j + 1) // 2
-            to_z = (z + (4 + hop if j % 2 else 4 - hop)) % 8
-            to_x = (x + g // 4 + j) % 4
-            to_y = (y + g + j + j // 4 * 2) % 4
+            to_z = (z + (4 + hop if j % 2 else 4 - hop)) & 7
+            to_x = (x + (g >> 2) + j) & 3
+            to_y = (y + g + j + j // 4 * 2) & 3
             target = to_x * 32 + to_z * 4 + to_y
             lo, hi = lo_ref[target], hi_ref[target]
             found = [jnp.where(hi >= 0, lo, -1), jnp.where(hi > lo, hi, -1)]
@@ -141,48 +141,73 @@
     settle(stage, out_ref, send_sem.at[1], recv_sem.at[1])
 
 
-def gather_kernel(chan_ref, line_ref, parts_ref, own_ref, other_ref, acc):
-    step = pl.program_id(0)
-    chan = chan_ref[0]
-
-    @pl.when(step == 0)
-    def clear():
-        own_ref[...] = jnp.zeros_like(own_ref)
-        acc[...] = jnp.zeros_like(acc)
-
-    def add(i, carry):
+def gather_kernel(chan_ref, line_ref, parts_hbm, own_hbm, other_hbm, parts_ref, acc, other, sem):
+    def load(k):
+        rows = pl.ds(k * 16, 16)
+        return pltpu.make_async_copy(parts_hbm.at[rows], parts_ref.at[rows], sem.at[k])
+
+    for k in range(8):
+        load(k).start()
+    acc[...] = jnp.zeros_like(acc)
+
+    def add(src):
         for r in range(2):
-            line = line_ref[step * 16 + i, 0, r]
+            line = line_ref[src, 0, r]
             line = jnp.where(line > 0, line - 1, G)
             rows = pl.ds(pl.multiple_of(line * HALF, HALF), HALF)
-            for half, total in ((chan, own_ref), (1 - chan, acc)):
-                first = pl.multiple_of(r * C + half * HALF, HALF)
-                total[rows, :] += parts_ref[i, pl.ds(first, HALF), :].astype(F32)
-        return carry
-
-    lax.fori_loop(0, 16, add, 0, unroll=4)
-
-    @pl.when(step == 7)
-    def finish():
-        other_ref[...] = acc[0 : G * HALF, :].astype(BF)
+            for h in range(2):
+                first = r * C + h * HALF
+                acc[h, rows, :] += parts_ref[src, first : first + HALF, :].astype(F32)
+
+    def chunk(k, carry):
+        load(k).wait()
+
+        def four(i, carry):
+            for u in range(4):
+                add(k * 16 + i * 4 + u)
+            return carry
+
+        return lax.fori_loop(0, 4, four, carry)
+
+    lax.fori_loop(0, 8, chunk, 0)
+    chan = chan_ref[0]
+    keep = pltpu.make_async_copy(acc.at[chan, pl.ds(0, G * HALF)], own_hbm, sem.at[8])
+    keep.start()
+    other[...] = acc[1 - chan, 0 : G * HALF, :].astype(BF)
+    give = pltpu.make_async_copy(other, other_hbm, sem.at[9])
+    give.start()
+    keep.wait()
+    give.wait()
+
+
+def each(first, last, step):
+    edge = -(-first // 8) * 8
+    for i in range(first, edge):
+        step(i)
+
+    def eight(group, carry):
+        for u in range(8):
+            step(group * 8 + u)
+        return carry
+
+    lax.fori_loop(edge // 8, last // 8, eight, 0)
 
 
 def greet_all(me, chan):
     barrier = pltpu.get_barrier_semaphore()
 
-    def greet(i, carry):
+    def greet(i):
         pl.semaphore_signal(
-            barrier, inc=1, device_id=((me + i) % G, chan), device_id_type=pl.DeviceIdType.MESH
+            barrier, inc=1, device_id=((me + i) & (G - 1), chan), device_id_type=pl.DeviceIdType.MESH
         )
-        return carry
-
-    lax.fori_loop(1, G, greet, 0)
+
+    each(1, G, greet)
     return barrier
 
 
 def send_blocks(first, last, me, chan, src, dst, send_sem, recv_sem):
-    def send(i, carry):
-        target = (me + i) % G
+    def send(i):
+        target = (me + i) & (G - 1)
         pltpu.make_async_remote_copy(
             src_ref=src.at[target],
             dst_ref=dst.at[me],
@@ -191,9 +216,8 @@
             device_id=(target, chan),
             device_id_type=pl.DeviceIdType.MESH,
         ).start()
-        return carry
-
-    lax.fori_loop(first, last, send, 0)
+
+    each(first, last, send)
 
 
 def scatter(me, chan, src, dst, send_sem, recv_sem):
@@ -208,12 +232,12 @@
 
 
 def middle_kernel(
-    line_ref, low_ref, slab_ref, count_ref, mine_ref, theirs_ref, weight_hbm, fwd_hbm, bwd_hbm, meta_ref,
-    dy_ref, dz_ref, ez_ref, ey_ref, skip_ref, bias_ref, proj_in_ref, proj_out_ref,
+    line_ref, low_ref, slab_ref, count_ref, bias_ref, mine_ref, theirs_ref, weight_hbm, fwd_hbm, bwd_hbm, meta_ref,
+    dy_ref, dz_ref, ez_ref, ey_ref, skip_ref, proj_in_ref, proj_out_ref,
     out_ref,
-    weight_ref, fwd_ref, bwd_ref, load_sem,
-    grid_ref, grid_other_ref, got_meta, send_v, recv_v,
-    got, latent, latent_other, total, ybuf, spec, spec_other, send_b, recv_b, xbuf, rhs, send_c, recv_c, recv_d, ubuf,
+    weight_ref, fwd_ref, bwd_ref, load_sem, nears, skip_rows, bias_rows, proj_rows,
+    grid, got_meta, send_v, recv_v,
+    got, latent, total, ybuf, spec, spec_other, send_b, recv_b, xbuf, rhs, send_c, recv_c, recv_d, ubuf,
     send_sem, recv_sem,
 ):
     me, chan = lax.axis_index("slab"), lax.axis_index("chan")
@@ -221,7 +245,7 @@
         pltpu.make_async_copy(src, dst, load_sem.at[n])
         for n, (src, dst) in enumerate(
             (
-                (mine_ref.at[pl.ds(0, G * HALF)], total),
+                (mine_ref, total),
                 (meta_ref.at[me], got_meta.at[me]),
                 (fwd_hbm, fwd_ref),
                 (weight_hbm, weight_ref),
@@ -248,11 +272,16 @@
     swap_latent = swap(theirs_ref, got, 0)
     swap_latent.start()
     send_blocks(1, G // 2, me, chan, meta_ref, got_meta, send_sem.at[7], recv_sem.at[7])
+    skip_rows[...] = skip_ref[...].astype(F32).T
+    proj_rows[...] = proj_in_ref[...].astype(F32).T.astype(BF)
+    for c in range(HALF):
+        bias_rows[c : c + 1, :] = jnp.full((1, G), bias_ref[chan * HALF + c], F32)
+    proj_out = jnp.broadcast_to(proj_out_ref[...].astype(F32), (8, 128)).astype(BF)
     loads[0].wait()
     swap_latent.wait()
     total[...] = total[...] + got[...].astype(F32)
-    latent[...] = total[...].astype(BF)
-    swap_other = swap(latent, latent_other, 1)
+    latent[chan] = total[...].astype(BF)
+    swap_other = swap(latent.at[chan], latent.at[chan], 1)
     swap_other.start()
 
     for c in range(HALF):
@@ -283,12 +312,13 @@
     scatter(me, chan, send_b, recv_b, send_sem.at[3], recv_sem.at[3])
 
     swap_other.wait()
+    skip = skip_rows[pl.ds(pl.multiple_of(chan * HALF, HALF), HALF), :].astype(BF)
 
     def mix_channels(group, carry):
         for u in range(8):
             rows = pl.ds(pl.multiple_of((group * 8 + u) * HALF, HALF), HALF)
-            both = jnp.concatenate([latent[rows, :], latent_other[rows, :]], axis=0)
-            total[rows, :] = dot(skip_ref[...], both) + bias_ref[...]
+            both = jnp.concatenate([latent[0, rows, :], latent[1, rows, :]], axis=0)
+            total[rows, :] = dot(skip, both) + bias_rows[...]
         return carry
 
     lax.fori_loop(0, G // 8, mix_channels, 0)
@@ -327,6 +357,19 @@
     lax.fori_loop(0, 4, chunk, 0)
     send_c[...] = dot(bwd_ref[...], rhs[...]).reshape(G, 8, 128).astype(BF)
     scatter(me, chan, send_c, recv_c, send_sem.at[4], recv_sem.at[4])
+
+    settle(meta_ref, got_meta, send_sem.at[7], recv_sem.at[7])
+
+    def build(group, carry):
+        for u in range(4):
+            slab = group * 4 + u
+            info = got_meta[slab, 16:24, :].astype(F32).astype(jnp.int32)
+            for r in range(2):
+                weight = got_meta[slab, r * 8 : (r + 1) * 8, :].astype(F32)
+                nears[2 * slab + r] = near_transposed(info[r : r + 1, :], weight)
+        return carry
+
+    lax.fori_loop(0, G // 4, build, 0)
     settle(send_c, recv_c, send_sem.at[4], recv_sem.at[4])
     swap_back = swap(recv_c, recv_d, 5)
     swap_back.start()
@@ -346,29 +389,29 @@
         for u in range(4):
             y = group * 4 + u
             rows = pl.ds(pl.multiple_of(y * HALF, HALF), HALF)
-            grid_ref[y] = gelu(total[rows, :]).astype(BF)
-        return carry
-
-    lax.fori_loop(0, G // 4, finish, 0)
-    swap_grid = swap(grid_ref, grid_other_ref, 6)
-    swap_grid.start()
-    settle(meta_ref, got_meta, send_sem.at[7], recv_sem.at[7])
-    swap_grid.wait()
+            grid[chan, y] = gelu(total[rows, :]).astype(BF)
+        return carry
+
+    swaps = []
+    for k in range(4):
+        lax.fori_loop(k * 8, k * 8 + 8, finish, 0)
+        piece = grid.at[chan, pl.ds(k * 32, 32)]
+        swaps.append(swap(piece, piece, 9 + k))
+        swaps[-1].start()
+    for piece in swaps:
+        piece.wait()
 
     def decode(group, carry):
-        slabs, cells, nears = [], [], []
+        slabs, values = [], []
         for j in range(8):
-            slab = (me + group * 8 + j) % G
+            slab = (me + group * 8 + j) & (G - 1)
             slabs.append(slab)
-            info = got_meta[slab, 16:24, :].astype(F32).astype(jnp.int32)
             for r in range(2):
                 line = jnp.maximum(line_ref[slab, 0, r] - 1, 0)
-                weight = got_meta[slab, r * 8 : (r + 1) * 8, :].astype(F32)
-                cells.append(jnp.concatenate([grid_ref[line], grid_other_ref[line]], axis=0))
-                nears.append(near_transposed(info[r : r + 1, :], weight))
-        values = [dot(cell, near).astype(BF) for cell, near in zip(cells, nears)]
-        hidden = gelu(dot(proj_in_ref[...], jnp.concatenate(values, axis=1))).astype(BF)
-        result = dot(proj_out_ref[...], hidden)
+                cells = jnp.concatenate([grid[0, line], grid[1, line]], axis=0)
+                values.append(dot(cells, nears[2 * slab + r]).astype(BF))
+        hidden = gelu(dot(proj_rows[...], jnp.concatenate(values, axis=1))).astype(BF)
+        result = dot(proj_out, hidden)
         for j in range(8):
             for r in range(2):
                 u = 2 * j + r
@@ -448,20 +491,17 @@
             vmem_limit_bytes=LIMIT, collective_id=0, has_side_effects=True
         ),
     )(low, high, dest_block, points, near_start, near_weight, lift_w)
-    mine, theirs = pl.pallas_call(
+    mine, theirs = call(
         gather_kernel,
-        grid=(8,),
-        out_shape=(
-            jax.ShapeDtypeStruct(((G + 1) * HALF, G), F32),
-            jax.ShapeDtypeStruct((G * HALF, G), BF),
-        ),
-        in_specs=[SM, SM, pl.BlockSpec((16, 2 * C, PB), lambda i: (i, 0, 0))],
-        out_specs=(
-            pl.BlockSpec(((G + 1) * HALF, G), lambda i: (0, 0)),
-            pl.BlockSpec((G * HALF, G), lambda i: (0, 0)),
-        ),
-        scratch_shapes=[pltpu.VMEM(((G + 1) * HALF, G), F32)],
-        compiler_params=pltpu.CompilerParams(vmem_limit_bytes=LIMIT),
+        (jax.ShapeDtypeStruct((G * HALF, G), F32), jax.ShapeDtypeStruct((G * HALF, G), BF)),
+        [SM, SM, ANY],
+        [
+            pltpu.VMEM((G, 2 * C, PB), BF),
+            pltpu.VMEM((2, (G + 1) * HALF, G), F32),
+            pltpu.VMEM((G * HALF, G), BF),
+            pltpu.SemaphoreType.DMA((10,)),
+        ],
+        (ANY, ANY),
     )(chan.reshape(1), lines, parts)
 
     dy = jnp.asarray(np.concatenate([cos.T, -sin.T, -cos.T], axis=0), BF)
@@ -477,45 +517,28 @@
     ez = ez.reshape(2, 2 * M, 2 * G)
     ey = np.stack([cos, -sin], axis=2).reshape(G, 2 * M) / G**3
     weight = jnp.transpose(spec_weight, (0, 1, 3, 4, 2)).reshape(2, C, 128, C)
-    own = chan * HALF
-    other = (1 - chan) * HALF
-    skip_own = lax.dynamic_slice_in_dim(skip_w, own, HALF, 1)
-    skip = jnp.concatenate(
-        [
-            lax.dynamic_slice_in_dim(skip_own, own, HALF, 0),
-            lax.dynamic_slice_in_dim(skip_own, other, HALF, 0),
-        ],
-        axis=0,
-    ).T
-    bias = jnp.broadcast_to(lax.dynamic_slice_in_dim(skip_bias, own, HALF, 0)[:, None], (HALF, G))
     plane = (G * HALF, G)
     block8 = pltpu.VMEM((G, 8, 128), BF)
-    proj = jnp.concatenate(
-        [
-            lax.dynamic_slice_in_dim(proj_in, own, HALF, 0),
-            lax.dynamic_slice_in_dim(proj_in, other, HALF, 0),
-        ],
-        axis=0,
-    ).T
-    proj_row = jnp.broadcast_to(proj_out[None, :], (8, 128))
     return pl.pallas_call(
         middle_kernel,
         out_shape=jax.ShapeDtypeStruct((128, PB), F32),
-        in_specs=[SM] * 4 + [ANY] * 6 + [VM] * 8,
+        in_specs=[SM] * 5 + [ANY] * 6 + [VM] * 7,
         out_specs=VM,
         scratch_shapes=[
             pltpu.VMEM((2, C, 128, C), BF),
             pltpu.VMEM((512, 1024), BF),
             pltpu.VMEM((1024, 512), BF),
             pltpu.SemaphoreType.DMA((5,)),
-            pltpu.VMEM((G, HALF, G), BF),
-            pltpu.VMEM((G, HALF, G), BF),
+            pltpu.VMEM((2 * G, G, PB), BF),
+            pltpu.VMEM((C, C), F32),
+            pltpu.VMEM((HALF, G), F32),
+            pltpu.VMEM((128, C), BF),
+            pltpu.VMEM((2, G, HALF, G), BF),
             pltpu.VMEM((G, 24, PB), BF),
             pltpu.VMEM((G, 2, PB), F32),
             pltpu.VMEM((G, 2, PB), F32),
             pltpu.VMEM(plane, BF),
-            pltpu.VMEM(plane, BF),
-            pltpu.VMEM(plane, BF),
+            pltpu.VMEM((2,) + plane, BF),
             pltpu.VMEM(plane, F32),
             pltpu.VMEM((3 * M * HALF, G), F32),
             pltpu.VMEM((2, 1024, 128), BF),
@@ -528,16 +551,17 @@
             block8,
             block8,
             pltpu.VMEM((M * C, G), F32),
-            pltpu.SemaphoreType.DMA((9,)),
-            pltpu.SemaphoreType.DMA((9,)),
+            pltpu.SemaphoreType.DMA((13,)),
+            pltpu.SemaphoreType.DMA((13,)),
         ],
         compiler_params=pltpu.CompilerParams(
             vmem_limit_bytes=LIMIT, collective_id=1, has_side_effects=True
         ),
     )(
-        lines, low, dest_slab[:, 0], live_count, mine, theirs, weight,
+        lines, low, dest_slab[:, 0], live_count, skip_bias, mine, theirs, weight,
         jnp.asarray(forward, BF), jnp.asarray(forward.T, BF), meta,
-        dy, jnp.asarray(dz, BF), jnp.asarray(ez, BF), jnp.asarray(ey, BF), skip, bias, proj, proj_row,
+        dy, jnp.asarray(dz, BF), jnp.asarray(ez, BF), jnp.asarray(ey, BF), skip_w, proj_in,
+        proj_out.reshape(1, 128),
     )
 
 

time: 198 us -> 190 us (0.960)
  Pallas kernels: 191 us -> 186 us
    pallas_call x1, Pallas kernels: 8.26 us -> 5.98 us  [shards(): call(gather_kernel, (jax.ShapeDtypeStruct((G * HALF, G), F32), jax.ShapeD...]
where the time goes in v7:
time: 190 us
  Pallas kernels  186 us (98%)
    pallas_call x1, Pallas kernels, shards(): pl.pallas_call(dispatch_kernel, out_shape=(jax.ShapeDtypeStruct((G, 2 * C...  109 us
    pallas_call x1, Pallas kernels, shards(): pl.pallas_call(middle_kernel, out_shape=jax.ShapeDtypeStruct((128, PB), F...  71.2 us
    pallas_call x1, Pallas kernels, shards(): call(gather_kernel, (jax.ShapeDtypeStruct((G * HALF, G), F32), jax.ShapeD...  5.98 us

profile of v7, /device:TPU:1, one launch (start us, length us, event | category | flops | bytes accessed | tf_op | source)
XLA Modules:
  0.0 189.5 jit_solution(6253494987350483318)
XLA Ops:
  0.7 0.7 compare_select_fusion
  1.3 0.6 select_reduce_fusion
  2.0 108.9 %shard_map.172 = (bf16[128,128,128]{2,1,0:T(8,128)(2,1)}, s32[128,1,128]{2,1,0:T(1,128)}, bf16[128,24,128]{2,1,0:T(8,128)(2,1)}) custom-call(s32[128]{0:T(128)} %get-tuple-element.16.lo_ref.low_ref, s32[128]{0:T(128)} %get-tuple-element.15.hi_ref, s32[128]{0:T(128)} %line_ref.1, bf16[128,64,128]{2,1,0:T(8,128)(2,1)} %points_hbm.1, s32[128,128]{1,0:T(8,128)} %start_hbm.1, ...), custom_call_target="tpu_custom_call" | custom-call | tf_op jit(solution)/shard_map/pallas_call | solution.py:471
  110.9 6.0 %shard_map.173 = (f32[4096,128]{1,0:T(8,128)}, bf16[4096,128]{1,0:T(8,128)(2,1)}) custom-call(s32[1]{0:T(128)} %bitcast.2.chan_ref, s32[128,1,128]{2,1,0:T(1,128)} %get-tuple-element.10.line_ref, bf16[128,128,128]{2,1,0:T(8,128)(2,1)} %get-tuple-element.11.parts_hbm), custom_call_target="tpu_custom_call" | custom-call | tf_op jit(solution)/shard_map/pallas_call | solution.py:494
  116.9 71.2 %shard_map.174 = f32[128,128]{1,0:T(8,128)} custom-call(s32[128,1,128]{2,1,0:T(1,128)} %get-tuple-element.10.line_ref, s32[128]{0:T(128)} %get-tuple-element.16.lo_ref.low_ref, s32[128]{0:T(128)} %bitcast.10, s32[1]{0:T(128)} %copy.20.count_ref, f32[64]{0:T(128)} %bias_ref.1, f32[4096,128]{1,0:T(8,128)} %get-tuple-element.12.mine_ref, ...), custom_call_target="tpu_custom_call" | custom-call | tf_op jit(solution)/shard_map/pallas_call | solution.py:522
  188.1 1.5 copy.21

commit v8 on v7

--- a/solution.py
+++ b/solution.py
@@ -300,6 +300,18 @@
 
     swap_spec = swap(spec.at[1 - chan], spec_other, 2)
     swap_spec.start()
+
+    swap_other.wait()
+    skip = skip_rows[pl.ds(pl.multiple_of(chan * HALF, HALF), HALF), :].astype(BF)
+
+    def mix_channels(group, carry):
+        for u in range(8):
+            rows = pl.ds(pl.multiple_of((group * 8 + u) * HALF, HALF), HALF)
+            both = jnp.concatenate([latent[0, rows, :], latent[1, rows, :]], axis=0)
+            total[rows, :] = dot(skip, both) + bias_rows[...]
+        return carry
+
+    lax.fori_loop(0, G // 16, mix_channels, 0)
     swap_spec.wait()
     row = lax.broadcasted_iota(jnp.int32, (8, 128), 0)
     from_own = (row // 4) == chan
@@ -311,17 +323,7 @@
             send_b[q * 4 + j] = jnp.where(from_own, own[rows], other[rows]).astype(BF)
     scatter(me, chan, send_b, recv_b, send_sem.at[3], recv_sem.at[3])
 
-    swap_other.wait()
-    skip = skip_rows[pl.ds(pl.multiple_of(chan * HALF, HALF), HALF), :].astype(BF)
-
-    def mix_channels(group, carry):
-        for u in range(8):
-            rows = pl.ds(pl.multiple_of((group * 8 + u) * HALF, HALF), HALF)
-            both = jnp.concatenate([latent[0, rows, :], latent[1, rows, :]], axis=0)
-            total[rows, :] = dot(skip, both) + bias_rows[...]
-        return carry
-
-    lax.fori_loop(0, G // 8, mix_channels, 0)
+    lax.fori_loop(G // 16, G // 8, mix_channels, 0)
     settle(send_b, recv_b, send_sem.at[3], recv_sem.at[3])
     send_blocks(G // 2, G, me, chan, meta_ref, got_meta, send_sem.at[7], recv_sem.at[7])
 
@@ -369,10 +371,11 @@
                 nears[2 * slab + r] = near_transposed(info[r : r + 1, :], weight)
         return carry
 
-    lax.fori_loop(0, G // 4, build, 0)
+    lax.fori_loop(0, G // 8, build, 0)
     settle(send_c, recv_c, send_sem.at[4], recv_sem.at[4])
     swap_back = swap(recv_c, recv_d, 5)
     swap_back.start()
+    lax.fori_loop(G // 8, G // 4, build, 0)
     swap_back.wait()
 
     for q in range(M):
@@ -403,8 +406,8 @@
 
     def decode(group, carry):
         slabs, values = [], []
-        for j in range(8):
-            slab = (me + group * 8 + j) & (G - 1)
+        for j in range(16):
+            slab = (me + group * 16 + j) & (G - 1)
             slabs.append(slab)
             for r in range(2):
                 line = jnp.maximum(line_ref[slab, 0, r] - 1, 0)
@@ -412,11 +415,11 @@
                 values.append(dot(cells, nears[2 * slab + r]).astype(BF))
         hidden = gelu(dot(proj_rows[...], jnp.concatenate(values, axis=1))).astype(BF)
         result = dot(proj_out, hidden)
-        for j in range(8):
+        for j in range(16):
             for r in range(2):
                 u = 2 * j + r
                 send_v[slabs[j], r : r + 1, :] = result[0:1, u * PB : (u + 1) * PB]
-        for j in range(8):
+        for j in range(16):
             copy = pltpu.make_async_remote_copy(
                 src_ref=send_v.at[slabs[j]],
                 dst_ref=recv_v.at[me],
@@ -431,7 +434,7 @@
                 pl.when(group > 0)(copy.start)
         return carry
 
-    lax.fori_loop(0, 16, decode, 0)
+    lax.fori_loop(0, 8, decode, 0)
     recv_v[me] = send_v[me]
     settle(send_v, recv_v, send_sem.at[8], recv_sem.at[8])
 

time: 190 us -> 189 us (level)
  no operation moved by 1% of the time
where the time goes in v8:
time: 189 us; the launch traced here: 188 us
  Pallas kernels  185 us (98%)
    pallas_call x1, Pallas kernels, shards(): pl.pallas_call(dispatch_kernel, out_shape=(jax.ShapeDtypeStruct((G, 2 * C...  109 us
    pallas_call x1, Pallas kernels, shards(): pl.pallas_call(middle_kernel, out_shape=jax.ShapeDtypeStruct((128, PB), F...  69.9 us
    pallas_call x1, Pallas kernels, shards(): call(gather_kernel, (jax.ShapeDtypeStruct((G * HALF, G), F32), jax.ShapeD...  5.95 us

profile of v8, /device:TPU:1, one launch (start us, length us, event | category | flops | bytes accessed | tf_op | source)
XLA Modules:
  0.0 188.3 jit_solution(15742281740400483193)
XLA Ops:
  0.7 0.7 compare_select_fusion
  1.3 0.6 select_reduce_fusion
  2.0 108.9 %shard_map.172 = (bf16[128,128,128]{2,1,0:T(8,128)(2,1)}, s32[128,1,128]{2,1,0:T(1,128)}, bf16[128,24,128]{2,1,0:T(8,128)(2,1)}) custom-call(s32[128]{0:T(128)} %get-tuple-element.16.lo_ref.low_ref, s32[128]{0:T(128)} %get-tuple-element.15.hi_ref, s32[128]{0:T(128)} %line_ref.1, bf16[128,64,128]{2,1,0:T(8,128)(2,1)} %points_hbm.1, s32[128,128]{1,0:T(8,128)} %start_hbm.1, ...), custom_call_target="tpu_custom_call" | custom-call | tf_op jit(solution)/shard_map/pallas_call | solution.py:474
  110.9 6.0 %shard_map.173 = (f32[4096,128]{1,0:T(8,128)}, bf16[4096,128]{1,0:T(8,128)(2,1)}) custom-call(s32[1]{0:T(128)} %bitcast.2.chan_ref, s32[128,1,128]{2,1,0:T(1,128)} %get-tuple-element.10.line_ref, bf16[128,128,128]{2,1,0:T(8,128)(2,1)} %get-tuple-element.11.parts_hbm), custom_call_target="tpu_custom_call" | custom-call | tf_op jit(solution)/shard_map/pallas_call | solution.py:497
  116.8 69.9 %shard_map.174 = f32[128,128]{1,0:T(8,128)} custom-call(s32[128,1,128]{2,1,0:T(1,128)} %get-tuple-element.10.line_ref, s32[128]{0:T(128)} %get-tuple-element.16.lo_ref.low_ref, s32[128]{0:T(128)} %bitcast.10, s32[1]{0:T(128)} %copy.20.count_ref, f32[64]{0:T(128)} %bias_ref.1, f32[4096,128]{1,0:T(8,128)} %get-tuple-element.12.mine_ref, ...), custom_call_target="tpu_custom_call" | custom-call | tf_op jit(solution)/shard_map/pallas_call | solution.py:525
  186.8 1.5 copy.21

commit v9 on v8

--- a/solution.py
+++ b/solution.py
@@ -198,7 +198,7 @@
 
     def greet(i):
         pl.semaphore_signal(
-            barrier, inc=1, device_id=((me + i) & (G - 1), chan), device_id_type=pl.DeviceIdType.MESH
+            barrier, inc=1, device_id=(me ^ i, chan), device_id_type=pl.DeviceIdType.MESH
         )
 
     each(1, G, greet)
@@ -207,7 +207,7 @@
 
 def send_blocks(first, last, me, chan, src, dst, send_sem, recv_sem):
     def send(i):
-        target = (me + i) & (G - 1)
+        target = me ^ i
         pltpu.make_async_remote_copy(
             src_ref=src.at[target],
             dst_ref=dst.at[me],
@@ -407,7 +407,7 @@
     def decode(group, carry):
         slabs, values = [], []
         for j in range(16):
-            slab = (me + group * 16 + j) & (G - 1)
+            slab = me ^ (group * 16 + j)
             slabs.append(slab)
             for r in range(2):
                 line = jnp.maximum(line_ref[slab, 0, r] - 1, 0)

time: 189 us -> 193 us (1.021)
  Pallas kernels: 185 us -> 189 us
    pallas_call x1, Pallas kernels: 69.9 us -> 73.8 us  [shards(): pl.pallas_call(middle_kernel, out_shape=jax.ShapeDtypeStruct((128, PB), F...]
where the time goes in v9:
time: 193 us; the launch traced here: 192 us
  Pallas kernels  189 us (98%)
    pallas_call x1, Pallas kernels, shards(): pl.pallas_call(dispatch_kernel, out_shape=(jax.ShapeDtypeStruct((G, 2 * C...  109 us
    pallas_call x1, Pallas kernels, shards(): pl.pallas_call(middle_kernel, out_shape=jax.ShapeDtypeStruct((128, PB), F...  73.8 us
    pallas_call x1, Pallas kernels, shards(): call(gather_kernel, (jax.ShapeDtypeStruct((G * HALF, G), F32), jax.ShapeD...  5.96 us

profile of v9, /device:TPU:1, one launch (start us, length us, event | category | flops | bytes accessed | tf_op | source)
XLA Modules:
  0.0 192.4 jit_solution(2554385745061225070)
XLA Ops:
  0.7 0.7 compare_select_fusion
  1.3 0.6 select_reduce_fusion
  2.0 109.2 %shard_map.172 = (bf16[128,128,128]{2,1,0:T(8,128)(2,1)}, s32[128,1,128]{2,1,0:T(1,128)}, bf16[128,24,128]{2,1,0:T(8,128)(2,1)}) custom-call(s32[128]{0:T(128)} %get-tuple-element.16.lo_ref.low_ref, s32[128]{0:T(128)} %get-tuple-element.15.hi_ref, s32[128]{0:T(128)} %line_ref.1, bf16[128,64,128]{2,1,0:T(8,128)(2,1)} %points_hbm.1, s32[128,128]{1,0:T(8,128)} %start_hbm.1, ...), custom_call_target="tpu_custom_call" | custom-call | tf_op jit(solution)/shard_map/pallas_call | solution.py:474
  111.1 6.0 %shard_map.173 = (f32[4096,128]{1,0:T(8,128)}, bf16[4096,128]{1,0:T(8,128)(2,1)}) custom-call(s32[1]{0:T(128)} %bitcast.2.chan_ref, s32[128,1,128]{2,1,0:T(1,128)} %get-tuple-element.10.line_ref, bf16[128,128,128]{2,1,0:T(8,128)(2,1)} %get-tuple-element.11.parts_hbm), custom_call_target="tpu_custom_call" | custom-call | tf_op jit(solution)/shard_map/pallas_call | solution.py:497
  117.1 73.8 %shard_map.174 = f32[128,128]{1,0:T(8,128)} custom-call(s32[128,1,128]{2,1,0:T(1,128)} %get-tuple-element.10.line_ref, s32[128]{0:T(128)} %get-tuple-element.16.lo_ref.low_ref, s32[128]{0:T(128)} %bitcast.10, s32[1]{0:T(128)} %copy.20.count_ref, f32[64]{0:T(128)} %bias_ref.1, f32[4096,128]{1,0:T(8,128)} %get-tuple-element.12.mine_ref, ...), custom_call_target="tpu_custom_call" | custom-call | tf_op jit(solution)/shard_map/pallas_call | solution.py:525
  190.9 1.5 copy.21
